TPU v7x, 32 devices: a whole 2x2x4 slice. The times are simulated.
32 devices in a mesh: dp: 8 (over z, x), tensor: 4 (over y, core).
Axes of the slice: x: 2, y: 2, z: 4, core: 2. Of those that a mesh axis runs over, the one named last changes fastest.
Arguments:
- query: bfloat16 [2048, 5120], P('dp', 'tensor'), may hold values from -140 to 140
- keys_values: bfloat16 [2, 2048, 1024], P(None, 'dp', 'tensor'), may hold values from -6 to 6
- out_weight: bfloat16 [5120, 5120], P(('tensor', 'dp')), may hold values from -0.5 to 0.5
- parents: int32 [8], replicated, may hold values from -1 to 6, as said below
- lengths: int32 [8], replicated, may hold values from 1 to 256, 1024 in all
Outputs:
- projected: bfloat16 [2048, 5120], P('dp', 'tensor')
Inputs may be any that keep to these rules, and one draw needn't show every extreme that they name: parents[n] is -1 for a root, else a node before n; every ancestor of n lies among the 3 nodes before n; node 0 is a root; node 4 has the node before it as parent, that one the node before it, and that one the node before it, which is a root.
All inputs are finite; a program needn't handle non-finite values.
Results may differ from a plain program's by a relative error of at most 0.0053.
Values may be sent and summed in bfloat16 or wider, within the bound.
No kernel may reach another device: no remote copies, remote signals or barrier semaphores. Data moves between devices by JAX's collectives and lax.ppermute only.
A program may use at most 64 MiB of HBM per device.

v0:
```python
import jax
import jax.numpy as jnp
from jax import lax
from jax.sharding import PartitionSpec as P

HEAD_DIM = 128
ANC = 3


neg_big = -1e30


def passed_along(x, axis, by):
    size = lax.axis_size(axis)
    pairs = [(i, i + by) for i in range(size) if 0 <= i + by < size]
    return lax.ppermute(x, axis, pairs)


def per_device(query, keys_values, out_weight, parents, lengths):
    capacity = query.shape[0]
    local_width = query.shape[1]
    kv_width = keys_values.shape[2]
    kv_count = kv_width // HEAD_DIM
    per_group = local_width // kv_width
    node_index = lax.axis_index("dp")
    score_scale = HEAD_DIM ** (-0.5)
    positions = jnp.arange(capacity, dtype=jnp.int32)
    spans = jnp.arange(ANC + 1, dtype=jnp.int32)
    ancestry = jnp.zeros((ANC + 1,), jnp.int32)
    climber = parents[node_index]
    for climb_step in range(ANC):
        hit = (climber >= 0) & (spans == node_index - climber)
        ancestry = jnp.where(hit, 1, ancestry)
        climber = jnp.where(climber >= 0, parents[jnp.maximum(climber, 0)], -1)
    nearest = passed_along(keys_values, "dp", 1)
    paired = jnp.stack([keys_values, nearest])
    farther = passed_along(paired, "dp", 2)
    kv_blocks = [keys_values, nearest, farther[0], farther[1]]
    masks = []
    for distance in range(ANC + 1):
        source = jnp.maximum(node_index - distance, 0)
        within = positions[None, :] < lengths[source]
        if distance == 0:
            allowed = within & (positions[None, :] <= positions[:, None])
        else:
            allowed = within & (ancestry[distance] > 0) & (node_index - distance >= 0)
            allowed = jnp.broadcast_to(allowed, (capacity, capacity))
        masks.append(allowed)
    outputs = []
    for kv_head in range(kv_count):
        queries = query[:, kv_head * per_group * HEAD_DIM : (kv_head + 1) * per_group * HEAD_DIM]
        queries = queries.reshape(capacity, per_group, HEAD_DIM)

        def scores_of(kv_block):
            key_cols = kv_block[0][:, kv_head * HEAD_DIM : (kv_head + 1) * HEAD_DIM]
            return (
                jnp.einsum("igd,jd->gij", queries, key_cols, preferred_element_type=jnp.float32)
                * score_scale
            )

        row_max = jnp.full((per_group, capacity, 1), neg_big, jnp.float32)
        for kv_block, allowed in zip(kv_blocks, masks):
            masked = jnp.where(allowed[None], scores_of(kv_block), neg_big)
            row_max = jnp.maximum(row_max, jnp.max(masked, axis=2, keepdims=True))
        row_sum = jnp.zeros((per_group, capacity, 1), jnp.float32)
        weighted = jnp.zeros((per_group, capacity, HEAD_DIM), jnp.float32)
        for kv_block, allowed in zip(kv_blocks, masks):
            weights = jnp.where(allowed[None], jnp.exp(scores_of(kv_block) - row_max), 0.0)
            row_sum = row_sum + jnp.sum(weights, axis=2, keepdims=True)
            value_cols = kv_block[1][:, kv_head * HEAD_DIM : (kv_head + 1) * HEAD_DIM]
            weighted = weighted + jnp.einsum(
                "gij,jd->gid",
                weights.astype(jnp.bfloat16),
                value_cols,
                preferred_element_type=jnp.float32,
            )
        mixed = jnp.transpose(weighted / row_sum, (1, 0, 2)).reshape(capacity, per_group * HEAD_DIM)
        outputs.append(mixed)
    attended = jnp.concatenate(outputs, 1)
    attended = jnp.where(positions[:, None] < lengths[node_index], attended, 0.0).astype(
        jnp.bfloat16
    )
    partial_value = jnp.dot(
        attended,
        lax.all_gather(out_weight, "dp", axis=0, tiled=True),
        preferred_element_type=jnp.float32,
    )
    summed = lax.psum_scatter(partial_value, "tensor", scatter_dimension=1, tiled=True)
    return summed.astype(jnp.bfloat16)


def solution(mesh):
    return jax.shard_map(
        per_device,
        mesh=mesh,
        in_specs=(P("dp", "tensor"), P(None, "dp", "tensor"), P(("tensor", "dp"), None), P(), P()),
        out_specs=P("dp", "tensor"),
        check_vma=False,
    )
```

profile of v0, /device:TPU:0, one launch (start us, length us, event | category | flops | bytes accessed | tf_op | source)
XLA Modules:
  0.0 274.8 jit_solution(11892079610171234781)
XLA Ops:
  6.5 0.7 all-gather.2.cloned.1.call-update
  7.5 4.8 %collective-permute-start = (bf16[2,256,256]{2,1,0:T(8,128)(2,1)S(1)}, bf16[2,256,256]{2,1,0:T(8,128)(2,1)S(1)}, u32[]{:S(2)}, u32[]{:S(2)}) collective-permute-start(bf16[2,256,256]{2,1,0:T(8,128)(2,1)S(1)} %copy-done), channel_id=1, source_target_pairs={{0,4},{4,8},{8,12},{12,16},{16,20},{20,24},{24,28},{1,5},{5,9},{9,... | collective-permute-start | bytes 786440 | tf_op jit(solution)/shard_map/ppermute | solution.py:16
  12.4 0.6 dynamic_slice.27
  14.2 0.6 dynamic_slice.28
  15.5 0.6 dynamic_slice.29
  17.9 0.6 fusion.81
  20.5 0.7 fusion.80
  21.2 0.6 iota_compare_fusion.1
  21.8 0.7 iota_compare_fusion.2
  22.5 0.6 and_and_fusion.2
  23.1 0.7 and_and_fusion
  23.8 0.6 and_and_fusion.1
  24.5 0.3 select_reduce_fusion.7
  25.0 3.5 %collective-permute-start.1 = (bf16[2,2,256,256]{3,2,1,0:T(8,128)(2,1)S(1)}, bf16[2,2,256,256]{3,2,1,0:T(8,128)(2,1)S(1)}, u32[]{:S(2)}, u32[]{:S(2)}) collective-permute-start(bf16[2,2,256,256]{3,2,1,0:T(8,128)(2,1)S(1)} %pad_maximum_fusion), channel_id=1, source_target_pairs={{0,8},{4,12},{8,16},{12,20},{16,24},{20,28},{1,9},{5,13},{9,17},{1... | collective-permute-start | bytes 1572872 | tf_op jit(solution)/shard_map/ppermute | solution.py:16
  28.8 0.5 select_reduce_fusion.6
  29.3 22.2 %collective-permute-done.1 = bf16[2,2,256,256]{3,2,1,0:T(8,128)(2,1)S(1)} collective-permute-done((bf16[2,2,256,256]{3,2,1,0:T(8,128)(2,1)S(1)}, bf16[2,2,256,256]{3,2,1,0:T(8,128)(2,1)S(1)}, u32[]{:S(2)}, u32[]{:S(2)}) %collective-permute-start.1) | collective-permute-done | bytes 524320 | tf_op jit(solution)/shard_map/ppermute | solution.py:16
  51.5 0.3 select_reduce_fusion.4
  51.9 0.3 select_reduce_fusion.5
  52.9 1.6 fusion.13
  54.5 1.0 fusion.23
  55.5 0.4 fusion.37
  55.8 0.4 fusion.32
  56.2 0.4 convolution_add_fusion.5
  56.6 0.4 convolution_add_fusion.4
  56.9 0.4 fusion.11
  57.3 0.4 convolution_add_fusion.2
  57.7 0.4 convolution_add_fusion.1
  58.1 0.4 fusion.12
  58.4 147.5 %all-gather.2.cloned.1.call-done = bf16[1280,5120]{1,0:T(8,128)(2,1)} async-done(((bf16[160,5120]{1,0:T(8,128)(2,1)}), bf16[1280,5120]{1,0:T(8,128)(2,1)}) %all-gather.2.cloned.1.call-update) | async-done | bytes 13107216 | tf_op jit(solution)/shard_map/all_gather | solution.py:85
  205.9 10.1 %fusion.39 = f32[256,5120]{1,0:T(8,128)} fusion(bf16[1280,5120]{1,0:T(8,128)(2,1)} %all-gather.2.cloned.1.call-done, bf16[256,640]{0,1:T(8,128)(2,1)S(1)} %bitcast.140, bf16[256,640]{0,1:T(8,128)(2,1)S(1)} %bitcast.139, pred[256]{0:T(512)(128)(4,1)S(1)} %iota_compare_fusion.2), kind=kOutput, calls=%fused_computation.62 | convolution fusion | flops 3357081600 | bytes 19005696 | tf_op jit(solution)/shard_map/dot_general | solution.py:83
  216.0 49.7 %reduce-scatter.2.cloned.1.call-done = f32[256,1280]{1,0:T(8,128)} async-done(((f32[256,5120]{1,0:T(8,128)}), f32[256,1280]{1,0:T(8,128)}) %reduce-scatter.2.cloned.1.call-update) | async-done | bytes 1310736 | tf_op jit(solution)/shard_map/reduce_scatter | solution.py:88
  265.7 2.2 convert_element_type.39
  (28 shorter events, 2.0 us)
Async XLA Ops:
  6.5 0.9 copy-start
  6.5 5.8 %copy-start.3 = (s32[8]{0:T(128)S(1)}, s32[8]{0:T(128)}, u32[]{:S(2)}) copy-start(s32[8]{0:T(128)} %param.8) | copy-start | bytes 100
  6.5 10.8 %copy-start.1 = (bf16[256,1280]{1,0:T(8,128)(2,1)S(1)}, bf16[256,1280]{1,0:T(8,128)(2,1)}, u32[]{:S(2)}) copy-start(bf16[256,1280]{1,0:T(8,128)(2,1)} %param.5) | copy-start | bytes 1966084
  6.5 199.4 %all-gather.2.cloned.1.call-start = ((), (), s32[]{:S(2)}) async-start(), calls=%async_computation.1 | async-start | bytes 14745600 | tf_op jit(solution)/shard_map/all_gather | solution.py:85
  7.3 258.5 %reduce-scatter.2.cloned.1.call-start = ((), (), s32[]{:S(2)}) async-start(), calls=%async_computation.2 | async-start | bytes 6553600 | tf_op jit(solution)/shard_map/reduce_scatter | solution.py:88
  7.5 17.4 %collective-permute-start = (bf16[2,256,256]{2,1,0:T(8,128)(2,1)S(1)}, bf16[2,256,256]{2,1,0:T(8,128)(2,1)S(1)}, u32[]{:S(2)}, u32[]{:S(2)}) collective-permute-start(bf16[2,256,256]{2,1,0:T(8,128)(2,1)S(1)} %copy-done), channel_id=1, source_target_pairs={{0,4},{4,8},{8,12},{12,16},{16,20},{20,24},{24,28},{1,5},{5,9},{9,... | collective-permute-start | bytes 786440 | tf_op jit(solution)/shard_map/ppermute | solution.py:16
  17.5 3.0 %copy-start.2 = (s32[8]{0:T(128)S(1)}, s32[8]{0:T(128)}, u32[]{:S(2)}) copy-start(s32[8]{0:T(128)} %param.9) | copy-start | bytes 100
  25.0 26.5 %collective-permute-start.1 = (bf16[2,2,256,256]{3,2,1,0:T(8,128)(2,1)S(1)}, bf16[2,2,256,256]{3,2,1,0:T(8,128)(2,1)S(1)}, u32[]{:S(2)}, u32[]{:S(2)}) collective-permute-start(bf16[2,2,256,256]{3,2,1,0:T(8,128)(2,1)S(1)} %pad_maximum_fusion), channel_id=1, source_target_pairs={{0,8},{4,12},{8,16},{12,20},{16,24},{20,28},{1,9},{5,13},{9,17},{1... | collective-permute-start | bytes 1572872 | tf_op jit(solution)/shard_map/ppermute | solution.py:16
Sparse Core Ops, SparseCore 0:
  9.6 196.3 all-gather.1
  216.1 49.5 reduce-scatter.1
where the time goes:
time: 275 us
  waiting for transfers between devices  220 us (80%)
  between operations  18.7 us (7%)
  matrix products  17.1 us (6%)
  starting transfers between devices  8.38 us (3%)
  other arithmetic  6.6 us (2%)
  local copies, waits for them, and re-layouts  3.93 us (1%)
    all_gather x1, waiting for transfers between devices, per_device(): lax.all_gather(out_weight, 'dp', axis=0, tiled=True)  147 us
    reduce_scatter x1, waiting for transfers between devices, per_device(): lax.psum_scatter(partial_value, 'tensor', scatter_dimension=1, tiled=True)  49.7 us
    ppermute x2, waiting for transfers between devices, passed_along(): return lax.ppermute(x, axis, pairs)  22.2 us
    dot_general x1, matrix products, per_device(): jnp.dot(attended, lax.all_gather(out_weight, 'dp', axis=0, tiled=True), p...  10.1 us
    ppermute x2, starting transfers between devices, passed_along(): return lax.ppermute(x, axis, pairs)  8.34 us
  transfers between devices with their start and end apart: 4, of which 3 were waited for; matrix products, arithmetic and copies ran while one was open for 5% of the time, Pallas kernels for 0%

commit v1 on v0

v1 whole, which is shorter than its diff:
```python
import functools

import jax
import jax.numpy as jnp
from jax import lax
from jax.sharding import Mesh
from jax.sharding import PartitionSpec as P

HEAD_DIM = 128
ANC = 3
NEG_BIG = -1e30

NODE_AXES = ("h", "q", "l", "x")
HEAD_AXES = ("y", "c")


def swapped(value, axis):
    return lax.ppermute(value, axis, [(0, 1), (1, 0)])


def passed_along(value, by):
    size = lax.axis_size(NODE_AXES)
    pairs = [(i, i + by) for i in range(size - by)]
    return lax.ppermute(value, NODE_AXES, pairs)


def attention_limits(node, parents, lengths):
    spans = jnp.arange(ANC + 1, dtype=jnp.int32)
    sources = jnp.maximum(node - spans, 0)
    seen = spans == 0
    climber = parents[node]
    for _ in range(ANC):
        seen = seen | ((climber >= 0) & (spans == node - climber))
        climber = jnp.where(climber >= 0, parents[jnp.maximum(climber, 0)], -1)
    return jnp.where(seen, lengths[sources], 0)


def attend(half, limits, query, kv_blocks):
    capacity, width = query.shape[0], query.shape[1] // 2
    kv_width = kv_blocks[0].shape[2] // 2
    kv_count = kv_width // HEAD_DIM
    per_group = width // kv_width
    score_scale = HEAD_DIM ** (-0.5)
    positions = jnp.arange(capacity, dtype=jnp.int32)
    queries = columns_of(query, half, 2).reshape(capacity, kv_count, per_group, HEAD_DIM)
    pairs = [
        lax.dynamic_slice_in_dim(kv, half * kv_width, kv_width, 2).reshape(2, capacity, kv_count, HEAD_DIM)
        for kv in kv_blocks
    ]
    scores = []
    for distance, pair in enumerate(pairs):
        allowed = jnp.broadcast_to(positions[None, :] < limits[distance], (capacity, capacity))
        if distance == 0:
            allowed = allowed & (positions[None, :] <= positions[:, None])
        s = jnp.einsum("irgd,jrd->rgij", queries, pair[0], preferred_element_type=jnp.float32)
        scores.append(jnp.where(allowed, s * score_scale, NEG_BIG))
    row_max = functools.reduce(jnp.maximum, [s.max(axis=-1, keepdims=True) for s in scores])
    weights = [jnp.exp(s - row_max) for s in scores]
    row_sum = sum(w.sum(axis=-1, keepdims=True) for w in weights)
    total = sum(
        jnp.einsum("rgij,jrd->rgid", w.astype(jnp.bfloat16), pair[1], preferred_element_type=jnp.float32)
        for w, pair in zip(weights, pairs)
    )
    mixed = jnp.transpose(total / row_sum, (2, 0, 1, 3)).reshape(capacity, width)
    return jnp.where(positions[:, None] < limits[0], mixed, 0.0).astype(jnp.bfloat16)


def columns_of(value, index, parts):
    width = value.shape[1] // parts
    return lax.dynamic_slice_in_dim(value, index * width, width, 1)


def per_device(query, keys_values, out_weight, parents, lengths):
    h, l, x = lax.axis_index("h"), lax.axis_index("l"), lax.axis_index("x")
    y, c = lax.axis_index("y"), lax.axis_index("c")
    node = lax.axis_index(NODE_AXES)
    limits = attention_limits(node, parents, lengths)
    kv_blocks = [keys_values] + [passed_along(keys_values, d) for d in range(1, ANC + 1)]

    parts = lax.axis_size("q")
    if parts > 1:
        out_weight = lax.all_gather(out_weight, "q", axis=0, tiled=True)
    own = columns_of(out_weight, y, 2)
    own_y = swapped(columns_of(out_weight, 1 - y, 2), "y")
    own_x, own_l = swapped(own, "x"), swapped(own, "l")
    y_x, y_l = swapped(own_y, "x"), swapped(own_y, "l")
    own_lx, y_lx = swapped(own_l, "x"), swapped(y_x, "l")
    pieces = [own, own_x, own_l, own_lx, own_y, y_x, y_l, y_lx]

    sent = attend(1 - h, limits, query, kv_blocks)
    far = swapped(sent, "h")
    near = attend(h, limits, query, kv_blocks)

    def blocks_of(attended):
        tokens = attended.shape[0]
        b = attended.reshape(tokens, parts, 2, 2, -1)
        b = jnp.where(x > 0, b[:, :, :, ::-1], b)
        b = jnp.where(l > 0, b[:, :, ::-1], b)
        return [b[:, :, i, j].reshape(tokens, -1) for i in range(2) for j in range(2)]

    def summed(attended):
        blocks = blocks_of(attended) + blocks_of(swapped(attended, "y"))
        total = sum(jnp.dot(a, w, preferred_element_type=jnp.float32) for a, w in zip(blocks, pieces))
        return columns_of(total, c, 2) + swapped(columns_of(total, 1 - c, 2), "c")

    arrived = swapped(summed(far).astype(jnp.bfloat16), "h")
    return (summed(near) + arrived.astype(jnp.float32)).astype(jnp.bfloat16)


def solution(mesh):
    dp, tensor = mesh.shape["dp"], mesh.shape["tensor"]
    fine = Mesh(mesh.devices.reshape(2, dp // 8, 2, 2, 2, tensor // 2), NODE_AXES + HEAD_AXES)
    return jax.shard_map(
        per_device,
        mesh=fine,
        in_specs=(
            P(NODE_AXES, HEAD_AXES),
            P(None, NODE_AXES, HEAD_AXES),
            P(HEAD_AXES + NODE_AXES, None),
            P(),
            P(),
        ),
        out_specs=P(NODE_AXES, HEAD_AXES),
        check_vma=False,
    )
```

time: 275 us -> 148 us (0.54)
  waiting for transfers between devices: 220 us -> 73.1 us
  starting transfers between devices: 8.38 us -> 25 us
  between operations: 18.7 us -> 3.71 us
  matrix products: 17.1 us -> 25.3 us
  local copies, waits for them, and re-layouts: 3.93 us -> 10.8 us
    all_gather x1 -> x0, waiting for transfers between devices: 147 us -> none  [per_device(): lax.all_gather(out_weight, 'dp', axis=0, tiled=True)]
    ppermute x2 -> x16, waiting for transfers between devices: 22.2 us -> 73.1 us  [the longest x13 73.1 us: swapped(): return lax.ppermute(value, axis, [(0, 1), (1, 0)])]
    reduce_scatter x1 -> x0, waiting for transfers between devices: 49.7 us -> none  [per_device(): lax.psum_scatter(partial_value, 'tensor', scatter_dimension=1, tiled=True)]
    ppermute x2 -> x16, starting transfers between devices: 8.34 us -> 25 us  [the longest x3 14.4 us: passed_along(): return lax.ppermute(value, NODE_AXES, pairs)]
    dot_general x17 -> x32, matrix products: 17.1 us -> 25.3 us  [the longest x16 8.72 us: summed(): jnp.dot(a, w, preferred_element_type=jnp.float32)]
    dynamic_slice x4 -> x7, local copies, waits for them, and re-layouts: 2.5 us -> 7.75 us  [the longest x4 5.95 us: columns_of(): return lax.dynamic_slice_in_dim(value, index * width, width, 1)]
  transfers between devices with their start and end apart: 4 -> 16, of which waited for: 3 -> 6; matrix products, arithmetic and copies ran while one was open for 5% -> 27% of each run, Pallas kernels for 0% -> 0%
where the time goes in v1:
time: 148 us; the launch traced here: 147 us
  waiting for transfers between devices  73.1 us (49%)
  matrix products  25.3 us (17%)
  starting transfers between devices  25 us (17%)
  local copies, waits for them, and re-layouts  10.8 us (7%)
  other arithmetic  9.07 us (6%)
  between operations  3.71 us (3%)
    ppermute x13, waiting for transfers between devices, swapped(): return lax.ppermute(value, axis, [(0, 1), (1, 0)])  73.1 us
    ppermute x3, starting transfers between devices, passed_along(): return lax.ppermute(value, NODE_AXES, pairs)  14.4 us
    ppermute x13, starting transfers between devices, swapped(): return lax.ppermute(value, axis, [(0, 1), (1, 0)])  10.6 us
    dot_general x16, matrix products, summed(): jnp.dot(a, w, preferred_element_type=jnp.float32)  8.72 us
    dot_general x8, matrix products, attend(): jnp.einsum('irgd,jrd->rgij', queries, pair[0], preferred_element_type=jnp...  8.69 us
    dot_general x8, matrix products, attend(): jnp.einsum('rgij,jrd->rgid', w.astype(jnp.bfloat16), pair[1], preferred_e...  7.89 us
    dynamic_slice x4, local copies, waits for them, and re-layouts, columns_of(): return lax.dynamic_slice_in_dim(value, index * width, width, 1)  5.95 us
  transfers between devices with their start and end apart: 16, of which 6 were waited for; matrix products, arithmetic and copies ran while one was open for 27% of the time, Pallas kernels for 0%

profile of v1, /device:TPU:0, one launch (start us, length us, event | category | flops | bytes accessed | tf_op | source)
XLA Modules:
  0.0 147.0 jit_solution(12034560846215710757)
XLA Ops:
  0.0 6.7 %collective-permute-start.2 = (bf16[2,256,256]{2,1,0:T(8,128)(2,1)}, bf16[2,256,256]{2,1,0:T(8,128)(2,1)}, u32[]{:S(2)}, u32[]{:S(2)}) collective-permute-start(bf16[2,256,256]{2,1,0:T(8,128)(2,1)} %param.6), channel_id=1, source_target_pairs={{0,12},{4,16},{8,20},{12,24},{16,28},{1,13},{5,17},{9,21},{13,25},... | collective-permute-start | bytes 786440 | tf_op jit(solution)/shard_map/ppermute | solution.py:24
  6.7 4.2 %collective-permute-start.1 = (bf16[2,256,256]{2,1,0:T(8,128)(2,1)}, bf16[2,256,256]{2,1,0:T(8,128)(2,1)}, u32[]{:S(2)}, u32[]{:S(2)}) collective-permute-start(bf16[2,256,256]{2,1,0:T(8,128)(2,1)} %param.6), channel_id=1, source_target_pairs={{0,8},{4,12},{8,16},{12,20},{16,24},{20,28},{1,9},{5,13},{9,17},{1... | collective-permute-start | bytes 786440 | tf_op jit(solution)/shard_map/ppermute | solution.py:24
  10.9 3.5 %collective-permute-start = (bf16[2,256,256]{2,1,0:T(8,128)(2,1)}, bf16[2,256,256]{2,1,0:T(8,128)(2,1)}, u32[]{:S(2)}, u32[]{:S(2)}) collective-permute-start(bf16[2,256,256]{2,1,0:T(8,128)(2,1)} %param.6), channel_id=1, source_target_pairs={{0,4},{4,8},{8,12},{12,16},{16,20},{20,24},{24,28},{1,5},{5,9},{9,... | collective-permute-start | bytes 786440 | tf_op jit(solution)/shard_map/ppermute | solution.py:24
  14.4 2.4 %constant_dynamic-slice_fusion.4 = (bf16[160,2560]{1,0:T(8,128)(2,1)S(1)}, bf16[160,2560]{1,0:T(8,128)(2,1)}) fusion(bf16[160,5120]{1,0:T(8,128)(2,1)} %param.7, s32[]{:T(128)S(6)} %select_n.164, s32[]{:T(128)S(6)} %select_n.168), kind=kLoop, calls=%fused_computation.178 | loop fusion | bytes 3276808 | tf_op jit(solution)/shard_map/dynamic_slice | solution.py:70
  23.9 1.1 constant_dynamic-slice_fusion.5
  27.4 1.3 fusion.101
  29.8 1.5 %collective-permute-start.7 = (bf16[160,2560]{1,0:T(8,128)(2,1)S(1)}, bf16[160,2560]{1,0:T(8,128)(2,1)S(1)}, u32[]{:S(2)}, u32[]{:S(2)}) collective-permute-start(bf16[160,2560]{1,0:T(8,128)(2,1)S(1)} %copy-done.3), channel_id=1, source_target_pairs={{0,2},{2,0},{1,3},{3,1},{4,6},{6,4},{5,7},{7,5},{8,10},{10,8},{9,1... | collective-permute-start | bytes 2457608 | tf_op jit(solution)/shard_map/ppermute | solution.py:18
  31.3 1.2 bitcast_reduce_fusion
  32.5 1.2 bitcast_reduce_fusion.1
  33.7 1.2 bitcast_reduce_fusion.2
  35.3 1.2 bitcast_reduce_fusion.3
  36.5 1.2 bitcast_reduce_fusion.4
  37.7 1.2 bitcast_reduce_fusion.5
  40.7 1.2 fusion.47
  41.9 1.2 fusion.54
  43.1 1.2 convolution_add_fusion.11
  44.3 1.2 convolution_add_fusion.13
  45.5 1.2 fusion.29
  46.7 1.2 fusion.27
  48.3 1.0 collective-permute-start.6
  49.4 15.0 %collective-permute-done.12 = bf16[256,640]{0,1:T(8,128)(2,1)S(1)} collective-permute-done((bf16[256,640]{0,1:T(8,128)(2,1)S(1)}, bf16[256,640]{0,1:T(8,128)(2,1)S(1)}, u32[]{:S(2)}, u32[]{:S(2)}) %collective-permute-start.12) | collective-permute-done | bytes 327712 | tf_op jit(solution)/shard_map/ppermute | solution.py:18
  66.4 1.8 %collective-permute-start.8 = (bf16[160,2560]{1,0:T(8,128)(2,1)S(1)}, bf16[160,2560]{1,0:T(8,128)(2,1)S(1)}, u32[]{:S(2)}, u32[]{:S(2)}) collective-permute-start(bf16[160,2560]{1,0:T(8,128)(2,1)S(1)} %collective-permute-done.7), channel_id=1, source_target_pairs={{0,4},{4,0},{1,5},{5,1},{2,6},{6,2},{3,7},{7,3},{8,12},{12,8},{9,1... | collective-permute-start | bytes 2457608 | tf_op jit(solution)/shard_map/ppermute | solution.py:18
  71.1 1.9 %collective-permute-done.13 = bf16[256,640]{0,1:T(8,128)(2,1)S(1)} collective-permute-done((bf16[256,640]{0,1:T(8,128)(2,1)S(1)}, bf16[256,640]{0,1:T(8,128)(2,1)S(1)}, u32[]{:S(2)}, u32[]{:S(2)}) %collective-permute-start.13) | collective-permute-done | bytes 327712 | tf_op jit(solution)/shard_map/ppermute | solution.py:18
  73.7 13.9 %collective-permute-done.8 = bf16[160,2560]{1,0:T(8,128)(2,1)S(1)} collective-permute-done((bf16[160,2560]{1,0:T(8,128)(2,1)S(1)}, bf16[160,2560]{1,0:T(8,128)(2,1)S(1)}, u32[]{:S(2)}, u32[]{:S(2)}) %collective-permute-start.8) | collective-permute-done | bytes 819232 | tf_op jit(solution)/shard_map/ppermute | solution.py:18
  87.6 1.9 %collective-permute-start.10 = (bf16[160,2560]{1,0:T(8,128)(2,1)S(1)}, bf16[160,2560]{1,0:T(8,128)(2,1)S(1)}, u32[]{:S(2)}, u32[]{:S(2)}) collective-permute-start(bf16[160,2560]{1,0:T(8,128)(2,1)S(1)} %collective-permute-done.8), channel_id=1, source_target_pairs={{0,8},{8,0},{1,9},{9,1},{2,10},{10,2},{3,11},{11,3},{4,12},{12,4},... | collective-permute-start | bytes 2457608 | tf_op jit(solution)/shard_map/ppermute | solution.py:18
  89.6 13.1 %collective-permute-done.5 = bf16[160,2560]{1,0:T(8,128)(2,1)S(1)} collective-permute-done((bf16[160,2560]{1,0:T(8,128)(2,1)S(1)}, bf16[160,2560]{1,0:T(8,128)(2,1)S(1)}, u32[]{:S(2)}, u32[]{:S(2)}) %collective-permute-start.5) | collective-permute-done | bytes 819232 | tf_op jit(solution)/shard_map/ppermute | solution.py:18
  105.6 1.2 constant_dynamic-slice_fusion
  109.2 1.2 constant_dynamic-slice_fusion.2
  110.9 1.8 %add_convert_fusion.1 = bf16[256,1280]{1,0:T(8,128)(2,1)S(1)} fusion(f32[256,1280]{1,0:T(8,128)} %collective-permute-done.14, f32[256,2560]{1,0:T(8,128)} %copy-done.2, s32[]{:T(128)S(6)} %select_n.169), kind=kLoop, calls=%fused_computation.50 | loop fusion | flops 655360 | bytes 3276804 | tf_op jit(solution)/shard_map/convert_element_type | solution.py:106
  112.8 2.7 %collective-permute-start.15 = (bf16[256,1280]{1,0:T(8,128)(2,1)S(1)}, bf16[256,1280]{1,0:T(8,128)(2,1)S(1)}, u32[]{:S(2)}, u32[]{:S(2)}) collective-permute-start(bf16[256,1280]{1,0:T(8,128)(2,1)S(1)} %add_convert_fusion.1), channel_id=1, source_target_pairs={{0,16},{16,0},{1,17},{17,1},{2,18},{18,2},{3,19},{19,3},{4,20},{20... | collective-permute-start | bytes 1966088 | tf_op jit(solution)/shard_map/ppermute | solution.py:18
  115.4 29.1 %collective-permute-done.15 = bf16[256,1280]{1,0:T(8,128)(2,1)S(1)} collective-permute-done((bf16[256,1280]{1,0:T(8,128)(2,1)S(1)}, bf16[256,1280]{1,0:T(8,128)(2,1)S(1)}, u32[]{:S(2)}, u32[]{:S(2)}) %collective-permute-start.15) | collective-permute-done | bytes 655392 | tf_op jit(solution)/shard_map/ppermute | solution.py:18
  144.5 2.4 %add_convert_fusion = bf16[256,1280]{1,0:T(8,128)(2,1)} fusion(bf16[256,1280]{1,0:T(8,128)(2,1)S(1)} %collective-permute-done.15, f32[256,1280]{1,0:T(8,128)} %collective-permute-done.11, f32[256,2560]{1,0:T(8,128)S(1)} %convolution_add_fusion.5, s32[]{:T(128)S(6)} %select_n.169), kind=kLoop, calls=%fused_computation.49 | loop fusion | flops 1310720 | bytes 3932164 | tf_op jit(solution)/shard_map/convert_element_type | solution.py:107
  (80 shorter events, 21.2 us)
Async XLA Ops:
  0.0 22.0 %copy-start = (s32[8]{0:T(128)S(1)}, s32[8]{0:T(128)}, u32[]{:S(2)}) copy-start(s32[8]{0:T(128)} %param.9) | copy-start | bytes 100
  0.0 29.1 %collective-permute-start.2 = (bf16[2,256,256]{2,1,0:T(8,128)(2,1)}, bf16[2,256,256]{2,1,0:T(8,128)(2,1)}, u32[]{:S(2)}, u32[]{:S(2)}) collective-permute-start(bf16[2,256,256]{2,1,0:T(8,128)(2,1)} %param.6), channel_id=1, source_target_pairs={{0,12},{4,16},{8,20},{12,24},{16,28},{1,13},{5,17},{9,21},{13,25},... | collective-permute-start | bytes 786440 | tf_op jit(solution)/shard_map/ppermute | solution.py:24
  6.7 25.8 %collective-permute-start.1 = (bf16[2,256,256]{2,1,0:T(8,128)(2,1)}, bf16[2,256,256]{2,1,0:T(8,128)(2,1)}, u32[]{:S(2)}, u32[]{:S(2)}) collective-permute-start(bf16[2,256,256]{2,1,0:T(8,128)(2,1)} %param.6), channel_id=1, source_target_pairs={{0,8},{4,12},{8,16},{12,20},{16,24},{20,28},{1,9},{5,13},{9,17},{1... | collective-permute-start | bytes 786440 | tf_op jit(solution)/shard_map/ppermute | solution.py:24
  10.9 22.8 %collective-permute-start = (bf16[2,256,256]{2,1,0:T(8,128)(2,1)}, bf16[2,256,256]{2,1,0:T(8,128)(2,1)}, u32[]{:S(2)}, u32[]{:S(2)}) collective-permute-start(bf16[2,256,256]{2,1,0:T(8,128)(2,1)} %param.6), channel_id=1, source_target_pairs={{0,4},{4,8},{8,12},{12,16},{16,20},{20,24},{24,28},{1,5},{5,9},{9,... | collective-permute-start | bytes 786440 | tf_op jit(solution)/shard_map/ppermute | solution.py:24
  14.4 2.5 %copy-start.5 = (s32[8]{0:T(128)S(1)}, s32[8]{0:T(128)}, u32[]{:S(2)}) copy-start(s32[8]{0:T(128)} %param.8) | copy-start | bytes 100
  16.8 51.7 %collective-permute-start.3 = (bf16[160,2560]{1,0:T(8,128)(2,1)S(1)}, bf16[160,2560]{1,0:T(8,128)(2,1)S(1)}, u32[]{:S(2)}, u32[]{:S(2)}) collective-permute-start(bf16[160,2560]{1,0:T(8,128)(2,1)S(1)} %get-tuple-element.13), channel_id=1, source_target_pairs={{0,4},{4,0},{1,5},{5,1},{2,6},{6,2},{3,7},{7,3},{8,12},{12,8},{9,1... | collective-permute-start | bytes 2457608 | tf_op jit(solution)/shard_map/ppermute | solution.py:18
  16.9 51.3 %collective-permute-start.4 = (bf16[160,2560]{1,0:T(8,128)(2,1)S(1)}, bf16[160,2560]{1,0:T(8,128)(2,1)S(1)}, u32[]{:S(2)}, u32[]{:S(2)}) collective-permute-start(bf16[160,2560]{1,0:T(8,128)(2,1)S(1)} %get-tuple-element.13), channel_id=1, source_target_pairs={{0,8},{8,0},{1,9},{9,1},{2,10},{10,2},{3,11},{11,3},{4,12},{12,4},... | collective-permute-start | bytes 2457608 | tf_op jit(solution)/shard_map/ppermute | solution.py:18
  27.4 1.3 copy-start.4
  28.7 1.1 copy-start.3
  29.8 36.5 %collective-permute-start.7 = (bf16[160,2560]{1,0:T(8,128)(2,1)S(1)}, bf16[160,2560]{1,0:T(8,128)(2,1)S(1)}, u32[]{:S(2)}, u32[]{:S(2)}) collective-permute-start(bf16[160,2560]{1,0:T(8,128)(2,1)S(1)} %copy-done.3), channel_id=1, source_target_pairs={{0,2},{2,0},{1,3},{3,1},{4,6},{6,4},{5,7},{7,5},{8,10},{10,8},{9,1... | collective-permute-start | bytes 2457608 | tf_op jit(solution)/shard_map/ppermute | solution.py:18
  48.1 16.2 %collective-permute-start.12 = (bf16[256,640]{0,1:T(8,128)(2,1)S(1)}, bf16[256,640]{0,1:T(8,128)(2,1)S(1)}, u32[]{:S(2)}, u32[]{:S(2)}) collective-permute-start(bf16[256,640]{0,1:T(8,128)(2,1)S(1)} %get-tuple-element.18), channel_id=1, source_target_pairs={{0,16},{16,0},{1,17},{17,1},{2,18},{18,2},{3,19},{19,3},{4,20},{20... | collective-permute-start | bytes 983048 | tf_op jit(solution)/shard_map/ppermute | solution.py:18
  48.3 16.1 %collective-permute-start.6 = (bf16[256,640]{0,1:T(8,128)(2,1)S(1)}, bf16[256,640]{0,1:T(8,128)(2,1)S(1)}, u32[]{:S(2)}, u32[]{:S(2)}) collective-permute-start(bf16[256,640]{0,1:T(8,128)(2,1)S(1)} %get-tuple-element.17), channel_id=1, source_target_pairs={{0,2},{2,0},{1,3},{3,1},{4,6},{6,4},{5,7},{7,5},{8,10},{10,8},{9,1... | collective-permute-start | bytes 983048 | tf_op jit(solution)/shard_map/ppermute | solution.py:18
  64.6 8.5 %collective-permute-start.13 = (bf16[256,640]{0,1:T(8,128)(2,1)S(1)}, bf16[256,640]{0,1:T(8,128)(2,1)S(1)}, u32[]{:S(2)}, u32[]{:S(2)}) collective-permute-start(bf16[256,640]{0,1:T(8,128)(2,1)S(1)} %collective-permute-done.12), channel_id=1, source_target_pairs={{0,2},{2,0},{1,3},{3,1},{4,6},{6,4},{5,7},{7,5},{8,10},{10,8},{9,1... | collective-permute-start | bytes 983048 | tf_op jit(solution)/shard_map/ppermute | solution.py:18
  66.3 37.7 %collective-permute-start.9 = (bf16[160,2560]{1,0:T(8,128)(2,1)S(1)}, bf16[160,2560]{1,0:T(8,128)(2,1)S(1)}, u32[]{:S(2)}, u32[]{:S(2)}) collective-permute-start(bf16[160,2560]{1,0:T(8,128)(2,1)S(1)} %collective-permute-done.7), channel_id=1, source_target_pairs={{0,8},{8,0},{1,9},{9,1},{2,10},{10,2},{3,11},{11,3},{4,12},{12,4},... | collective-permute-start | bytes 2457608 | tf_op jit(solution)/shard_map/ppermute | solution.py:18
  66.4 21.2 %collective-permute-start.8 = (bf16[160,2560]{1,0:T(8,128)(2,1)S(1)}, bf16[160,2560]{1,0:T(8,128)(2,1)S(1)}, u32[]{:S(2)}, u32[]{:S(2)}) collective-permute-start(bf16[160,2560]{1,0:T(8,128)(2,1)S(1)} %collective-permute-done.7), channel_id=1, source_target_pairs={{0,4},{4,0},{1,5},{5,1},{2,6},{6,2},{3,7},{7,3},{8,12},{12,8},{9,1... | collective-permute-start | bytes 2457608 | tf_op jit(solution)/shard_map/ppermute | solution.py:18
  68.2 34.5 %collective-permute-start.5 = (bf16[160,2560]{1,0:T(8,128)(2,1)S(1)}, bf16[160,2560]{1,0:T(8,128)(2,1)S(1)}, u32[]{:S(2)}, u32[]{:S(2)}) collective-permute-start(bf16[160,2560]{1,0:T(8,128)(2,1)S(1)} %collective-permute-done.4), channel_id=1, source_target_pairs={{0,4},{4,0},{1,5},{5,1},{2,6},{6,2},{3,7},{7,3},{8,12},{12,8},{9,1... | collective-permute-start | bytes 2457608 | tf_op jit(solution)/shard_map/ppermute | solution.py:18
  87.6 17.5 %collective-permute-start.10 = (bf16[160,2560]{1,0:T(8,128)(2,1)S(1)}, bf16[160,2560]{1,0:T(8,128)(2,1)S(1)}, u32[]{:S(2)}, u32[]{:S(2)}) collective-permute-start(bf16[160,2560]{1,0:T(8,128)(2,1)S(1)} %collective-permute-done.8), channel_id=1, source_target_pairs={{0,8},{8,0},{1,9},{9,1},{2,10},{10,2},{3,11},{11,3},{4,12},{12,4},... | collective-permute-start | bytes 2457608 | tf_op jit(solution)/shard_map/ppermute | solution.py:18
  105.6 1.9 %copy-start.2 = (f32[256,2560]{1,0:T(8,128)}, f32[256,2560]{1,0:T(8,128)S(1)}, u32[]{:S(2)}) copy-start(f32[256,2560]{1,0:T(8,128)S(1)} %convolution_add_fusion) | copy-start | bytes 7864324
  107.5 3.4 %collective-permute-start.14 = (f32[256,1280]{1,0:T(8,128)}, f32[256,1280]{1,0:T(8,128)}, u32[]{:S(2)}, u32[]{:S(2)}) collective-permute-start(f32[256,1280]{1,0:T(8,128)} %constant_dynamic-slice_fusion), channel_id=1, source_target_pairs={{0,1},{1,0},{2,3},{3,2},{4,5},{5,4},{6,7},{7,6},{8,9},{9,8},{10,11... | collective-permute-start | bytes 3932168 | tf_op jit(solution)/shard_map/ppermute | solution.py:18
  110.3 5.1 %collective-permute-start.11 = (f32[256,1280]{1,0:T(8,128)}, f32[256,1280]{1,0:T(8,128)}, u32[]{:S(2)}, u32[]{:S(2)}) collective-permute-start(f32[256,1280]{1,0:T(8,128)} %constant_dynamic-slice_fusion.2), channel_id=1, source_target_pairs={{0,1},{1,0},{2,3},{3,2},{4,5},{5,4},{6,7},{7,6},{8,9},{9,8},{10,11... | collective-permute-start | bytes 3932168 | tf_op jit(solution)/shard_map/ppermute | solution.py:18
  110.9 36.1 %copy-start.1 = (s32[8]{0:T(128)S(1)}, s32[8]{0:T(128)}, u32[]{:S(2)}) copy-start(s32[8]{0:T(128)} %param.9) | copy-start | bytes 100
  112.8 31.8 %collective-permute-start.15 = (bf16[256,1280]{1,0:T(8,128)(2,1)S(1)}, bf16[256,1280]{1,0:T(8,128)(2,1)S(1)}, u32[]{:S(2)}, u32[]{:S(2)}) collective-permute-start(bf16[256,1280]{1,0:T(8,128)(2,1)S(1)} %add_convert_fusion.1), channel_id=1, source_target_pairs={{0,16},{16,0},{1,17},{17,1},{2,18},{18,2},{3,19},{19,3},{4,20},{20... | collective-permute-start | bytes 1966088 | tf_op jit(solution)/shard_map/ppermute | solution.py:18

commit v2 on v1

--- a/solution.py
+++ b/solution.py
@@ -9,6 +9,7 @@
 HEAD_DIM = 128
 ANC = 3
 NEG_BIG = -1e30
+CHUNKS = 2
 
 NODE_AXES = ("h", "q", "l", "x")
 HEAD_AXES = ("y", "c")
@@ -20,8 +21,7 @@
 
 def passed_along(value, by):
     size = lax.axis_size(NODE_AXES)
-    pairs = [(i, i + by) for i in range(size - by)]
-    return lax.ppermute(value, NODE_AXES, pairs)
+    return lax.ppermute(value, NODE_AXES, [(i, (i + by) % size) for i in range(size)])
 
 
 def attention_limits(node, parents, lengths):
@@ -80,12 +80,21 @@
     parts = lax.axis_size("q")
     if parts > 1:
         out_weight = lax.all_gather(out_weight, "q", axis=0, tiled=True)
-    own = columns_of(out_weight, y, 2)
-    own_y = swapped(columns_of(out_weight, 1 - y, 2), "y")
-    own_x, own_l = swapped(own, "x"), swapped(own, "l")
-    y_x, y_l = swapped(own_y, "x"), swapped(own_y, "l")
-    own_lx, y_lx = swapped(own_l, "x"), swapped(y_x, "l")
-    pieces = [own, own_x, own_l, own_lx, own_y, y_x, y_l, y_lx]
+    width = out_weight.shape[1] // 4
+    step = width // CHUNKS
+
+    def chunk_of(y_index, chunk):
+        starts = [(y_index * 2 + c_index) * width + chunk * step for c_index in (1 - c, c)]
+        return jnp.concatenate([lax.dynamic_slice_in_dim(out_weight, s, step, 1) for s in starts], 1)
+
+    chunks = []
+    for chunk in range(CHUNKS):
+        own_y = swapped(chunk_of(1 - y, chunk), "y")
+        own = chunk_of(y, chunk)
+        own_x, own_l = swapped(own, "x"), swapped(own, "l")
+        y_x, y_l = swapped(own_y, "x"), swapped(own_y, "l")
+        own_lx, y_lx = swapped(own_l, "x"), swapped(y_x, "l")
+        chunks.append([own, own_x, own_l, own_lx, own_y, y_x, y_l, y_lx])
 
     sent = attend(1 - h, limits, query, kv_blocks)
     far = swapped(sent, "h")
@@ -98,13 +107,18 @@
         b = jnp.where(l > 0, b[:, :, ::-1], b)
         return [b[:, :, i, j].reshape(tokens, -1) for i in range(2) for j in range(2)]
 
-    def summed(attended):
-        blocks = blocks_of(attended) + blocks_of(swapped(attended, "y"))
+    near_blocks = blocks_of(near) + blocks_of(swapped(near, "y"))
+    far_blocks = blocks_of(far) + blocks_of(swapped(far, "y"))
+
+    def summed(blocks, pieces):
         total = sum(jnp.dot(a, w, preferred_element_type=jnp.float32) for a, w in zip(blocks, pieces))
-        return columns_of(total, c, 2) + swapped(columns_of(total, 1 - c, 2), "c")
+        return total[:, step:] + swapped(total[:, :step], "c")
 
-    arrived = swapped(summed(far).astype(jnp.bfloat16), "h")
-    return (summed(near) + arrived.astype(jnp.float32)).astype(jnp.bfloat16)
+    outputs = []
+    for pieces in chunks:
+        arrived = swapped(summed(far_blocks, pieces).astype(jnp.bfloat16), "h")
+        outputs.append((summed(near_blocks, pieces) + arrived.astype(jnp.float32)).astype(jnp.bfloat16))
+    return jnp.concatenate(outputs, 1)
 
 
 def solution(mesh):

time: 148 us -> 160 us (1.081)
  waiting for transfers between devices: 73.1 us -> 87.3 us
  local copies, waits for them, and re-layouts: 10.8 us -> 7.22 us
  matrix products: 25.3 us -> 27.9 us
  other arithmetic: 9.07 us -> 6.91 us
  starting transfers between devices: 25 us -> 26.6 us
    ppermute x13 -> x23, starting transfers between devices: 10.6 us -> 19.6 us  [swapped(): return lax.ppermute(value, axis, [(0, 1), (1, 0)])]
    ppermute x13 -> x23, waiting for transfers between devices: 73.1 us -> 81.8 us  [swapped(): return lax.ppermute(value, axis, [(0, 1), (1, 0)])]
    ppermute x3, starting transfers between devices: 14.4 us -> 7.08 us  [passed_along(): lax.ppermute(value, NODE_AXES, [(i, (i + by) % size) for i in range(size)])]
    ppermute x3, waiting for transfers between devices: 0.01 us -> 5.49 us  [passed_along(): lax.ppermute(value, NODE_AXES, [(i, (i + by) % size) for i in range(size)])]
    dynamic_slice x4 -> x1, local copies, waits for them, and re-layouts: 5.95 us -> 1.14 us  [columns_of(): return lax.dynamic_slice_in_dim(value, index * width, width, 1)]
    convert_element_type x2 -> x4, other arithmetic: 4.27 us -> 0.37 us  [the longest x2 0.2 us: per_device(): (summed(near_blocks, pieces) + arrived.astype(jnp.float32)).astype(jnp.bf...]
    dot_general x16 -> x32, matrix products: 8.72 us -> 12.2 us  [summed(): jnp.dot(a, w, preferred_element_type=jnp.float32)]
    concatenate x0 -> x5, other arithmetic: none -> 1.77 us  [the longest x1 0.89 us: per_device(): return jnp.concatenate(outputs, 1)]
  transfers between devices with their start and end apart: 16 -> 26, of which waited for: 6 -> 11; matrix products, arithmetic and copies ran while one was open for 27% -> 25% of each run, Pallas kernels for 0% -> 0%
where the time goes in v2:
time: 160 us
  waiting for transfers between devices  87.3 us (55%)
  matrix products  27.9 us (17%)
  starting transfers between devices  26.6 us (17%)
  local copies, waits for them, and re-layouts  7.22 us (5%)
  other arithmetic  6.91 us (4%)
  between operations  3.71 us (2%)
    ppermute x23, waiting for transfers between devices, swapped(): return lax.ppermute(value, axis, [(0, 1), (1, 0)])  81.8 us
    ppermute x23, starting transfers between devices, swapped(): return lax.ppermute(value, axis, [(0, 1), (1, 0)])  19.6 us
    dot_general x32, matrix products, summed(): jnp.dot(a, w, preferred_element_type=jnp.float32)  12.2 us
    dot_general x8, matrix products, attend(): jnp.einsum('rgij,jrd->rgid', w.astype(jnp.bfloat16), pair[1], preferred_e...  7.89 us
    dot_general x8, matrix products, attend(): jnp.einsum('irgd,jrd->rgij', queries, pair[0], preferred_element_type=jnp...  7.78 us
    ppermute x3, starting transfers between devices, passed_along(): lax.ppermute(value, NODE_AXES, [(i, (i + by) % size) for i in range(size)])  7.08 us
    ppermute x3, waiting for transfers between devices, passed_along(): lax.ppermute(value, NODE_AXES, [(i, (i + by) % size) for i in range(size)])  5.49 us
  transfers between devices with their start and end apart: 26, of which 11 were waited for; matrix products, arithmetic and copies ran while one was open for 25% of the time, Pallas kernels for 0%

profile of v2, /device:TPU:0, one launch (start us, length us, event | category | flops | bytes accessed | tf_op | source)
XLA Modules:
  0.0 159.6 jit_solution(443115506005788764)
XLA Ops:
  0.0 4.0 %collective-permute-start.2 = (bf16[2,256,256]{2,1,0:T(8,128)(2,1)}, bf16[2,256,256]{2,1,0:T(8,128)(2,1)}, u32[]{:S(2)}, u32[]{:S(2)}) collective-permute-start(bf16[2,256,256]{2,1,0:T(8,128)(2,1)} %param.6), channel_id=1, source_target_pairs={{0,12},{4,16},{8,20},{12,24},{16,28},{20,0},{24,4},{28,8},{1,13},{... | collective-permute-start | bytes 786440 | tf_op jit(solution)/shard_map/ppermute | solution.py:24
  4.0 1.6 collective-permute-start.1
  5.5 1.5 collective-permute-start
  7.1 1.6 %constant_dynamic-slice_fusion.8 = (bf16[160,640]{1,0:T(8,128)(2,1)S(1)}, bf16[160,640]{1,0:T(8,128)(2,1)S(1)}, bf16[160,640]{1,0:T(8,128)(2,1)S(1)}, bf16[160,6...) fusion(bf16[160,5120]{1,0:T(8,128)(2,1)} %param.7, ...), kind=kLoop, calls=%fused_computation.215 | loop fusion | bytes 3276832 | tf_op jit(solution)/shard_map/dynamic_slice | solution.py:88
  9.5 1.5 collective-permute-start.3
  23.2 5.5 %collective-permute-done.2 = bf16[2,256,256]{2,1,0:T(8,128)(2,1)} collective-permute-done((bf16[2,256,256]{2,1,0:T(8,128)(2,1)}, bf16[2,256,256]{2,1,0:T(8,128)(2,1)}, u32[]{:S(2)}, u32[]{:S(2)}) %collective-permute-start.2) | collective-permute-done | bytes 262176 | tf_op jit(solution)/shard_map/ppermute | solution.py:24
  29.9 1.2 bitcast_reduce_fusion.4
  38.1 1.2 fusion.58
  39.3 1.2 fusion.51
  40.5 1.2 convolution_add_fusion.23
  41.7 1.2 convolution_add_fusion.21
  42.9 1.2 fusion.31
  44.1 1.2 fusion.33
  45.8 16.5 %collective-permute-done.12 = bf16[256,640]{0,1:T(8,128)(2,1)S(1)} collective-permute-done((bf16[256,640]{0,1:T(8,128)(2,1)S(1)}, bf16[256,640]{0,1:T(8,128)(2,1)S(1)}, u32[]{:S(2)}, u32[]{:S(2)}) %collective-permute-start.12) | collective-permute-done | bytes 327712 | tf_op jit(solution)/shard_map/ppermute | solution.py:19
  62.3 1.2 collective-permute-start.7
  66.1 1.3 collective-permute-start.6
  68.5 6.2 %collective-permute-done.7 = bf16[160,1280]{1,0:T(8,128)(2,1)S(1)} collective-permute-done((bf16[160,1280]{1,0:T(8,128)(2,1)S(1)}, bf16[160,1280]{1,0:T(8,128)(2,1)S(1)}, u32[]{:S(2)}, u32[]{:S(2)}) %collective-permute-start.7) | collective-permute-done | bytes 409632 | tf_op jit(solution)/shard_map/ppermute | solution.py:19
  74.7 1.7 %collective-permute-start.5 = (bf16[160,1280]{1,0:T(8,128)(2,1)S(1)}, bf16[160,1280]{1,0:T(8,128)(2,1)S(1)}, u32[]{:S(2)}, u32[]{:S(2)}) collective-permute-start(bf16[160,1280]{1,0:T(8,128)(2,1)S(1)} %collective-permute-done.4), channel_id=1, source_target_pairs={{0,4},{4,0},{1,5},{5,1},{2,6},{6,2},{3,7},{7,3},{8,12},{12,8},{9,1... | collective-permute-start | bytes 1228808 | tf_op jit(solution)/shard_map/ppermute | solution.py:19
  77.6 1.3 collective-permute-start.13
  79.6 3.8 %collective-permute-done.19 = bf16[160,1280]{1,0:T(8,128)(2,1)S(1)} collective-permute-done((bf16[160,1280]{1,0:T(8,128)(2,1)S(1)}, bf16[160,1280]{1,0:T(8,128)(2,1)S(1)}, u32[]{:S(2)}, u32[]{:S(2)}) %collective-permute-start.19) | collective-permute-done | bytes 409632 | tf_op jit(solution)/shard_map/ppermute | solution.py:19
  83.5 1.7 %collective-permute-start.8 = (bf16[160,1280]{1,0:T(8,128)(2,1)S(1)}, bf16[160,1280]{1,0:T(8,128)(2,1)S(1)}, u32[]{:S(2)}, u32[]{:S(2)}) collective-permute-start(bf16[160,1280]{1,0:T(8,128)(2,1)S(1)} %collective-permute-done.7), channel_id=1, source_target_pairs={{0,4},{4,0},{1,5},{5,1},{2,6},{6,2},{3,7},{7,3},{8,12},{12,8},{9,1... | collective-permute-start | bytes 1228808 | tf_op jit(solution)/shard_map/ppermute | solution.py:19
  85.2 5.3 %collective-permute-done.6 = bf16[256,640]{0,1:T(8,128)(2,1)S(1)} collective-permute-done((bf16[256,640]{0,1:T(8,128)(2,1)S(1)}, bf16[256,640]{0,1:T(8,128)(2,1)S(1)}, u32[]{:S(2)}, u32[]{:S(2)}) %collective-permute-start.6) | collective-permute-done | bytes 327712 | tf_op jit(solution)/shard_map/ppermute | solution.py:19
  90.5 1.7 %collective-permute-start.18 = (bf16[160,1280]{1,0:T(8,128)(2,1)S(1)}, bf16[160,1280]{1,0:T(8,128)(2,1)S(1)}, u32[]{:S(2)}, u32[]{:S(2)}) collective-permute-start(bf16[160,1280]{1,0:T(8,128)(2,1)S(1)} %collective-permute-done.17), channel_id=1, source_target_pairs={{0,4},{4,0},{1,5},{5,1},{2,6},{6,2},{3,7},{7,3},{8,12},{12,8},{9,1... | collective-permute-start | bytes 1228808 | tf_op jit(solution)/shard_map/ppermute | solution.py:19
  92.2 3.0 %collective-permute-done.13 = bf16[256,640]{0,1:T(8,128)(2,1)S(1)} collective-permute-done((bf16[256,640]{0,1:T(8,128)(2,1)S(1)}, bf16[256,640]{0,1:T(8,128)(2,1)S(1)}, u32[]{:S(2)}, u32[]{:S(2)}) %collective-permute-start.13) | collective-permute-done | bytes 327712 | tf_op jit(solution)/shard_map/ppermute | solution.py:19
  95.3 1.7 %collective-permute-start.20 = (bf16[160,1280]{1,0:T(8,128)(2,1)S(1)}, bf16[160,1280]{1,0:T(8,128)(2,1)S(1)}, u32[]{:S(2)}, u32[]{:S(2)}) collective-permute-start(bf16[160,1280]{1,0:T(8,128)(2,1)S(1)} %collective-permute-done.19), channel_id=1, source_target_pairs={{0,4},{4,0},{1,5},{5,1},{2,6},{6,2},{3,7},{7,3},{8,12},{12,8},{9,1... | collective-permute-start | bytes 1228808 | tf_op jit(solution)/shard_map/ppermute | solution.py:19
  97.9 2.0 %collective-permute-start.10 = (bf16[160,1280]{1,0:T(8,128)(2,1)S(1)}, bf16[160,1280]{1,0:T(8,128)(2,1)S(1)}, u32[]{:S(2)}, u32[]{:S(2)}) collective-permute-start(bf16[160,1280]{1,0:T(8,128)(2,1)S(1)} %collective-permute-done.8), channel_id=1, source_target_pairs={{0,8},{8,0},{1,9},{9,1},{2,10},{10,2},{3,11},{11,3},{4,12},{12,4},... | collective-permute-start | bytes 1228808 | tf_op jit(solution)/shard_map/ppermute | solution.py:19
  99.9 9.1 %collective-permute-done.20 = bf16[160,1280]{1,0:T(8,128)(2,1)S(1)} collective-permute-done((bf16[160,1280]{1,0:T(8,128)(2,1)S(1)}, bf16[160,1280]{1,0:T(8,128)(2,1)S(1)}, u32[]{:S(2)}, u32[]{:S(2)}) %collective-permute-start.20) | collective-permute-done | bytes 409632 | tf_op jit(solution)/shard_map/ppermute | solution.py:19
  114.8 4.2 %collective-permute-done.10 = bf16[160,1280]{1,0:T(8,128)(2,1)S(1)} collective-permute-done((bf16[160,1280]{1,0:T(8,128)(2,1)S(1)}, bf16[160,1280]{1,0:T(8,128)(2,1)S(1)}, u32[]{:S(2)}, u32[]{:S(2)}) %collective-permute-start.10) | collective-permute-done | bytes 409632 | tf_op jit(solution)/shard_map/ppermute | solution.py:19
  119.6 4.8 %collective-permute-done.22 = bf16[160,1280]{1,0:T(8,128)(2,1)S(1)} collective-permute-done((bf16[160,1280]{1,0:T(8,128)(2,1)S(1)}, bf16[160,1280]{1,0:T(8,128)(2,1)S(1)}, u32[]{:S(2)}, u32[]{:S(2)}) %collective-permute-start.22) | collective-permute-done | bytes 409632 | tf_op jit(solution)/shard_map/ppermute | solution.py:19
  126.5 2.6 %collective-permute-start.15 = (bf16[256,640]{1,0:T(8,128)(2,1)S(1)}, bf16[256,640]{1,0:T(8,128)(2,1)S(1)}, u32[]{:S(2)}, u32[]{:S(2)}) collective-permute-start(bf16[256,640]{1,0:T(8,128)(2,1)S(1)} %fusion.73), channel_id=1, source_target_pairs={{0,16},{16,0},{1,17},{17,1},{2,18},{18,2},{3,19},{19,3},{4,20},{20... | collective-permute-start | bytes 983048 | tf_op jit(solution)/shard_map/ppermute | solution.py:19
  129.7 22.3 %collective-permute-done.15 = bf16[256,640]{1,0:T(8,128)(2,1)S(1)} collective-permute-done((bf16[256,640]{1,0:T(8,128)(2,1)S(1)}, bf16[256,640]{1,0:T(8,128)(2,1)S(1)}, u32[]{:S(2)}, u32[]{:S(2)}) %collective-permute-start.15) | collective-permute-done | bytes 327712 | tf_op jit(solution)/shard_map/ppermute | solution.py:19
  152.1 6.5 %collective-permute-done.25 = bf16[256,640]{1,0:T(8,128)(2,1)S(1)} collective-permute-done((bf16[256,640]{1,0:T(8,128)(2,1)S(1)}, bf16[256,640]{1,0:T(8,128)(2,1)S(1)}, u32[]{:S(2)}, u32[]{:S(2)}) %collective-permute-start.25) | collective-permute-done | bytes 327712 | tf_op jit(solution)/shard_map/ppermute | solution.py:19
  (120 shorter events, 34.7 us)
Async XLA Ops:
  0.0 16.1 %copy-start = (s32[8]{0:T(128)S(1)}, s32[8]{0:T(128)}, u32[]{:S(2)}) copy-start(s32[8]{0:T(128)} %param.9) | copy-start | bytes 100
  0.0 28.6 %collective-permute-start.2 = (bf16[2,256,256]{2,1,0:T(8,128)(2,1)}, bf16[2,256,256]{2,1,0:T(8,128)(2,1)}, u32[]{:S(2)}, u32[]{:S(2)}) collective-permute-start(bf16[2,256,256]{2,1,0:T(8,128)(2,1)} %param.6), channel_id=1, source_target_pairs={{0,12},{4,16},{8,20},{12,24},{16,28},{20,0},{24,4},{28,8},{1,13},{... | collective-permute-start | bytes 786440 | tf_op jit(solution)/shard_map/ppermute | solution.py:24
  4.0 25.9 %collective-permute-start.1 = (bf16[2,256,256]{2,1,0:T(8,128)(2,1)}, bf16[2,256,256]{2,1,0:T(8,128)(2,1)}, u32[]{:S(2)}, u32[]{:S(2)}) collective-permute-start(bf16[2,256,256]{2,1,0:T(8,128)(2,1)} %param.6), channel_id=1, source_target_pairs={{0,8},{4,12},{8,16},{12,20},{16,24},{20,28},{24,0},{28,4},{1,9},{5... | collective-permute-start | bytes 786440 | tf_op jit(solution)/shard_map/ppermute | solution.py:24
  5.5 25.6 %collective-permute-start = (bf16[2,256,256]{2,1,0:T(8,128)(2,1)}, bf16[2,256,256]{2,1,0:T(8,128)(2,1)}, u32[]{:S(2)}, u32[]{:S(2)}) collective-permute-start(bf16[2,256,256]{2,1,0:T(8,128)(2,1)} %param.6), channel_id=1, source_target_pairs={{0,4},{4,8},{8,12},{12,16},{16,20},{20,24},{24,28},{28,0},{1,5},{5... | collective-permute-start | bytes 786440 | tf_op jit(solution)/shard_map/ppermute | solution.py:24
  7.1 4.2 %copy-start.3 = (s32[8]{0:T(128)S(1)}, s32[8]{0:T(128)}, u32[]{:S(2)}) copy-start(s32[8]{0:T(128)} %param.8) | copy-start | bytes 100
  9.5 54.6 %collective-permute-start.3 = (bf16[160,1280]{1,0:T(8,128)(2,1)}, bf16[160,1280]{1,0:T(8,128)(2,1)S(1)}, u32[]{:S(2)}, u32[]{:S(2)}) collective-permute-start(bf16[160,1280]{1,0:T(8,128)(2,1)} %pad_maximum_fusion.1), channel_id=1, source_target_pairs={{0,4},{4,0},{1,5},{5,1},{2,6},{6,2},{3,7},{7,3},{8,12},{12,8},{9,1... | collective-permute-start | bytes 1228808 | tf_op jit(solution)/shard_map/ppermute | solution.py:19
  11.0 55.1 %collective-permute-start.4 = (bf16[160,1280]{1,0:T(8,128)(2,1)}, bf16[160,1280]{1,0:T(8,128)(2,1)S(1)}, u32[]{:S(2)}, u32[]{:S(2)}) collective-permute-start(bf16[160,1280]{1,0:T(8,128)(2,1)} %pad_maximum_fusion.1), channel_id=1, source_target_pairs={{0,8},{8,0},{1,9},{9,1},{2,10},{10,2},{3,11},{11,3},{4,12},{12,4},... | collective-permute-start | bytes 1228808 | tf_op jit(solution)/shard_map/ppermute | solution.py:19
  21.5 1.0 copy-start.2
  28.6 47.8 %collective-permute-start.16 = (bf16[160,1280]{1,0:T(8,128)(2,1)S(1)}, bf16[160,1280]{1,0:T(8,128)(2,1)S(1)}, u32[]{:S(2)}, u32[]{:S(2)}) collective-permute-start(bf16[160,1280]{1,0:T(8,128)(2,1)S(1)} %pad_maximum_fusion.3), channel_id=1, source_target_pairs={{0,4},{4,0},{1,5},{5,1},{2,6},{6,2},{3,7},{7,3},{8,12},{12,8},{9,1... | collective-permute-start | bytes 1228808 | tf_op jit(solution)/shard_map/ppermute | solution.py:19
  29.8 47.7 %collective-permute-start.17 = (bf16[160,1280]{1,0:T(8,128)(2,1)S(1)}, bf16[160,1280]{1,0:T(8,128)(2,1)S(1)}, u32[]{:S(2)}, u32[]{:S(2)}) collective-permute-start(bf16[160,1280]{1,0:T(8,128)(2,1)S(1)} %pad_maximum_fusion.3), channel_id=1, source_target_pairs={{0,8},{8,0},{1,9},{9,1},{2,10},{10,2},{3,11},{11,3},{4,12},{12,4},... | collective-permute-start | bytes 1228808 | tf_op jit(solution)/shard_map/ppermute | solution.py:19
  45.5 16.8 %collective-permute-start.12 = (bf16[256,640]{0,1:T(8,128)(2,1)S(1)}, bf16[256,640]{0,1:T(8,128)(2,1)S(1)}, u32[]{:S(2)}, u32[]{:S(2)}) collective-permute-start(bf16[256,640]{0,1:T(8,128)(2,1)S(1)} %get-tuple-element.23), channel_id=1, source_target_pairs={{0,16},{16,0},{1,17},{17,1},{2,18},{18,2},{3,19},{19,3},{4,20},{20... | collective-permute-start | bytes 983048 | tf_op jit(solution)/shard_map/ppermute | solution.py:19
  62.3 12.4 %collective-permute-start.7 = (bf16[160,1280]{1,0:T(8,128)(2,1)S(1)}, bf16[160,1280]{1,0:T(8,128)(2,1)S(1)}, u32[]{:S(2)}, u32[]{:S(2)}) collective-permute-start(bf16[160,1280]{1,0:T(8,128)(2,1)S(1)} %pad_maximum_fusion.2), channel_id=1, source_target_pairs={{0,2},{2,0},{1,3},{3,1},{4,6},{6,4},{5,7},{7,5},{8,10},{10,8},{9,1... | collective-permute-start | bytes 1228808 | tf_op jit(solution)/shard_map/ppermute | solution.py:19
  64.1 19.4 %collective-permute-start.19 = (bf16[160,1280]{1,0:T(8,128)(2,1)S(1)}, bf16[160,1280]{1,0:T(8,128)(2,1)S(1)}, u32[]{:S(2)}, u32[]{:S(2)}) collective-permute-start(bf16[160,1280]{1,0:T(8,128)(2,1)S(1)} %pad_maximum_fusion.4), channel_id=1, source_target_pairs={{0,2},{2,0},{1,3},{3,1},{4,6},{6,4},{5,7},{7,5},{8,10},{10,8},{9,1... | collective-permute-start | bytes 1228808 | tf_op jit(solution)/shard_map/ppermute | solution.py:19
  66.1 24.4 %collective-permute-start.6 = (bf16[256,640]{0,1:T(8,128)(2,1)S(1)}, bf16[256,640]{0,1:T(8,128)(2,1)S(1)}, u32[]{:S(2)}, u32[]{:S(2)}) collective-permute-start(bf16[256,640]{0,1:T(8,128)(2,1)S(1)} %get-tuple-element.24), channel_id=1, source_target_pairs={{0,2},{2,0},{1,3},{3,1},{4,6},{6,4},{5,7},{7,5},{8,10},{10,8},{9,1... | collective-permute-start | bytes 983048 | tf_op jit(solution)/shard_map/ppermute | solution.py:19
  74.7 35.8 %collective-permute-start.5 = (bf16[160,1280]{1,0:T(8,128)(2,1)S(1)}, bf16[160,1280]{1,0:T(8,128)(2,1)S(1)}, u32[]{:S(2)}, u32[]{:S(2)}) collective-permute-start(bf16[160,1280]{1,0:T(8,128)(2,1)S(1)} %collective-permute-done.4), channel_id=1, source_target_pairs={{0,4},{4,0},{1,5},{5,1},{2,6},{6,2},{3,7},{7,3},{8,12},{12,8},{9,1... | collective-permute-start | bytes 1228808 | tf_op jit(solution)/shard_map/ppermute | solution.py:19
  76.4 21.4 %collective-permute-start.9 = (bf16[160,1280]{1,0:T(8,128)(2,1)S(1)}, bf16[160,1280]{1,0:T(8,128)(2,1)S(1)}, u32[]{:S(2)}, u32[]{:S(2)}) collective-permute-start(bf16[160,1280]{1,0:T(8,128)(2,1)S(1)} %collective-permute-done.7), channel_id=1, source_target_pairs={{0,8},{8,0},{1,9},{9,1},{2,10},{10,2},{3,11},{11,3},{4,12},{12,4},... | collective-permute-start | bytes 1228808 | tf_op jit(solution)/shard_map/ppermute | solution.py:19
  77.6 17.7 %collective-permute-start.13 = (bf16[256,640]{0,1:T(8,128)(2,1)S(1)}, bf16[256,640]{0,1:T(8,128)(2,1)S(1)}, u32[]{:S(2)}, u32[]{:S(2)}) collective-permute-start(bf16[256,640]{0,1:T(8,128)(2,1)S(1)} %collective-permute-done.12), channel_id=1, source_target_pairs={{0,2},{2,0},{1,3},{3,1},{4,6},{6,4},{5,7},{7,5},{8,10},{10,8},{9,1... | collective-permute-start | bytes 983048 | tf_op jit(solution)/shard_map/ppermute | solution.py:19
  83.5 14.4 %collective-permute-start.8 = (bf16[160,1280]{1,0:T(8,128)(2,1)S(1)}, bf16[160,1280]{1,0:T(8,128)(2,1)S(1)}, u32[]{:S(2)}, u32[]{:S(2)}) collective-permute-start(bf16[160,1280]{1,0:T(8,128)(2,1)S(1)} %collective-permute-done.7), channel_id=1, source_target_pairs={{0,4},{4,0},{1,5},{5,1},{2,6},{6,2},{3,7},{7,3},{8,12},{12,8},{9,1... | collective-permute-start | bytes 1228808 | tf_op jit(solution)/shard_map/ppermute | solution.py:19
  90.5 22.3 %collective-permute-start.18 = (bf16[160,1280]{1,0:T(8,128)(2,1)S(1)}, bf16[160,1280]{1,0:T(8,128)(2,1)S(1)}, u32[]{:S(2)}, u32[]{:S(2)}) collective-permute-start(bf16[160,1280]{1,0:T(8,128)(2,1)S(1)} %collective-permute-done.17), channel_id=1, source_target_pairs={{0,4},{4,0},{1,5},{5,1},{2,6},{6,2},{3,7},{7,3},{8,12},{12,8},{9,1... | collective-permute-start | bytes 1228808 | tf_op jit(solution)/shard_map/ppermute | solution.py:19
  95.3 13.7 %collective-permute-start.20 = (bf16[160,1280]{1,0:T(8,128)(2,1)S(1)}, bf16[160,1280]{1,0:T(8,128)(2,1)S(1)}, u32[]{:S(2)}, u32[]{:S(2)}) collective-permute-start(bf16[160,1280]{1,0:T(8,128)(2,1)S(1)} %collective-permute-done.19), channel_id=1, source_target_pairs={{0,4},{4,0},{1,5},{5,1},{2,6},{6,2},{3,7},{7,3},{8,12},{12,8},{9,1... | collective-permute-start | bytes 1228808 | tf_op jit(solution)/shard_map/ppermute | solution.py:19
  97.8 14.3 %collective-permute-start.21 = (bf16[160,1280]{1,0:T(8,128)(2,1)S(1)}, bf16[160,1280]{1,0:T(8,128)(2,1)S(1)}, u32[]{:S(2)}, u32[]{:S(2)}) collective-permute-start(bf16[160,1280]{1,0:T(8,128)(2,1)S(1)} %collective-permute-done.19), channel_id=1, source_target_pairs={{0,8},{8,0},{1,9},{9,1},{2,10},{10,2},{3,11},{11,3},{4,12},{12,4},... | collective-permute-start | bytes 1228808 | tf_op jit(solution)/shard_map/ppermute | solution.py:19
  97.9 21.2 %collective-permute-start.10 = (bf16[160,1280]{1,0:T(8,128)(2,1)S(1)}, bf16[160,1280]{1,0:T(8,128)(2,1)S(1)}, u32[]{:S(2)}, u32[]{:S(2)}) collective-permute-start(bf16[160,1280]{1,0:T(8,128)(2,1)S(1)} %collective-permute-done.8), channel_id=1, source_target_pairs={{0,8},{8,0},{1,9},{9,1},{2,10},{10,2},{3,11},{11,3},{4,12},{12,4},... | collective-permute-start | bytes 1228808 | tf_op jit(solution)/shard_map/ppermute | solution.py:19
  109.0 15.4 %collective-permute-start.22 = (bf16[160,1280]{1,0:T(8,128)(2,1)S(1)}, bf16[160,1280]{1,0:T(8,128)(2,1)S(1)}, u32[]{:S(2)}, u32[]{:S(2)}) collective-permute-start(bf16[160,1280]{1,0:T(8,128)(2,1)S(1)} %collective-permute-done.20), channel_id=1, source_target_pairs={{0,8},{8,0},{1,9},{9,1},{2,10},{10,2},{3,11},{11,3},{4,12},{12,4},... | collective-permute-start | bytes 1228808 | tf_op jit(solution)/shard_map/ppermute | solution.py:19
  119.5 6.9 %collective-permute-start.14 = (f32[256,640]{1,0:T(8,128)S(1)}, f32[256,640]{1,0:T(8,128)S(1)}, u32[]{:S(2)}, u32[]{:S(2)}) collective-permute-start(f32[256,640]{1,0:T(8,128)S(1)} %slice.219), channel_id=1, source_target_pairs={{0,1},{1,0},{2,3},{3,2},{4,5},{5,4},{6,7},{7,6},{8,9},{9,8},{10,11... | collective-permute-start | bytes 1966088 | tf_op jit(solution)/shard_map/ppermute | solution.py:19
  124.8 4.3 %collective-permute-start.24 = (f32[256,640]{1,0:T(8,128)S(1)}, f32[256,640]{1,0:T(8,128)S(1)}, u32[]{:S(2)}, u32[]{:S(2)}) collective-permute-start(f32[256,640]{1,0:T(8,128)S(1)} %slice.223), channel_id=1, source_target_pairs={{0,1},{1,0},{2,3},{3,2},{4,5},{5,4},{6,7},{7,6},{8,9},{9,8},{10,11... | collective-permute-start | bytes 1966088 | tf_op jit(solution)/shard_map/ppermute | solution.py:19
  125.3 4.4 %collective-permute-start.11 = (f32[256,640]{1,0:T(8,128)S(1)}, f32[256,640]{1,0:T(8,128)S(1)}, u32[]{:S(2)}, u32[]{:S(2)}) collective-permute-start(f32[256,640]{1,0:T(8,128)S(1)} %slice.209), channel_id=1, source_target_pairs={{0,1},{1,0},{2,3},{3,2},{4,5},{5,4},{6,7},{7,6},{8,9},{9,8},{10,11... | collective-permute-start | bytes 1966088 | tf_op jit(solution)/shard_map/ppermute | solution.py:19
  126.3 25.8 %collective-permute-start.23 = (f32[256,640]{1,0:T(8,128)S(1)}, f32[256,640]{1,0:T(8,128)S(1)}, u32[]{:S(2)}, u32[]{:S(2)}) collective-permute-start(f32[256,640]{1,0:T(8,128)S(1)} %slice.221), channel_id=1, source_target_pairs={{0,1},{1,0},{2,3},{3,2},{4,5},{5,4},{6,7},{7,6},{8,9},{9,8},{10,11... | collective-permute-start | bytes 1966088 | tf_op jit(solution)/shard_map/ppermute | solution.py:19
  126.5 25.5 %collective-permute-start.15 = (bf16[256,640]{1,0:T(8,128)(2,1)S(1)}, bf16[256,640]{1,0:T(8,128)(2,1)S(1)}, u32[]{:S(2)}, u32[]{:S(2)}) collective-permute-start(bf16[256,640]{1,0:T(8,128)(2,1)S(1)} %fusion.73), channel_id=1, source_target_pairs={{0,16},{16,0},{1,17},{17,1},{2,18},{18,2},{3,19},{19,3},{4,20},{20... | collective-permute-start | bytes 983048 | tf_op jit(solution)/shard_map/ppermute | solution.py:19
  129.2 29.4 %collective-permute-start.25 = (bf16[256,640]{1,0:T(8,128)(2,1)S(1)}, bf16[256,640]{1,0:T(8,128)(2,1)S(1)}, u32[]{:S(2)}, u32[]{:S(2)}) collective-permute-start(bf16[256,640]{1,0:T(8,128)(2,1)S(1)} %fusion.70), channel_id=1, source_target_pairs={{0,16},{16,0},{1,17},{17,1},{2,18},{18,2},{3,19},{19,3},{4,20},{20... | collective-permute-start | bytes 983048 | tf_op jit(solution)/shard_map/ppermute | solution.py:19
  152.0 7.6 %copy-start.1 = (s32[8]{0:T(128)S(1)}, s32[8]{0:T(128)}, u32[]{:S(2)}) copy-start(s32[8]{0:T(128)} %param.9) | copy-start | bytes 100

commit v3 on v2

v3 whole, which is shorter than its diff:
```python
import functools

import jax
import jax.numpy as jnp
from jax import lax
from jax.experimental import pallas as pl
from jax.experimental.pallas import tpu as pltpu
from jax.sharding import Mesh
from jax.sharding import PartitionSpec as P

HEAD_DIM = 128
ANC = 3
NEG_BIG = -1e30
CHUNKS = 1

NODE_AXES = ("h", "q", "l", "x")
HEAD_AXES = ("y", "c")


def swapped(value, axis):
    return lax.ppermute(value, axis, [(0, 1), (1, 0)])


def passed_along(value, by):
    size = lax.axis_size(NODE_AXES)
    return lax.ppermute(value, NODE_AXES, [(i, (i + by) % size) for i in range(size)])


def attend_kernel(where_ref, parents_ref, lengths_ref, query_ref, *refs):
    kv_refs, out_ref = refs[: ANC + 1], refs[ANC + 1]
    node = where_ref[1]
    capacity = query_ref.shape[0]
    kv_count = kv_refs[0].shape[2] // HEAD_DIM
    per_group = query_ref.shape[1] // HEAD_DIM // kv_count
    score_scale = HEAD_DIM ** (-0.5)
    limits = [lengths_ref[node]] + [jnp.int32(0)] * ANC
    climber = parents_ref[node]
    for _ in range(ANC):
        reached = jnp.maximum(climber, 0)
        for distance in range(1, ANC + 1):
            hit = (climber >= 0) & (node - climber == distance)
            limits[distance] = jnp.where(hit, lengths_ref[reached], limits[distance])
        climber = jnp.where(climber >= 0, parents_ref[reached], -1)
    row = lax.broadcasted_iota(jnp.int32, (capacity, capacity), 0)
    col = lax.broadcasted_iota(jnp.int32, (capacity, capacity), 1)
    masks = [(col <= row) & (col < limits[0])] + [col < limits[d] for d in range(1, ANC + 1)]
    live = lax.broadcasted_iota(jnp.int32, (capacity, HEAD_DIM), 0) < limits[0]
    for kv_head in range(kv_count):
        kv_cols = slice(kv_head * HEAD_DIM, (kv_head + 1) * HEAD_DIM)
        for member in range(per_group):
            head = kv_head * per_group + member
            cols = slice(head * HEAD_DIM, (head + 1) * HEAD_DIM)
            q = query_ref[:, cols]
            scores = []
            for kv_ref, mask in zip(kv_refs, masks):
                s = lax.dot_general(
                    q, kv_ref[0, :, kv_cols], (((1,), (1,)), ((), ())), preferred_element_type=jnp.float32
                )
                scores.append(jnp.where(mask, s * score_scale, NEG_BIG))
            row_max = functools.reduce(jnp.maximum, scores).max(axis=1, keepdims=True)
            weights = [jnp.exp(s - row_max) for s in scores]
            row_sum = functools.reduce(jnp.add, weights).sum(axis=1, keepdims=True)
            total = jnp.zeros((capacity, HEAD_DIM), jnp.float32)
            for kv_ref, w in zip(kv_refs, weights):
                total = total + jnp.dot(
                    w.astype(jnp.bfloat16), kv_ref[1, :, kv_cols], preferred_element_type=jnp.float32
                )
            out_ref[:, cols] = jnp.where(live, total / row_sum, 0.0).astype(out_ref.dtype)


def attend(half, node, parents, lengths, query, kv_blocks):
    capacity, width = query.shape[0], query.shape[1] // 2
    kv_width = kv_blocks[0].shape[2] // 2
    return pl.pallas_call(
        attend_kernel,
        out_shape=jax.ShapeDtypeStruct((capacity, width), jnp.bfloat16),
        grid_spec=pltpu.PrefetchScalarGridSpec(
            num_scalar_prefetch=3,
            grid=(1,),
            in_specs=[pl.BlockSpec((capacity, width), lambda i, w, p, n: (0, w[0]))]
            + [pl.BlockSpec((2, capacity, kv_width), lambda i, w, p, n: (0, 0, w[0]))] * (ANC + 1),
            out_specs=pl.BlockSpec((capacity, width), lambda i, w, p, n: (0, 0)),
        ),
        compiler_params=pltpu.CompilerParams(vmem_limit_bytes=8 * 2**20),
        cost_estimate=pl.CostEstimate(
            flops=capacity * capacity * (ANC + 1) * width,
            bytes_accessed=4 * capacity * width + 4 * capacity * kv_width * (ANC + 1),
            transcendentals=capacity * capacity * (ANC + 1) * width // HEAD_DIM,
        ),
    )(jnp.stack([half, node]).astype(jnp.int32), parents, lengths, query, *kv_blocks)


def per_device(query, keys_values, out_weight, parents, lengths):
    h, l, x = lax.axis_index("h"), lax.axis_index("l"), lax.axis_index("x")
    y, c = lax.axis_index("y"), lax.axis_index("c")
    node = lax.axis_index(NODE_AXES)
    kv_blocks = [keys_values] + [passed_along(keys_values, d) for d in range(1, ANC + 1)]

    parts = lax.axis_size("q")
    if parts > 1:
        out_weight = lax.all_gather(out_weight, "q", axis=0, tiled=True)
    width = out_weight.shape[1] // 4
    step = width // CHUNKS

    def chunk_of(y_index, chunk):
        starts = [(y_index * 2 + c_index) * width + chunk * step for c_index in (1 - c, c)]
        return jnp.concatenate([lax.dynamic_slice_in_dim(out_weight, s, step, 1) for s in starts], 1)

    chunks = []
    for chunk in range(CHUNKS):
        own_y = swapped(chunk_of(1 - y, chunk), "y")
        own = chunk_of(y, chunk)
        own_x, own_l = swapped(own, "x"), swapped(own, "l")
        y_x, y_l = swapped(own_y, "x"), swapped(own_y, "l")
        own_lx, y_lx = swapped(own_l, "x"), swapped(y_x, "l")
        chunks.append([own, own_x, own_l, own_lx, own_y, y_x, y_l, y_lx])

    sent = attend(1 - h, node, parents, lengths, query, kv_blocks)
    far = swapped(sent, "h")
    near = attend(h, node, parents, lengths, query, kv_blocks)

    def blocks_of(attended):
        tokens = attended.shape[0]
        split = attended.reshape(tokens, parts, 4, -1)
        b = [split[:, :, i].reshape(tokens, -1) for i in range(4)]
        b = [jnp.where(x > 0, b[i ^ 1], b[i]) for i in range(4)]
        return [jnp.where(l > 0, b[i ^ 2], b[i]) for i in range(4)]

    near_blocks = blocks_of(near) + blocks_of(swapped(near, "y"))
    far_blocks = blocks_of(far) + blocks_of(swapped(far, "y"))

    def summed(blocks, pieces):
        total = sum(jnp.dot(a, w, preferred_element_type=jnp.float32) for a, w in zip(blocks, pieces))
        return total[:, step:] + swapped(total[:, :step], "c")

    outputs = []
    for pieces in chunks:
        arrived = swapped(summed(far_blocks, pieces).astype(jnp.bfloat16), "h")
        outputs.append((summed(near_blocks, pieces) + arrived.astype(jnp.float32)).astype(jnp.bfloat16))
    return jnp.concatenate(outputs, 1)


def solution(mesh):
    dp, tensor = mesh.shape["dp"], mesh.shape["tensor"]
    fine = Mesh(mesh.devices.reshape(2, dp // 8, 2, 2, 2, tensor // 2), NODE_AXES + HEAD_AXES)
    return jax.shard_map(
        per_device,
        mesh=fine,
        in_specs=(
            P(NODE_AXES, HEAD_AXES),
            P(None, NODE_AXES, HEAD_AXES),
            P(HEAD_AXES + NODE_AXES, None),
            P(),
            P(),
        ),
        out_specs=P(NODE_AXES, HEAD_AXES),
        check_vma=False,
    )
```

time: 160 us -> 137 us (0.86)
  waiting for transfers between devices: 87.3 us -> 73.4 us
  starting transfers between devices: 26.6 us -> 19.2 us
  Pallas kernels: 0 us -> 6.4 us
  other arithmetic: 6.91 us -> 3.29 us
  between operations: 3.71 us -> 0.31 us
  matrix products: 27.9 us -> 26.1 us
    ppermute x23 -> x13, waiting for transfers between devices: 81.8 us -> 58.1 us  [swapped(): return lax.ppermute(value, axis, [(0, 1), (1, 0)])]
    dot_general x16 -> x0, matrix products: 15.7 us -> none  [the longest x8 7.89 us: attend(): jnp.einsum('rgij,jrd->rgid', w.astype(jnp.bfloat16), pair[1], preferred_e...]
    dot_general x32 -> x16, matrix products: 12.2 us -> 26.1 us  [summed(): jnp.dot(a, w, preferred_element_type=jnp.float32)]
    ppermute x3, waiting for transfers between devices: 5.49 us -> 15.4 us  [passed_along(): lax.ppermute(value, NODE_AXES, [(i, (i + by) % size) for i in range(size)])]
    ppermute x23 -> x13, starting transfers between devices: 19.6 us -> 12.1 us  [swapped(): return lax.ppermute(value, axis, [(0, 1), (1, 0)])]
    pallas_call x0 -> x2, Pallas kernels: none -> 6.4 us  [attend(): pl.pallas_call(attend_kernel, out_shape=jax.ShapeDtypeStruct((capacity, w...]
    ppermute x0 -> x3, local copies, waits for them, and re-layouts: none -> 3.94 us  [swapped(): return lax.ppermute(value, axis, [(0, 1), (1, 0)])]
    dynamic_slice x4 -> x0, local copies, waits for them, and re-layouts: 2.9 us -> none  [the longest x1 1.14 us: columns_of(): return lax.dynamic_slice_in_dim(value, index * width, width, 1)]
  transfers between devices with their start and end apart: 26 -> 16, of which waited for: 11 -> 7; matrix products, arithmetic and copies ran while one was open for 25% -> 25% of each run, Pallas kernels for 0% -> 5%
where the time goes in v3:
time: 137 us; the launch traced here: 136 us
  waiting for transfers between devices  73.4 us (54%)
  matrix products  26.1 us (19%)
  starting transfers between devices  19.2 us (14%)
  local copies, waits for them, and re-layouts  7.47 us (5%)
  Pallas kernels  6.4 us (5%)
  other arithmetic  3.29 us (2%)
    ppermute x13, waiting for transfers between devices, swapped(): return lax.ppermute(value, axis, [(0, 1), (1, 0)])  58.1 us
    dot_general x16, matrix products, summed(): jnp.dot(a, w, preferred_element_type=jnp.float32)  26.1 us
    ppermute x3, waiting for transfers between devices, passed_along(): lax.ppermute(value, NODE_AXES, [(i, (i + by) % size) for i in range(size)])  15.4 us
    ppermute x13, starting transfers between devices, swapped(): return lax.ppermute(value, axis, [(0, 1), (1, 0)])  12.1 us
    ppermute x3, starting transfers between devices, passed_along(): lax.ppermute(value, NODE_AXES, [(i, (i + by) % size) for i in range(size)])  7.08 us
    pallas_call x2, Pallas kernels, attend(): pl.pallas_call(attend_kernel, out_shape=jax.ShapeDtypeStruct((capacity, w...  6.4 us
    ppermute x3, local copies, waits for them, and re-layouts, swapped(): return lax.ppermute(value, axis, [(0, 1), (1, 0)])  3.94 us
  transfers between devices with their start and end apart: 16, of which 7 were waited for; matrix products, arithmetic and copies ran while one was open for 25% of the time, Pallas kernels for 5%

profile of v3, /device:TPU:0, one launch (start us, length us, event | category | flops | bytes accessed | tf_op | source)
XLA Modules:
  0.0 136.2 jit_solution(9177584370625053980)
XLA Ops:
  0.0 2.9 %collective-permute-start = (bf16[2,256,256]{2,1,0:T(8,128)(2,1)}, bf16[2,256,256]{2,1,0:T(8,128)(2,1)S(1)}, u32[]{:S(2)}, u32[]{:S(2)}) collective-permute-start(bf16[2,256,256]{2,1,0:T(8,128)(2,1)} %refs_0_.3), channel_id=1, source_target_pairs={{0,4},{4,8},{8,12},{12,16},{16,20},{20,24},{24,28},{28,0},{1,5},{5... | collective-permute-start | bytes 786440 | tf_op jit(solution)/shard_map/ppermute | solution.py:26
  2.9 1.6 %collective-permute-start.1 = (bf16[2,256,256]{2,1,0:T(8,128)(2,1)}, bf16[2,256,256]{2,1,0:T(8,128)(2,1)S(1)}, u32[]{:S(2)}, u32[]{:S(2)}) collective-permute-start(bf16[2,256,256]{2,1,0:T(8,128)(2,1)} %refs_0_.3), channel_id=1, source_target_pairs={{0,8},{4,12},{8,16},{12,20},{16,24},{20,28},{24,0},{28,4},{1,9},{5... | collective-permute-start | bytes 786440 | tf_op jit(solution)/shard_map/ppermute | solution.py:26
  4.5 2.6 %collective-permute-start.2 = (bf16[2,256,256]{2,1,0:T(8,128)(2,1)}, bf16[2,256,256]{2,1,0:T(8,128)(2,1)S(1)}, u32[]{:S(2)}, u32[]{:S(2)}) collective-permute-start(bf16[2,256,256]{2,1,0:T(8,128)(2,1)} %refs_0_.3), channel_id=1, source_target_pairs={{0,12},{4,16},{8,20},{12,24},{16,28},{20,0},{24,4},{28,8},{1,13},{... | collective-permute-start | bytes 786440 | tf_op jit(solution)/shard_map/ppermute | solution.py:26
  7.1 1.6 %constant_dynamic-slice_fusion.3 = (bf16[160,1280]{1,0:T(8,128)(2,1)S(1)}, bf16[160,1280]{1,0:T(8,128)(2,1)S(1)}, bf16[160,1280]{1,0:T(8,128)(2,1)S(1)}, bf16[160,1280]{1,0:T(8,128)(2,1)S(1)}) fusion(bf16[160,5120]{1,0:T(8,128)(2,1)} %param.7, s32[]{:T(128)S(6)} %select_n.216, s32[]{:T(128)S(6)} %select_n.217, s32[]{:T(128)S(6)} %select_n.231, s32[]{:T(128)S(6)} %select_n.230), kind=kLoop, calls=%fused_computation.94 | loop fusion | bytes 3276816 | tf_op jit(solution)/shard_map/dynamic_slice | solution.py:107
  9.6 1.5 %collective-permute-start.3 = (bf16[160,2560]{1,0:T(8,128)(2,1)}, bf16[160,2560]{1,0:T(8,128)(2,1)}, u32[]{:S(2)}, u32[]{:S(2)}) collective-permute-start(bf16[160,2560]{1,0:T(8,128)(2,1)} %pad_maximum_fusion), channel_id=1, source_target_pairs={{0,4},{4,0},{1,5},{5,1},{2,6},{6,2},{3,7},{7,3},{8,12},{12,8},{9,1... | collective-permute-start | bytes 2457608 | tf_op jit(solution)/shard_map/ppermute | solution.py:21
  12.3 1.2 collective-permute-done.refs_1_
  13.5 1.8 %collective-permute-start.7 = (bf16[160,2560]{1,0:T(8,128)(2,1)}, bf16[160,2560]{1,0:T(8,128)(2,1)}, u32[]{:S(2)}, u32[]{:S(2)}) collective-permute-start(bf16[160,2560]{1,0:T(8,128)(2,1)} %pad_maximum_fusion.1), channel_id=1, source_target_pairs={{0,2},{2,0},{1,3},{3,1},{4,6},{6,4},{5,7},{7,5},{8,10},{10,8},{9,1... | collective-permute-start | bytes 2457608 | tf_op jit(solution)/shard_map/ppermute | solution.py:21
  15.4 14.1 %collective-permute-done.2.refs_3_ = bf16[2,256,256]{2,1,0:T(8,128)(2,1)S(1)} collective-permute-done((bf16[2,256,256]{2,1,0:T(8,128)(2,1)}, bf16[2,256,256]{2,1,0:T(8,128)(2,1)S(1)}, u32[]{:S(2)}, u32[]{:S(2)}) %collective-permute-start.2) | collective-permute-done | bytes 262176 | tf_op jit(solution)/shard_map/ppermute | solution.py:26
  29.6 3.2 %shard_map.56 = bf16[256,640]{1,0:T(8,128)(2,1)S(1)} custom-call(s32[2]{0:T(128)S(1)} %pad_add_fusion.1.where_ref, s32[8]{0:T(128)S(1)} %copy-done.2, s32[8]{0:T(128)S(1)} %copy-done.3, bf16[256,1280]{1,0:T(8,128)(2,1)S(1)} %copy-done, bf16[2,256,256]{2,1,0:T(8,128)(2,1)S(1)} %copy-done.1, bf16[2,256,256]{2,1,0:T(8,128)(2,1)S(1)} %collective-permute-done.refs_1_, ...), custom_call_target="tpu_custom_call" | custom-call | flops 167772160 | bytes 1179648 | tf_op jit(solution)/shard_map/pallas_call | solution.py:74
  32.9 3.2 %shard_map.55 = bf16[256,640]{1,0:T(8,128)(2,1)S(1)} custom-call(s32[2]{0:T(128)S(1)} %pad_add_fusion.where_ref, s32[8]{0:T(128)S(1)} %copy-done.2, s32[8]{0:T(128)S(1)} %copy-done.3, bf16[256,1280]{1,0:T(8,128)(2,1)S(1)} %copy-done, bf16[2,256,256]{2,1,0:T(8,128)(2,1)S(1)} %copy-done.1, bf16[2,256,256]{2,1,0:T(8,128)(2,1)S(1)} %collective-permute-done.refs_1_, ...), custom_call_target="tpu_custom_call" | custom-call | flops 167772160 | bytes 1179648 | tf_op jit(solution)/shard_map/pallas_call | solution.py:74
  36.1 1.6 %collective-permute-start.6 = (bf16[256,640]{1,0:T(8,128)(2,1)S(1)}, bf16[256,640]{1,0:T(8,128)(2,1)S(1)}, u32[]{:S(2)}, u32[]{:S(2)}) collective-permute-start(bf16[256,640]{1,0:T(8,128)(2,1)S(1)} %shard_map.55), channel_id=1, source_target_pairs={{0,2},{2,0},{1,3},{3,1},{4,6},{6,4},{5,7},{7,5},{8,10},{10,8},{9,1... | collective-permute-start | bytes 983048 | tf_op jit(solution)/shard_map/ppermute | solution.py:21
  37.9 2.0 %fusion.27 = f32[256,2560]{1,0:T(8,128)} fusion(pred[]{:T(512)S(6)} %gt.4, pred[]{:T(512)S(6)} %gt.5, bf16[256,1,4,160]{0,3,2,1:T(8,128)(2,1)S(1)} %bitcast.69, bf16[160,1280]{1,0:T(8,128)(2,1)S(1)} %get-tuple-element.6, bf16[160,1280]{1,0:T(8,128)(2,1)S(1)} %get-tuple-element.5), kind=kOutput, calls=%fused_computation.41 | convolution fusion | flops 211476480 | bytes 3768322 | tf_op jit(solution)/shard_map/dot_general | solution.py:133
  39.9 9.7 %collective-permute-done.12 = bf16[256,640]{1,0:T(8,128)(2,1)} collective-permute-done((bf16[256,640]{1,0:T(8,128)(2,1)S(1)}, bf16[256,640]{1,0:T(8,128)(2,1)}, u32[]{:S(2)}, u32[]{:S(2)}) %collective-permute-start.12) | collective-permute-done | bytes 327712 | tf_op jit(solution)/shard_map/ppermute | solution.py:21
  50.8 1.6 %collective-permute-start.13 = (bf16[256,640]{1,0:T(8,128)(2,1)}, bf16[256,640]{1,0:T(8,128)(2,1)}, u32[]{:S(2)}, u32[]{:S(2)}) collective-permute-start(bf16[256,640]{1,0:T(8,128)(2,1)} %collective-permute-done.12), channel_id=1, source_target_pairs={{0,2},{2,0},{1,3},{3,1},{4,6},{6,4},{5,7},{7,5},{8,10},{10,8},{9,1... | collective-permute-start | bytes 983048 | tf_op jit(solution)/shard_map/ppermute | solution.py:21
  54.0 2.0 %collective-permute-start.5 = (bf16[160,2560]{1,0:T(8,128)(2,1)}, bf16[160,2560]{1,0:T(8,128)(2,1)}, u32[]{:S(2)}, u32[]{:S(2)}) collective-permute-start(bf16[160,2560]{1,0:T(8,128)(2,1)} %collective-permute-done.4), channel_id=1, source_target_pairs={{0,4},{4,0},{1,5},{5,1},{2,6},{6,2},{3,7},{7,3},{8,12},{12,8},{9,1... | collective-permute-start | bytes 2457608 | tf_op jit(solution)/shard_map/ppermute | solution.py:21
  56.0 1.7 %convolution_add_fusion.4 = f32[256,2560]{1,0:T(8,128)S(1)} fusion(f32[256,2560]{1,0:T(8,128)S(1)} %fusion.16, bf16[160,2560]{1,0:T(8,128)(2,1)} %collective-permute-done.3, pred[]{:T(512)S(6)} %gt.4, pred[]{:T(512)S(6)} %gt.5, bf16[256,1,4,160]{0,3,2,1:T(8,128)(2,1)S(1)} %bitcast.78), kind=kOutput, calls=%fused_computation.6 | convolution fusion | flops 210493440 | bytes 6389762 | tf_op jit(solution)/shard_map/dot_general | solution.py:133
  57.7 3.4 %convolution_add_fusion.3 = f32[256,2560]{1,0:T(8,128)} fusion(f32[256,2560]{1,0:T(8,128)S(1)} %convolution_add_fusion.4, bf16[160,2560]{1,0:T(8,128)(2,1)} %collective-permute-done.4, pred[]{:T(512)S(6)} %gt.4, pred[]{:T(512)S(6)} %gt.5, bf16[256,1,4,160]{0,3,2,1:T(8,128)(2,1)S(1)} %bitcast.79), kind=kOutput, calls=%fused_computation.5 | convolution fusion | flops 210493440 | bytes 6389762 | tf_op jit(solution)/shard_map/dot_general | solution.py:133
  61.1 1.7 %convolution_add_fusion.9 = f32[256,2560]{1,0:T(8,128)S(1)} fusion(f32[256,2560]{1,0:T(8,128)S(1)} %copy-done.5, bf16[160,2560]{1,0:T(8,128)(2,1)} %collective-permute-done.3, pred[]{:T(512)S(6)} %gt.4, pred[]{:T(512)S(6)} %gt.5, bf16[256,1,4,160]{0,3,2,1:T(8,128)(2,1)S(1)} %bitcast.70), kind=kOutput, calls=%fused_computation.13 | convolution fusion | flops 210493440 | bytes 6389762 | tf_op jit(solution)/shard_map/dot_general | solution.py:133
  62.8 1.9 %convolution_add_fusion.8 = f32[256,2560]{1,0:T(8,128)S(1)} fusion(f32[256,2560]{1,0:T(8,128)S(1)} %convolution_add_fusion.9, bf16[160,2560]{1,0:T(8,128)(2,1)} %collective-permute-done.4, pred[]{:T(512)S(6)} %gt.4, pred[]{:T(512)S(6)} %gt.5, bf16[256,1,4,160]{0,3,2,1:T(8,128)(2,1)} %bitcast.71), kind=kOutput, calls=%fused_computation.12 | convolution fusion | flops 210493440 | bytes 6389762 | tf_op jit(solution)/shard_map/dot_general | solution.py:133
  64.6 3.4 %fusion.22 = f32[256,2560]{1,0:T(8,128)} fusion(bf16[160,2560]{1,0:T(8,128)(2,1)} %collective-permute-done.7, pred[]{:T(512)S(6)} %gt.4, pred[]{:T(512)S(6)} %gt.5, bf16[256,1,4,160]{0,3,2,1:T(8,128)(2,1)} %bitcast.73), kind=kOutput, calls=%fused_computation.36 | convolution fusion | flops 209838080 | bytes 3768322 | tf_op jit(solution)/shard_map/dot_general | solution.py:133
  68.0 1.9 %copy.9 = bf16[256,640]{0,1:T(8,128)(2,1)} copy(bf16[256,640]{1,0:T(8,128)(2,1)} %collective-permute-done.13) | data formatting | bytes 655360 | tf_op jit(solution)/shard_map/ppermute | solution.py:21
  69.9 2.0 %fusion.11 = f32[256,2560]{1,0:T(8,128)S(1)} fusion(bf16[160,2560]{1,0:T(8,128)(2,1)} %collective-permute-done.7, pred[]{:T(512)S(6)} %gt.4, pred[]{:T(512)S(6)} %gt.5, bf16[256,1,4,160]{0,3,2,1:T(8,128)(2,1)} %bitcast.81), kind=kOutput, calls=%fused_computation.25 | convolution fusion | flops 209838080 | bytes 3768322 | tf_op jit(solution)/shard_map/dot_general | solution.py:133
  71.9 3.5 %collective-permute-done.8 = bf16[160,2560]{1,0:T(8,128)(2,1)S(1)} collective-permute-done((bf16[160,2560]{1,0:T(8,128)(2,1)}, bf16[160,2560]{1,0:T(8,128)(2,1)S(1)}, u32[]{:S(2)}, u32[]{:S(2)}) %collective-permute-start.8) | collective-permute-done | bytes 819232 | tf_op jit(solution)/shard_map/ppermute | solution.py:21
  75.3 1.9 %collective-permute-start.10 = (bf16[160,2560]{1,0:T(8,128)(2,1)S(1)}, bf16[160,2560]{1,0:T(8,128)(2,1)S(1)}, u32[]{:S(2)}, u32[]{:S(2)}) collective-permute-start(bf16[160,2560]{1,0:T(8,128)(2,1)S(1)} %collective-permute-done.8), channel_id=1, source_target_pairs={{0,8},{8,0},{1,9},{9,1},{2,10},{10,2},{3,11},{11,3},{4,12},{12,4},... | collective-permute-start | bytes 2457608 | tf_op jit(solution)/shard_map/ppermute | solution.py:21
  77.3 14.0 %collective-permute-done.5 = bf16[160,2560]{1,0:T(8,128)(2,1)} collective-permute-done((bf16[160,2560]{1,0:T(8,128)(2,1)}, bf16[160,2560]{1,0:T(8,128)(2,1)}, u32[]{:S(2)}, u32[]{:S(2)}) %collective-permute-start.5) | collective-permute-done | bytes 819232 | tf_op jit(solution)/shard_map/ppermute | solution.py:21
  91.2 1.9 %fusion.1 = f32[256,2560]{1,0:T(8,128)S(1)} fusion(f32[256,2560]{1,0:T(8,128)S(1)} %fusion.11, f32[256,2560]{1,0:T(8,128)S(1)} %copy-done.4, bf16[160,2560]{1,0:T(8,128)(2,1)} %collective-permute-done.5, pred[]{:T(512)S(6)} %gt.4, pred[]{:T(512)S(6)} %gt.5, bf16[256,1,4,160]{0,3,2,1:T(8,128)(2,1)} %bitcast.80), kind=kOutput, calls=%fused_computation.4 | convolution fusion | flops 211148800 | bytes 9011202 | tf_op jit(solution)/shard_map/dot_general | solution.py:133
  93.1 1.7 %fusion.8 = f32[256,2560]{1,0:T(8,128)S(1)} fusion(bf16[160,2560]{1,0:T(8,128)(2,1)} %collective-permute-done.9, pred[]{:T(512)S(6)} %gt.4, pred[]{:T(512)S(6)} %gt.5, bf16[256,1,4,160]{0,3,2,1:T(8,128)(2,1)S(1)} %bitcast.82), kind=kOutput, calls=%fused_computation.22 | convolution fusion | flops 209838080 | bytes 3768322 | tf_op jit(solution)/shard_map/dot_general | solution.py:133
  94.9 1.7 %fusion.19 = f32[256,2560]{1,0:T(8,128)S(1)} fusion(bf16[160,2560]{1,0:T(8,128)(2,1)} %collective-permute-done.9, pred[]{:T(512)S(6)} %gt.4, pred[]{:T(512)S(6)} %gt.5, bf16[256,1,4,160]{0,3,2,1:T(8,128)(2,1)S(1)} %bitcast.74), kind=kOutput, calls=%fused_computation.33 | convolution fusion | flops 209838080 | bytes 3768322 | tf_op jit(solution)/shard_map/dot_general | solution.py:133
  98.0 1.6 %copy-done.6 = f32[256,2560]{1,0:T(8,128)S(1)} copy-done((f32[256,2560]{1,0:T(8,128)S(1)}, f32[256,2560]{1,0:T(8,128)}, u32[]{:S(2)}) %copy-start.6) | copy-done | bytes 2621464
  99.6 1.9 %fusion.3 = f32[256,2560]{1,0:T(8,128)S(1)} fusion(f32[256,2560]{1,0:T(8,128)S(1)} %copy-done.6, f32[256,2560]{1,0:T(8,128)S(1)} %convolution_add_fusion.8, bf16[160,2560]{1,0:T(8,128)(2,1)} %collective-permute-done.5, pred[]{:T(512)S(6)} %gt.4, pred[]{:T(512)S(6)} %gt.5, bf16[256,1,4,160]{0,3,2,1:T(8,128)(2,1)} %bitcast.72), kind=kOutput, calls=%fused_computation.11 | convolution fusion | flops 211148800 | bytes 9011202 | tf_op jit(solution)/shard_map/dot_general | solution.py:133
  104.2 1.7 %collective-permute-done.11 = f32[256,1280]{1,0:T(8,128)S(1)} collective-permute-done((f32[256,1280]{1,0:T(8,128)S(1)}, f32[256,1280]{1,0:T(8,128)S(1)}, u32[]{:S(2)}, u32[]{:S(2)}) %collective-permute-start.11) | collective-permute-done | bytes 1310752 | tf_op jit(solution)/shard_map/ppermute | solution.py:21
  105.8 29.3 %collective-permute-done.15 = bf16[256,1280]{1,0:T(8,128)(2,1)S(1)} collective-permute-done((bf16[256,1280]{1,0:T(8,128)(2,1)S(1)}, bf16[256,1280]{1,0:T(8,128)(2,1)S(1)}, u32[]{:S(2)}, u32[]{:S(2)}) %collective-permute-start.15) | collective-permute-done | bytes 655392 | tf_op jit(solution)/shard_map/ppermute | solution.py:21
  (53 shorter events, 10.4 us)
Async XLA Ops:
  0.0 13.5 %collective-permute-start = (bf16[2,256,256]{2,1,0:T(8,128)(2,1)}, bf16[2,256,256]{2,1,0:T(8,128)(2,1)S(1)}, u32[]{:S(2)}, u32[]{:S(2)}) collective-permute-start(bf16[2,256,256]{2,1,0:T(8,128)(2,1)} %refs_0_.3), channel_id=1, source_target_pairs={{0,4},{4,8},{8,12},{12,16},{16,20},{20,24},{24,28},{28,0},{1,5},{5... | collective-permute-start | bytes 786440 | tf_op jit(solution)/shard_map/ppermute | solution.py:26
  2.9 12.5 %collective-permute-start.1 = (bf16[2,256,256]{2,1,0:T(8,128)(2,1)}, bf16[2,256,256]{2,1,0:T(8,128)(2,1)S(1)}, u32[]{:S(2)}, u32[]{:S(2)}) collective-permute-start(bf16[2,256,256]{2,1,0:T(8,128)(2,1)} %refs_0_.3), channel_id=1, source_target_pairs={{0,8},{4,12},{8,16},{12,20},{16,24},{20,28},{24,0},{28,4},{1,9},{5... | collective-permute-start | bytes 786440 | tf_op jit(solution)/shard_map/ppermute | solution.py:26
  4.5 25.0 %collective-permute-start.2 = (bf16[2,256,256]{2,1,0:T(8,128)(2,1)}, bf16[2,256,256]{2,1,0:T(8,128)(2,1)S(1)}, u32[]{:S(2)}, u32[]{:S(2)}) collective-permute-start(bf16[2,256,256]{2,1,0:T(8,128)(2,1)} %refs_0_.3), channel_id=1, source_target_pairs={{0,12},{4,16},{8,20},{12,24},{16,28},{20,0},{24,4},{28,8},{1,13},{... | collective-permute-start | bytes 786440 | tf_op jit(solution)/shard_map/ppermute | solution.py:26
  7.1 22.5 %copy-start = (bf16[256,1280]{1,0:T(8,128)(2,1)S(1)}, bf16[256,1280]{1,0:T(8,128)(2,1)}, u32[]{:S(2)}) copy-start(bf16[256,1280]{1,0:T(8,128)(2,1)} %query_ref.3) | copy-start | bytes 1966084
  7.1 22.5 %copy-start.1 = (bf16[2,256,256]{2,1,0:T(8,128)(2,1)S(1)}, bf16[2,256,256]{2,1,0:T(8,128)(2,1)}, u32[]{:S(2)}) copy-start(bf16[2,256,256]{2,1,0:T(8,128)(2,1)} %refs_0_.3) | copy-start | bytes 786436
  7.1 22.5 %copy-start.2 = (s32[8]{0:T(128)S(1)}, s32[8]{0:T(128)}, u32[]{:S(2)}) copy-start(s32[8]{0:T(128)} %parents_ref.3) | copy-start | bytes 100
  7.1 22.5 %copy-start.3 = (s32[8]{0:T(128)S(1)}, s32[8]{0:T(128)}, u32[]{:S(2)}) copy-start(s32[8]{0:T(128)} %lengths_ref.3) | copy-start | bytes 100
  9.6 46.3 %collective-permute-start.3 = (bf16[160,2560]{1,0:T(8,128)(2,1)}, bf16[160,2560]{1,0:T(8,128)(2,1)}, u32[]{:S(2)}, u32[]{:S(2)}) collective-permute-start(bf16[160,2560]{1,0:T(8,128)(2,1)} %pad_maximum_fusion), channel_id=1, source_target_pairs={{0,4},{4,0},{1,5},{5,1},{2,6},{6,2},{3,7},{7,3},{8,12},{12,8},{9,1... | collective-permute-start | bytes 2457608 | tf_op jit(solution)/shard_map/ppermute | solution.py:21
  11.1 42.8 %collective-permute-start.4 = (bf16[160,2560]{1,0:T(8,128)(2,1)}, bf16[160,2560]{1,0:T(8,128)(2,1)}, u32[]{:S(2)}, u32[]{:S(2)}) collective-permute-start(bf16[160,2560]{1,0:T(8,128)(2,1)} %pad_maximum_fusion), channel_id=1, source_target_pairs={{0,8},{8,0},{1,9},{9,1},{2,10},{10,2},{3,11},{11,3},{4,12},{12,4},... | collective-permute-start | bytes 2457608 | tf_op jit(solution)/shard_map/ppermute | solution.py:21
  13.5 40.3 %collective-permute-start.7 = (bf16[160,2560]{1,0:T(8,128)(2,1)}, bf16[160,2560]{1,0:T(8,128)(2,1)}, u32[]{:S(2)}, u32[]{:S(2)}) collective-permute-start(bf16[160,2560]{1,0:T(8,128)(2,1)} %pad_maximum_fusion.1), channel_id=1, source_target_pairs={{0,2},{2,0},{1,3},{3,1},{4,6},{6,4},{5,7},{7,5},{8,10},{10,8},{9,1... | collective-permute-start | bytes 2457608 | tf_op jit(solution)/shard_map/ppermute | solution.py:21
  32.8 16.8 %collective-permute-start.12 = (bf16[256,640]{1,0:T(8,128)(2,1)S(1)}, bf16[256,640]{1,0:T(8,128)(2,1)}, u32[]{:S(2)}, u32[]{:S(2)}) collective-permute-start(bf16[256,640]{1,0:T(8,128)(2,1)S(1)} %shard_map.56), channel_id=1, source_target_pairs={{0,16},{16,0},{1,17},{17,1},{2,18},{18,2},{3,19},{19,3},{4,20},{20... | collective-permute-start | bytes 983048 | tf_op jit(solution)/shard_map/ppermute | solution.py:21
  36.1 16.3 %collective-permute-start.6 = (bf16[256,640]{1,0:T(8,128)(2,1)S(1)}, bf16[256,640]{1,0:T(8,128)(2,1)S(1)}, u32[]{:S(2)}, u32[]{:S(2)}) collective-permute-start(bf16[256,640]{1,0:T(8,128)(2,1)S(1)} %shard_map.55), channel_id=1, source_target_pairs={{0,2},{2,0},{1,3},{3,1},{4,6},{6,4},{5,7},{7,5},{8,10},{10,8},{9,1... | collective-permute-start | bytes 983048 | tf_op jit(solution)/shard_map/ppermute | solution.py:21
  37.8 23.2 %copy-start.7 = (bf16[256,640]{0,1:T(8,128)(2,1)}, bf16[256,640]{0,1:T(8,128)(2,1)S(1)}, u32[]{:S(2)}) copy-start(bf16[256,640]{0,1:T(8,128)(2,1)S(1)} %copy.6) | copy-start | bytes 983044
  50.7 6.9 %copy-start.9 = (bf16[256,640]{0,1:T(8,128)(2,1)}, bf16[256,640]{0,1:T(8,128)(2,1)S(1)}, u32[]{:S(2)}) copy-start(bf16[256,640]{0,1:T(8,128)(2,1)S(1)} %copy.8) | copy-start | bytes 983044
  50.8 17.2 %collective-permute-start.13 = (bf16[256,640]{1,0:T(8,128)(2,1)}, bf16[256,640]{1,0:T(8,128)(2,1)}, u32[]{:S(2)}, u32[]{:S(2)}) collective-permute-start(bf16[256,640]{1,0:T(8,128)(2,1)} %collective-permute-done.12), channel_id=1, source_target_pairs={{0,2},{2,0},{1,3},{3,1},{4,6},{6,4},{5,7},{7,5},{8,10},{10,8},{9,1... | collective-permute-start | bytes 983048 | tf_op jit(solution)/shard_map/ppermute | solution.py:21
  53.8 39.3 %collective-permute-start.9 = (bf16[160,2560]{1,0:T(8,128)(2,1)}, bf16[160,2560]{1,0:T(8,128)(2,1)}, u32[]{:S(2)}, u32[]{:S(2)}) collective-permute-start(bf16[160,2560]{1,0:T(8,128)(2,1)} %collective-permute-done.7), channel_id=1, source_target_pairs={{0,8},{8,0},{1,9},{9,1},{2,10},{10,2},{3,11},{11,3},{4,12},{12,4},... | collective-permute-start | bytes 2457608 | tf_op jit(solution)/shard_map/ppermute | solution.py:21
  53.9 21.5 %collective-permute-start.8 = (bf16[160,2560]{1,0:T(8,128)(2,1)}, bf16[160,2560]{1,0:T(8,128)(2,1)S(1)}, u32[]{:S(2)}, u32[]{:S(2)}) collective-permute-start(bf16[160,2560]{1,0:T(8,128)(2,1)} %collective-permute-done.7), channel_id=1, source_target_pairs={{0,4},{4,0},{1,5},{5,1},{2,6},{6,2},{3,7},{7,3},{8,12},{12,8},{9,1... | collective-permute-start | bytes 2457608 | tf_op jit(solution)/shard_map/ppermute | solution.py:21
  54.0 37.3 %collective-permute-start.5 = (bf16[160,2560]{1,0:T(8,128)(2,1)}, bf16[160,2560]{1,0:T(8,128)(2,1)}, u32[]{:S(2)}, u32[]{:S(2)}) collective-permute-start(bf16[160,2560]{1,0:T(8,128)(2,1)} %collective-permute-done.4), channel_id=1, source_target_pairs={{0,4},{4,0},{1,5},{5,1},{2,6},{6,2},{3,7},{7,3},{8,12},{12,8},{9,1... | collective-permute-start | bytes 2457608 | tf_op jit(solution)/shard_map/ppermute | solution.py:21
  57.7 3.4 %copy-start.5 = (f32[256,2560]{1,0:T(8,128)S(1)}, f32[256,2560]{1,0:T(8,128)}, u32[]{:S(2)}) copy-start(f32[256,2560]{1,0:T(8,128)} %fusion.27) | copy-start | bytes 7864324
  69.9 21.4 %copy-start.4 = (f32[256,2560]{1,0:T(8,128)S(1)}, f32[256,2560]{1,0:T(8,128)}, u32[]{:S(2)}) copy-start(f32[256,2560]{1,0:T(8,128)} %convolution_add_fusion.3) | copy-start | bytes 7864324
  71.9 21.3 %copy-start.10 = (bf16[256,640]{0,1:T(8,128)(2,1)S(1)}, bf16[256,640]{0,1:T(8,128)(2,1)}, u32[]{:S(2)}) copy-start(bf16[256,640]{0,1:T(8,128)(2,1)} %copy.9) | copy-start | bytes 983044
  75.3 22.0 %collective-permute-start.10 = (bf16[160,2560]{1,0:T(8,128)(2,1)S(1)}, bf16[160,2560]{1,0:T(8,128)(2,1)S(1)}, u32[]{:S(2)}, u32[]{:S(2)}) collective-permute-start(bf16[160,2560]{1,0:T(8,128)(2,1)S(1)} %collective-permute-done.8), channel_id=1, source_target_pairs={{0,8},{8,0},{1,9},{9,1},{2,10},{10,2},{3,11},{11,3},{4,12},{12,4},... | collective-permute-start | bytes 2457608 | tf_op jit(solution)/shard_map/ppermute | solution.py:21
  93.1 1.8 %copy-start.8 = (bf16[256,640]{0,1:T(8,128)(2,1)S(1)}, bf16[256,640]{0,1:T(8,128)(2,1)}, u32[]{:S(2)}) copy-start(bf16[256,640]{0,1:T(8,128)(2,1)} %copy.7) | copy-start | bytes 983044
  97.8 1.7 %copy-start.6 = (f32[256,2560]{1,0:T(8,128)S(1)}, f32[256,2560]{1,0:T(8,128)}, u32[]{:S(2)}) copy-start(f32[256,2560]{1,0:T(8,128)} %fusion.22) | copy-start | bytes 7864324
  97.9 4.9 %collective-permute-start.14 = (f32[256,1280]{1,0:T(8,128)S(1)}, f32[256,1280]{1,0:T(8,128)S(1)}, u32[]{:S(2)}, u32[]{:S(2)}) collective-permute-start(f32[256,1280]{1,0:T(8,128)S(1)} %slice.99), channel_id=1, source_target_pairs={{0,1},{1,0},{2,3},{3,2},{4,5},{5,4},{6,7},{7,6},{8,9},{9,8},{10,11... | collective-permute-start | bytes 3932168 | tf_op jit(solution)/shard_map/ppermute | solution.py:21
  102.7 3.1 %collective-permute-start.11 = (f32[256,1280]{1,0:T(8,128)S(1)}, f32[256,1280]{1,0:T(8,128)S(1)}, u32[]{:S(2)}, u32[]{:S(2)}) collective-permute-start(f32[256,1280]{1,0:T(8,128)S(1)} %slice.89), channel_id=1, source_target_pairs={{0,1},{1,0},{2,3},{3,2},{4,5},{5,4},{6,7},{7,6},{8,9},{9,8},{10,11... | collective-permute-start | bytes 3932168 | tf_op jit(solution)/shard_map/ppermute | solution.py:21
  103.0 32.1 %collective-permute-start.15 = (bf16[256,1280]{1,0:T(8,128)(2,1)S(1)}, bf16[256,1280]{1,0:T(8,128)(2,1)S(1)}, u32[]{:S(2)}, u32[]{:S(2)}) collective-permute-start(bf16[256,1280]{1,0:T(8,128)(2,1)S(1)} %fusion.4), channel_id=1, source_target_pairs={{0,16},{16,0},{1,17},{17,1},{2,18},{18,2},{3,19},{19,3},{4,20},{20... | collective-permute-start | bytes 1966088 | tf_op jit(solution)/shard_map/ppermute | solution.py:21

commit v4 on v3

--- a/solution.py
+++ b/solution.py
@@ -11,7 +11,7 @@
 HEAD_DIM = 128
 ANC = 3
 NEG_BIG = -1e30
-CHUNKS = 1
+CHUNKS = 2
 
 NODE_AXES = ("h", "q", "l", "x")
 HEAD_AXES = ("y", "c")
@@ -90,6 +90,42 @@
     )(jnp.stack([half, node]).astype(jnp.int32), parents, lengths, query, *kv_blocks)
 
 
+def project_kernel(where_ref, far_ref, far_y_ref, near_ref, near_y_ref, *refs):
+    pieces, (theirs_ref, mine_ref, weight_ref) = refs[:8], refs[8:]
+    rows, depth = pieces[0].shape[0], far_ref.shape[1]
+    tokens, half = far_ref.shape[0], theirs_ref.shape[1]
+    for i, piece in enumerate(pieces):
+        block = where_ref[0] ^ (i % 4)
+        start = pl.multiple_of(block * rows + (i // 4) * depth, 32)
+        weight_ref[pl.ds(start, rows), :] = piece[...]
+    for place, (a_ref, b_ref) in enumerate([(far_ref, far_y_ref), (near_ref, near_y_ref)]):
+        out_rows = slice(place * tokens, (place + 1) * tokens)
+        for out_ref, cols in ((theirs_ref, slice(0, half)), (mine_ref, slice(half, 2 * half))):
+            total = jnp.dot(a_ref[...], weight_ref[:depth, cols], preferred_element_type=jnp.float32)
+            total = total + jnp.dot(b_ref[...], weight_ref[depth:, cols], preferred_element_type=jnp.float32)
+            out_ref[out_rows, :] = total
+
+
+def project(place, inputs, pieces):
+    tokens, depth = inputs[0].shape
+    columns = pieces[0].shape[1]
+    vmem = pl.BlockSpec(memory_space=pltpu.VMEM)
+    out = jax.ShapeDtypeStruct((2 * tokens, columns // 2), jnp.float32)
+    return pl.pallas_call(
+        project_kernel,
+        out_shape=(out, out),
+        in_specs=[pl.BlockSpec(memory_space=pltpu.SMEM)] + [vmem] * (len(inputs) + len(pieces)),
+        out_specs=(vmem, vmem),
+        scratch_shapes=[pltpu.VMEM((2 * depth, columns), jnp.bfloat16)],
+        compiler_params=pltpu.CompilerParams(vmem_limit_bytes=24 * 2**20),
+        cost_estimate=pl.CostEstimate(
+            flops=2 * tokens * 2 * depth * columns,
+            bytes_accessed=4 * depth * columns + 8 * tokens * columns,
+            transcendentals=0,
+        ),
+    )(jnp.reshape(place, (1,)).astype(jnp.int32), *inputs, *pieces)
+
+
 def per_device(query, keys_values, out_weight, parents, lengths):
     h, l, x = lax.axis_index("h"), lax.axis_index("l"), lax.axis_index("x")
     y, c = lax.axis_index("y"), lax.axis_index("c")
@@ -119,24 +155,21 @@
     far = swapped(sent, "h")
     near = attend(h, node, parents, lengths, query, kv_blocks)
 
-    def blocks_of(attended):
-        tokens = attended.shape[0]
-        split = attended.reshape(tokens, parts, 4, -1)
-        b = [split[:, :, i].reshape(tokens, -1) for i in range(4)]
-        b = [jnp.where(x > 0, b[i ^ 1], b[i]) for i in range(4)]
-        return [jnp.where(l > 0, b[i ^ 2], b[i]) for i in range(4)]
+    def ordered(attended):
+        if parts == 1:
+            return attended
+        split = attended.reshape(attended.shape[0], parts, 4, -1)
+        return jnp.swapaxes(split, 1, 2).reshape(attended.shape)
 
-    near_blocks = blocks_of(near) + blocks_of(swapped(near, "y"))
-    far_blocks = blocks_of(far) + blocks_of(swapped(far, "y"))
-
-    def summed(blocks, pieces):
-        total = sum(jnp.dot(a, w, preferred_element_type=jnp.float32) for a, w in zip(blocks, pieces))
-        return total[:, step:] + swapped(total[:, :step], "c")
-
+    near, far = ordered(near), ordered(far)
+    tokens = near.shape[0]
+    inputs = [far, swapped(far, "y"), near, swapped(near, "y")]
     outputs = []
     for pieces in chunks:
-        arrived = swapped(summed(far_blocks, pieces).astype(jnp.bfloat16), "h")
-        outputs.append((summed(near_blocks, pieces) + arrived.astype(jnp.float32)).astype(jnp.bfloat16))
+        theirs, mine = project(l * 2 + x, inputs, pieces)
+        both = mine + swapped(theirs, "c")
+        arrived = swapped(both[:tokens].astype(jnp.bfloat16), "h")
+        outputs.append((both[tokens:] + arrived.astype(jnp.float32)).astype(jnp.bfloat16))
     return jnp.concatenate(outputs, 1)
 
 

time: 137 us -> 120 us (0.88)
  matrix products: 26.1 us -> 0 us
  waiting for transfers between devices: 73.4 us -> 80.8 us
  local copies, waits for them, and re-layouts: 7.47 us -> 1.73 us
  Pallas kernels: 6.4 us -> 11.8 us
  starting transfers between devices: 19.2 us -> 22.4 us
    dot_general x16 -> x0, matrix products: 26.1 us -> none  [summed(): jnp.dot(a, w, preferred_element_type=jnp.float32)]
    ppermute x13 -> x21, waiting for transfers between devices: 58.1 us -> 65.3 us  [swapped(): return lax.ppermute(value, axis, [(0, 1), (1, 0)])]
    pallas_call x0 -> x2, Pallas kernels: none -> 5.39 us  [project(): pl.pallas_call(project_kernel, out_shape=(out, out), in_specs=[pl.BlockSp...]
    ppermute x3 -> x0, local copies, waits for them, and re-layouts: 3.94 us -> none  [swapped(): return lax.ppermute(value, axis, [(0, 1), (1, 0)])]
    ppermute x13 -> x21, starting transfers between devices: 12.1 us -> 15.3 us  [swapped(): return lax.ppermute(value, axis, [(0, 1), (1, 0)])]
    unnamed x22 -> x8, local copies, waits for them, and re-layouts: 1.6 us -> 0.01 us
  transfers between devices with their start and end apart: 16 -> 24, of which waited for: 7 -> 13; matrix products, arithmetic and copies ran while one was open for 25% -> 3% of each run, Pallas kernels for 5% -> 10%
where the time goes in v4:
time: 120 us
  waiting for transfers between devices  80.8 us (67%)
  starting transfers between devices  22.4 us (19%)
  Pallas kernels  11.8 us (10%)
  other arithmetic  3.08 us (3%)
  local copies, waits for them, and re-layouts  1.73 us (1%)
    ppermute x21, waiting for transfers between devices, swapped(): return lax.ppermute(value, axis, [(0, 1), (1, 0)])  65.3 us
    ppermute x3, waiting for transfers between devices, passed_along(): lax.ppermute(value, NODE_AXES, [(i, (i + by) % size) for i in range(size)])  15.4 us
    ppermute x21, starting transfers between devices, swapped(): return lax.ppermute(value, axis, [(0, 1), (1, 0)])  15.3 us
    ppermute x3, starting transfers between devices, passed_along(): lax.ppermute(value, NODE_AXES, [(i, (i + by) % size) for i in range(size)])  7.08 us
    pallas_call x2, Pallas kernels, attend(): pl.pallas_call(attend_kernel, out_shape=jax.ShapeDtypeStruct((capacity, w...  6.39 us
    pallas_call x2, Pallas kernels, project(): pl.pallas_call(project_kernel, out_shape=(out, out), in_specs=[pl.BlockSp...  5.39 us
  transfers between devices with their start and end apart: 24, of which 13 were waited for; matrix products, arithmetic and copies ran while one was open for 3% of the time, Pallas kernels for 10%

profile of v4, /device:TPU:0, one launch (start us, length us, event | category | flops | bytes accessed | tf_op | source)
XLA Modules:
  0.0 119.9 jit_solution(6261644075353125908)
XLA Ops:
  0.0 2.9 %collective-permute-start = (bf16[2,256,256]{2,1,0:T(8,128)(2,1)}, bf16[2,256,256]{2,1,0:T(8,128)(2,1)S(1)}, u32[]{:S(2)}, u32[]{:S(2)}) collective-permute-start(bf16[2,256,256]{2,1,0:T(8,128)(2,1)} %refs_0_.3), channel_id=1, source_target_pairs={{0,4},{4,8},{8,12},{12,16},{16,20},{20,24},{24,28},{28,0},{1,5},{5... | collective-permute-start | bytes 786440 | tf_op jit(solution)/shard_map/ppermute | solution.py:26
  2.9 1.6 %collective-permute-start.1 = (bf16[2,256,256]{2,1,0:T(8,128)(2,1)}, bf16[2,256,256]{2,1,0:T(8,128)(2,1)S(1)}, u32[]{:S(2)}, u32[]{:S(2)}) collective-permute-start(bf16[2,256,256]{2,1,0:T(8,128)(2,1)} %refs_0_.3), channel_id=1, source_target_pairs={{0,8},{4,12},{8,16},{12,20},{16,24},{20,28},{24,0},{28,4},{1,9},{5... | collective-permute-start | bytes 786440 | tf_op jit(solution)/shard_map/ppermute | solution.py:26
  4.5 2.6 %collective-permute-start.2 = (bf16[2,256,256]{2,1,0:T(8,128)(2,1)}, bf16[2,256,256]{2,1,0:T(8,128)(2,1)S(1)}, u32[]{:S(2)}, u32[]{:S(2)}) collective-permute-start(bf16[2,256,256]{2,1,0:T(8,128)(2,1)} %refs_0_.3), channel_id=1, source_target_pairs={{0,12},{4,16},{8,20},{12,24},{16,28},{20,0},{24,4},{28,8},{1,13},{... | collective-permute-start | bytes 786440 | tf_op jit(solution)/shard_map/ppermute | solution.py:26
  7.1 1.6 %constant_dynamic-slice_fusion.5 = (bf16[160,640]{1,0:T(8,128)(2,1)S(1)}, bf16[160,640]{1,0:T(8,128)(2,1)S(1)}, bf16[160,640]{1,0:T(8,128)(2,1)S(1)}, bf16[160,6...) fusion(bf16[160,5120]{1,0:T(8,128)(2,1)} %param.7, ...), kind=kLoop, calls=%fused_computation.16 | loop fusion | bytes 3276832 | tf_op jit(solution)/shard_map/dynamic_slice | solution.py:143
  8.7 0.8 pad_maximum_fusion.2
  9.5 1.6 %collective-permute-start.9 = (bf16[160,1280]{1,0:T(8,128)(2,1)}, bf16[160,1280]{1,0:T(8,128)(2,1)S(1)}, u32[]{:S(2)}, u32[]{:S(2)}) collective-permute-start(bf16[160,1280]{1,0:T(8,128)(2,1)} %pad_maximum_fusion.2), channel_id=1, source_target_pairs={{0,2},{2,0},{1,3},{3,1},{4,6},{6,4},{5,7},{7,5},{8,10},{10,8},{9,1... | collective-permute-start | bytes 1228808 | tf_op jit(solution)/shard_map/ppermute | solution.py:21
  11.1 0.3 collective-permute-start.7
  11.4 0.8 pad_maximum_fusion.4
  12.2 1.2 %collective-permute-done.refs_1_ = bf16[2,256,256]{2,1,0:T(8,128)(2,1)S(1)} collective-permute-done((bf16[2,256,256]{2,1,0:T(8,128)(2,1)}, bf16[2,256,256]{2,1,0:T(8,128)(2,1)S(1)}, u32[]{:S(2)}, u32[]{:S(2)}) %collective-permute-start) | collective-permute-done | bytes 262176 | tf_op jit(solution)/shard_map/ppermute | solution.py:26
  13.7 0.5 collective-permute-done.1.refs_2_
  14.3 1.5 %collective-permute-start.18 = (bf16[160,1280]{1,0:T(8,128)(2,1)}, bf16[160,1280]{1,0:T(8,128)(2,1)S(1)}, u32[]{:S(2)}, u32[]{:S(2)}) collective-permute-start(bf16[160,1280]{1,0:T(8,128)(2,1)} %pad_maximum_fusion.4), channel_id=1, source_target_pairs={{0,2},{2,0},{1,3},{3,1},{4,6},{6,4},{5,7},{7,5},{8,10},{10,8},{9,1... | collective-permute-start | bytes 1228808 | tf_op jit(solution)/shard_map/ppermute | solution.py:21
  15.8 13.7 %collective-permute-done.2.refs_3_ = bf16[2,256,256]{2,1,0:T(8,128)(2,1)S(1)} collective-permute-done((bf16[2,256,256]{2,1,0:T(8,128)(2,1)}, bf16[2,256,256]{2,1,0:T(8,128)(2,1)S(1)}, u32[]{:S(2)}, u32[]{:S(2)}) %collective-permute-start.2) | collective-permute-done | bytes 262176 | tf_op jit(solution)/shard_map/ppermute | solution.py:26
  29.6 3.2 %shard_map.55 = bf16[256,640]{1,0:T(8,128)(2,1)S(1)} custom-call(s32[2]{0:T(128)S(1)} %pad_add_fusion.where_ref, s32[8]{0:T(128)S(1)} %copy-done.2, s32[8]{0:T(128)S(1)} %copy-done.3, bf16[256,1280]{1,0:T(8,128)(2,1)S(1)} %copy-done, bf16[2,256,256]{2,1,0:T(8,128)(2,1)S(1)} %copy-done.1, bf16[2,256,256]{2,1,0:T(8,128)(2,1)S(1)} %collective-permute-done.refs_1_, ...), custom_call_target="tpu_custom_call" | custom-call | flops 167772160 | bytes 1179648 | tf_op jit(solution)/shard_map/pallas_call | solution.py:74
  32.8 2.2 %collective-permute-start.3 = (bf16[256,640]{1,0:T(8,128)(2,1)S(1)}, bf16[256,640]{1,0:T(8,128)(2,1)S(1)}, u32[]{:S(2)}, u32[]{:S(2)}) collective-permute-start(bf16[256,640]{1,0:T(8,128)(2,1)S(1)} %shard_map.55), channel_id=1, source_target_pairs={{0,16},{16,0},{1,17},{17,1},{2,18},{18,2},{3,19},{19,3},{4,20},{20... | collective-permute-start | bytes 983048 | tf_op jit(solution)/shard_map/ppermute | solution.py:21
  35.1 3.2 %shard_map.56.near_ref = bf16[256,640]{1,0:T(8,128)(2,1)S(1)} custom-call(s32[2]{0:T(128)S(1)} %pad_add_fusion.1.where_ref, s32[8]{0:T(128)S(1)} %copy-done.2, s32[8]{0:T(128)S(1)} %copy-done.3, bf16[256,1280]{1,0:T(8,128)(2,1)S(1)} %copy-done, bf16[2,256,256]{2,1,0:T(8,128)(2,1)S(1)} %copy-done.1, bf16[2,256,256]{2,1,0:T(8,128)(2,1)S(1)} %collective-permute-done.refs_1_, ...), custom_call_target="tpu_custom_call" | custom-call | flops 167772160 | bytes 1179648 | tf_op jit(solution)/shard_map/pallas_call | solution.py:74
  38.3 1.6 %collective-permute-start.5 = (bf16[256,640]{1,0:T(8,128)(2,1)S(1)}, bf16[256,640]{1,0:T(8,128)(2,1)S(1)}, u32[]{:S(2)}, u32[]{:S(2)}) collective-permute-start(bf16[256,640]{1,0:T(8,128)(2,1)S(1)} %shard_map.56.near_ref), channel_id=1, source_target_pairs={{0,2},{2,0},{1,3},{3,1},{4,6},{6,4},{5,7},{7,5},{8,10},{10,8},{9,1... | collective-permute-start | bytes 983048 | tf_op jit(solution)/shard_map/ppermute | solution.py:21
  39.9 5.5 %collective-permute-done.16.refs_2_ = bf16[160,1280]{1,0:T(8,128)(2,1)S(1)} collective-permute-done((bf16[160,1280]{1,0:T(8,128)(2,1)S(1)}, bf16[160,1280]{1,0:T(8,128)(2,1)S(1)}, u32[]{:S(2)}, u32[]{:S(2)}) %collective-permute-start.16) | collective-permute-done | bytes 409632 | tf_op jit(solution)/shard_map/ppermute | solution.py:21
  45.4 3.6 %collective-permute-start.8 = (bf16[160,1280]{1,0:T(8,128)(2,1)S(1)}, bf16[160,1280]{1,0:T(8,128)(2,1)S(1)}, u32[]{:S(2)}, u32[]{:S(2)}) collective-permute-start(bf16[160,1280]{1,0:T(8,128)(2,1)S(1)} %collective-permute-done.7.refs_2_), channel_id=1, source_target_pairs={{0,4},{4,0},{1,5},{5,1},{2,6},{6,2},{3,7},{7,3},{8,12},{12,8},{9,1... | collective-permute-start | bytes 1228808 | tf_op jit(solution)/shard_map/ppermute | solution.py:21
  49.0 1.6 %collective-permute-done.3.far_ref = bf16[256,640]{1,0:T(8,128)(2,1)S(1)} collective-permute-done((bf16[256,640]{1,0:T(8,128)(2,1)S(1)}, bf16[256,640]{1,0:T(8,128)(2,1)S(1)}, u32[]{:S(2)}, u32[]{:S(2)}) %collective-permute-start.3) | collective-permute-done | bytes 327712 | tf_op jit(solution)/shard_map/ppermute | solution.py:21
  50.5 1.5 %collective-permute-start.4 = (bf16[256,640]{1,0:T(8,128)(2,1)S(1)}, bf16[256,640]{1,0:T(8,128)(2,1)S(1)}, u32[]{:S(2)}, u32[]{:S(2)}) collective-permute-start(bf16[256,640]{1,0:T(8,128)(2,1)S(1)} %collective-permute-done.3.far_ref), channel_id=1, source_target_pairs={{0,2},{2,0},{1,3},{3,1},{4,6},{6,4},{5,7},{7,5},{8,10},{10,8},{9,1... | collective-permute-start | bytes 983048 | tf_op jit(solution)/shard_map/ppermute | solution.py:21
  52.1 5.5 %collective-permute-done.11.refs_6_ = bf16[160,1280]{1,0:T(8,128)(2,1)S(1)} collective-permute-done((bf16[160,1280]{1,0:T(8,128)(2,1)S(1)}, bf16[160,1280]{1,0:T(8,128)(2,1)S(1)}, u32[]{:S(2)}, u32[]{:S(2)}) %collective-permute-start.11) | collective-permute-done | bytes 409632 | tf_op jit(solution)/shard_map/ppermute | solution.py:21
  57.7 1.5 %collective-permute-done.8.refs_3_ = bf16[160,1280]{1,0:T(8,128)(2,1)S(1)} collective-permute-done((bf16[160,1280]{1,0:T(8,128)(2,1)S(1)}, bf16[160,1280]{1,0:T(8,128)(2,1)S(1)}, u32[]{:S(2)}, u32[]{:S(2)}) %collective-permute-start.8) | collective-permute-done | bytes 409632 | tf_op jit(solution)/shard_map/ppermute | solution.py:21
  59.2 8.8 %collective-permute-done.19.refs_5_ = bf16[160,1280]{1,0:T(8,128)(2,1)S(1)} collective-permute-done((bf16[160,1280]{1,0:T(8,128)(2,1)S(1)}, bf16[160,1280]{1,0:T(8,128)(2,1)S(1)}, u32[]{:S(2)}, u32[]{:S(2)}) %collective-permute-start.19) | collective-permute-done | bytes 409632 | tf_op jit(solution)/shard_map/ppermute | solution.py:21
  68.0 2.1 %collective-permute-start.17 = (bf16[160,1280]{1,0:T(8,128)(2,1)S(1)}, bf16[160,1280]{1,0:T(8,128)(2,1)S(1)}, u32[]{:S(2)}, u32[]{:S(2)}) collective-permute-start(bf16[160,1280]{1,0:T(8,128)(2,1)S(1)} %collective-permute-done.16.refs_2_), channel_id=1, source_target_pairs={{0,4},{4,0},{1,5},{5,1},{2,6},{6,2},{3,7},{7,3},{8,12},{12,8},{9,1... | collective-permute-start | bytes 1228808 | tf_op jit(solution)/shard_map/ppermute | solution.py:21
  70.1 2.7 %shard_map.57 = (f32[512,640]{1,0:T(8,128)S(1)}, f32[512,640]{1,0:T(8,128)S(1)}) custom-call(s32[1]{0:T(128)} %bitcast.where_ref, bf16[256,640]{1,0:T(8,128)(2,1)S(1)} %collective-permute-done.3.far_ref, bf16[256,640]{1,0:T(8,128)(2,1)S(1)} %collective-permute-done.4.far_y_ref, bf16[256,640]{1,0:T(8,128)(2,1)S(1)} %shard_map.56.near_ref, ...), custom_call_target="tpu_custom_call" | custom-call | flops 838860800 | bytes 5898240 | tf_op jit(solution)/shard_map/pallas_call | solution.py:114
  72.9 3.9 %collective-permute-done.15.refs_1_ = bf16[160,1280]{1,0:T(8,128)(2,1)S(1)} collective-permute-done((bf16[160,1280]{1,0:T(8,128)(2,1)S(1)}, bf16[160,1280]{1,0:T(8,128)(2,1)S(1)}, u32[]{:S(2)}, u32[]{:S(2)}) %collective-permute-start.15) | collective-permute-done | bytes 409632 | tf_op jit(solution)/shard_map/ppermute | solution.py:21
  76.8 8.0 %collective-permute-done.17.refs_3_ = bf16[160,1280]{1,0:T(8,128)(2,1)S(1)} collective-permute-done((bf16[160,1280]{1,0:T(8,128)(2,1)S(1)}, bf16[160,1280]{1,0:T(8,128)(2,1)S(1)}, u32[]{:S(2)}, u32[]{:S(2)}) %collective-permute-start.17) | collective-permute-done | bytes 409632 | tf_op jit(solution)/shard_map/ppermute | solution.py:21
  84.9 2.7 %shard_map.58 = (f32[512,640]{1,0:T(8,128)S(1)}, f32[512,640]{1,0:T(8,128)S(1)}) custom-call(s32[1]{0:T(128)} %bitcast.where_ref, bf16[256,640]{1,0:T(8,128)(2,1)S(1)} %collective-permute-done.3.far_ref, bf16[256,640]{1,0:T(8,128)(2,1)S(1)} %collective-permute-done.4.far_y_ref, bf16[256,640]{1,0:T(8,128)(2,1)S(1)} %shard_map.56.near_ref, ...), custom_call_target="tpu_custom_call" | custom-call | flops 838860800 | bytes 5898240 | tf_op jit(solution)/shard_map/pallas_call | solution.py:114
  87.9 2.7 %collective-permute-done.22 = f32[512,640]{1,0:T(8,128)S(1)} collective-permute-done((f32[512,640]{1,0:T(8,128)S(1)}, f32[512,640]{1,0:T(8,128)S(1)}, u32[]{:S(2)}, u32[]{:S(2)}) %collective-permute-start.22) | collective-permute-done | bytes 1310752 | tf_op jit(solution)/shard_map/ppermute | solution.py:21
  91.1 20.9 %collective-permute-done.14 = bf16[256,640]{1,0:T(8,128)(2,1)S(1)} collective-permute-done((bf16[256,640]{1,0:T(8,128)(2,1)S(1)}, bf16[256,640]{1,0:T(8,128)(2,1)S(1)}, u32[]{:S(2)}, u32[]{:S(2)}) %collective-permute-start.14) | collective-permute-done | bytes 327712 | tf_op jit(solution)/shard_map/ppermute | solution.py:21
  112.0 6.9 %collective-permute-done.23 = bf16[256,640]{1,0:T(8,128)(2,1)S(1)} collective-permute-done((bf16[256,640]{1,0:T(8,128)(2,1)S(1)}, bf16[256,640]{1,0:T(8,128)(2,1)S(1)}, u32[]{:S(2)}, u32[]{:S(2)}) %collective-permute-start.23) | collective-permute-done | bytes 327712 | tf_op jit(solution)/shard_map/ppermute | solution.py:21
  119.0 0.9 pad_maximum_fusion
  (42 shorter events, 1.7 us)
Async XLA Ops:
  0.0 13.4 %collective-permute-start = (bf16[2,256,256]{2,1,0:T(8,128)(2,1)}, bf16[2,256,256]{2,1,0:T(8,128)(2,1)S(1)}, u32[]{:S(2)}, u32[]{:S(2)}) collective-permute-start(bf16[2,256,256]{2,1,0:T(8,128)(2,1)} %refs_0_.3), channel_id=1, source_target_pairs={{0,4},{4,8},{8,12},{12,16},{16,20},{20,24},{24,28},{28,0},{1,5},{5... | collective-permute-start | bytes 786440 | tf_op jit(solution)/shard_map/ppermute | solution.py:26
  2.9 11.3 %collective-permute-start.1 = (bf16[2,256,256]{2,1,0:T(8,128)(2,1)}, bf16[2,256,256]{2,1,0:T(8,128)(2,1)S(1)}, u32[]{:S(2)}, u32[]{:S(2)}) collective-permute-start(bf16[2,256,256]{2,1,0:T(8,128)(2,1)} %refs_0_.3), channel_id=1, source_target_pairs={{0,8},{4,12},{8,16},{12,20},{16,24},{20,28},{24,0},{28,4},{1,9},{5... | collective-permute-start | bytes 786440 | tf_op jit(solution)/shard_map/ppermute | solution.py:26
  4.5 25.0 %collective-permute-start.2 = (bf16[2,256,256]{2,1,0:T(8,128)(2,1)}, bf16[2,256,256]{2,1,0:T(8,128)(2,1)S(1)}, u32[]{:S(2)}, u32[]{:S(2)}) collective-permute-start(bf16[2,256,256]{2,1,0:T(8,128)(2,1)} %refs_0_.3), channel_id=1, source_target_pairs={{0,12},{4,16},{8,20},{12,24},{16,28},{20,0},{24,4},{28,8},{1,13},{... | collective-permute-start | bytes 786440 | tf_op jit(solution)/shard_map/ppermute | solution.py:26
  9.5 20.1 %copy-start = (bf16[256,1280]{1,0:T(8,128)(2,1)S(1)}, bf16[256,1280]{1,0:T(8,128)(2,1)}, u32[]{:S(2)}) copy-start(bf16[256,1280]{1,0:T(8,128)(2,1)} %query_ref.3) | copy-start | bytes 1966084
  9.5 20.1 %copy-start.1 = (bf16[2,256,256]{2,1,0:T(8,128)(2,1)S(1)}, bf16[2,256,256]{2,1,0:T(8,128)(2,1)}, u32[]{:S(2)}) copy-start(bf16[2,256,256]{2,1,0:T(8,128)(2,1)} %refs_0_.3) | copy-start | bytes 786436
  9.5 20.1 %copy-start.2 = (s32[8]{0:T(128)S(1)}, s32[8]{0:T(128)}, u32[]{:S(2)}) copy-start(s32[8]{0:T(128)} %parents_ref.3) | copy-start | bytes 100
  9.5 20.1 %copy-start.3 = (s32[8]{0:T(128)S(1)}, s32[8]{0:T(128)}, u32[]{:S(2)}) copy-start(s32[8]{0:T(128)} %lengths_ref.3) | copy-start | bytes 100
  9.5 23.3 %collective-permute-start.9 = (bf16[160,1280]{1,0:T(8,128)(2,1)}, bf16[160,1280]{1,0:T(8,128)(2,1)S(1)}, u32[]{:S(2)}, u32[]{:S(2)}) collective-permute-start(bf16[160,1280]{1,0:T(8,128)(2,1)} %pad_maximum_fusion.2), channel_id=1, source_target_pairs={{0,2},{2,0},{1,3},{3,1},{4,6},{6,4},{5,7},{7,5},{8,10},{10,8},{9,1... | collective-permute-start | bytes 1228808 | tf_op jit(solution)/shard_map/ppermute | solution.py:21
  11.1 23.9 %collective-permute-start.7 = (bf16[160,1280]{1,0:T(8,128)(2,1)S(1)}, bf16[160,1280]{1,0:T(8,128)(2,1)S(1)}, u32[]{:S(2)}, u32[]{:S(2)}) collective-permute-start(bf16[160,1280]{1,0:T(8,128)(2,1)S(1)} %pad_maximum_fusion.1.refs_0_), channel_id=1, source_target_pairs={{0,8},{8,0},{1,9},{9,1},{2,10},{10,2},{3,11},{11,3},{4,12},{12,4},... | collective-permute-start | bytes 1228808 | tf_op jit(solution)/shard_map/ppermute | solution.py:21
  13.4 24.9 %collective-permute-start.6 = (bf16[160,1280]{1,0:T(8,128)(2,1)S(1)}, bf16[160,1280]{1,0:T(8,128)(2,1)S(1)}, u32[]{:S(2)}, u32[]{:S(2)}) collective-permute-start(bf16[160,1280]{1,0:T(8,128)(2,1)S(1)} %pad_maximum_fusion.1.refs_0_), channel_id=1, source_target_pairs={{0,4},{4,0},{1,5},{5,1},{2,6},{6,2},{3,7},{7,3},{8,12},{12,8},{9,1... | collective-permute-start | bytes 1228808 | tf_op jit(solution)/shard_map/ppermute | solution.py:21
  14.3 25.6 %collective-permute-start.18 = (bf16[160,1280]{1,0:T(8,128)(2,1)}, bf16[160,1280]{1,0:T(8,128)(2,1)S(1)}, u32[]{:S(2)}, u32[]{:S(2)}) collective-permute-start(bf16[160,1280]{1,0:T(8,128)(2,1)} %pad_maximum_fusion.4), channel_id=1, source_target_pairs={{0,2},{2,0},{1,3},{3,1},{4,6},{6,4},{5,7},{7,5},{8,10},{10,8},{9,1... | collective-permute-start | bytes 1228808 | tf_op jit(solution)/shard_map/ppermute | solution.py:21
  29.5 15.9 %collective-permute-start.16 = (bf16[160,1280]{1,0:T(8,128)(2,1)S(1)}, bf16[160,1280]{1,0:T(8,128)(2,1)S(1)}, u32[]{:S(2)}, u32[]{:S(2)}) collective-permute-start(bf16[160,1280]{1,0:T(8,128)(2,1)S(1)} %pad_maximum_fusion.3.refs_0_), channel_id=1, source_target_pairs={{0,8},{8,0},{1,9},{9,1},{2,10},{10,2},{3,11},{11,3},{4,12},{12,4},... | collective-permute-start | bytes 1228808 | tf_op jit(solution)/shard_map/ppermute | solution.py:21
  32.8 17.7 %collective-permute-start.3 = (bf16[256,640]{1,0:T(8,128)(2,1)S(1)}, bf16[256,640]{1,0:T(8,128)(2,1)S(1)}, u32[]{:S(2)}, u32[]{:S(2)}) collective-permute-start(bf16[256,640]{1,0:T(8,128)(2,1)S(1)} %shard_map.55), channel_id=1, source_target_pairs={{0,16},{16,0},{1,17},{17,1},{2,18},{18,2},{3,19},{19,3},{4,20},{20... | collective-permute-start | bytes 983048 | tf_op jit(solution)/shard_map/ppermute | solution.py:21
  35.1 17.0 %collective-permute-start.10 = (bf16[160,1280]{1,0:T(8,128)(2,1)S(1)}, bf16[160,1280]{1,0:T(8,128)(2,1)S(1)}, u32[]{:S(2)}, u32[]{:S(2)}) collective-permute-start(bf16[160,1280]{1,0:T(8,128)(2,1)S(1)} %collective-permute-done.9.refs_4_), channel_id=1, source_target_pairs={{0,4},{4,0},{1,5},{5,1},{2,6},{6,2},{3,7},{7,3},{8,12},{12,8},{9,1... | collective-permute-start | bytes 1228808 | tf_op jit(solution)/shard_map/ppermute | solution.py:21
  38.3 12.2 %collective-permute-start.5 = (bf16[256,640]{1,0:T(8,128)(2,1)S(1)}, bf16[256,640]{1,0:T(8,128)(2,1)S(1)}, u32[]{:S(2)}, u32[]{:S(2)}) collective-permute-start(bf16[256,640]{1,0:T(8,128)(2,1)S(1)} %shard_map.56.near_ref), channel_id=1, source_target_pairs={{0,2},{2,0},{1,3},{3,1},{4,6},{6,4},{5,7},{7,5},{8,10},{10,8},{9,1... | collective-permute-start | bytes 983048 | tf_op jit(solution)/shard_map/ppermute | solution.py:21
  39.9 17.8 %collective-permute-start.11 = (bf16[160,1280]{1,0:T(8,128)(2,1)S(1)}, bf16[160,1280]{1,0:T(8,128)(2,1)S(1)}, u32[]{:S(2)}, u32[]{:S(2)}) collective-permute-start(bf16[160,1280]{1,0:T(8,128)(2,1)S(1)} %collective-permute-done.9.refs_4_), channel_id=1, source_target_pairs={{0,8},{8,0},{1,9},{9,1},{2,10},{10,2},{3,11},{11,3},{4,12},{12,4},... | collective-permute-start | bytes 1228808 | tf_op jit(solution)/shard_map/ppermute | solution.py:21
  45.4 13.9 %collective-permute-start.8 = (bf16[160,1280]{1,0:T(8,128)(2,1)S(1)}, bf16[160,1280]{1,0:T(8,128)(2,1)S(1)}, u32[]{:S(2)}, u32[]{:S(2)}) collective-permute-start(bf16[160,1280]{1,0:T(8,128)(2,1)S(1)} %collective-permute-done.7.refs_2_), channel_id=1, source_target_pairs={{0,4},{4,0},{1,5},{5,1},{2,6},{6,2},{3,7},{7,3},{8,12},{12,8},{9,1... | collective-permute-start | bytes 1228808 | tf_op jit(solution)/shard_map/ppermute | solution.py:21
  50.5 17.5 %collective-permute-start.19 = (bf16[160,1280]{1,0:T(8,128)(2,1)S(1)}, bf16[160,1280]{1,0:T(8,128)(2,1)S(1)}, u32[]{:S(2)}, u32[]{:S(2)}) collective-permute-start(bf16[160,1280]{1,0:T(8,128)(2,1)S(1)} %collective-permute-done.18.refs_4_), channel_id=1, source_target_pairs={{0,4},{4,0},{1,5},{5,1},{2,6},{6,2},{3,7},{7,3},{8,12},{12,8},{9,1... | collective-permute-start | bytes 1228808 | tf_op jit(solution)/shard_map/ppermute | solution.py:21
  50.5 19.6 %collective-permute-start.4 = (bf16[256,640]{1,0:T(8,128)(2,1)S(1)}, bf16[256,640]{1,0:T(8,128)(2,1)S(1)}, u32[]{:S(2)}, u32[]{:S(2)}) collective-permute-start(bf16[256,640]{1,0:T(8,128)(2,1)S(1)} %collective-permute-done.3.far_ref), channel_id=1, source_target_pairs={{0,2},{2,0},{1,3},{3,1},{4,6},{6,4},{5,7},{7,5},{8,10},{10,8},{9,1... | collective-permute-start | bytes 983048 | tf_op jit(solution)/shard_map/ppermute | solution.py:21
  52.0 18.0 %collective-permute-start.12 = (bf16[160,1280]{1,0:T(8,128)(2,1)S(1)}, bf16[160,1280]{1,0:T(8,128)(2,1)S(1)}, u32[]{:S(2)}, u32[]{:S(2)}) collective-permute-start(bf16[160,1280]{1,0:T(8,128)(2,1)S(1)} %collective-permute-done.10.refs_5_), channel_id=1, source_target_pairs={{0,8},{8,0},{1,9},{9,1},{2,10},{10,2},{3,11},{11,3},{4,12},{12,4},... | collective-permute-start | bytes 1228808 | tf_op jit(solution)/shard_map/ppermute | solution.py:21
  57.6 19.2 %collective-permute-start.15 = (bf16[160,1280]{1,0:T(8,128)(2,1)S(1)}, bf16[160,1280]{1,0:T(8,128)(2,1)S(1)}, u32[]{:S(2)}, u32[]{:S(2)}) collective-permute-start(bf16[160,1280]{1,0:T(8,128)(2,1)S(1)} %pad_maximum_fusion.3.refs_0_), channel_id=1, source_target_pairs={{0,4},{4,0},{1,5},{5,1},{2,6},{6,2},{3,7},{7,3},{8,12},{12,8},{9,1... | collective-permute-start | bytes 1228808 | tf_op jit(solution)/shard_map/ppermute | solution.py:21
  59.2 25.6 %collective-permute-start.20 = (bf16[160,1280]{1,0:T(8,128)(2,1)S(1)}, bf16[160,1280]{1,0:T(8,128)(2,1)S(1)}, u32[]{:S(2)}, u32[]{:S(2)}) collective-permute-start(bf16[160,1280]{1,0:T(8,128)(2,1)S(1)} %collective-permute-done.18.refs_4_), channel_id=1, source_target_pairs={{0,8},{8,0},{1,9},{9,1},{2,10},{10,2},{3,11},{11,3},{4,12},{12,4},... | collective-permute-start | bytes 1228808 | tf_op jit(solution)/shard_map/ppermute | solution.py:21
  68.0 16.8 %collective-permute-start.17 = (bf16[160,1280]{1,0:T(8,128)(2,1)S(1)}, bf16[160,1280]{1,0:T(8,128)(2,1)S(1)}, u32[]{:S(2)}, u32[]{:S(2)}) collective-permute-start(bf16[160,1280]{1,0:T(8,128)(2,1)S(1)} %collective-permute-done.16.refs_2_), channel_id=1, source_target_pairs={{0,4},{4,0},{1,5},{5,1},{2,6},{6,2},{3,7},{7,3},{8,12},{12,8},{9,1... | collective-permute-start | bytes 1228808 | tf_op jit(solution)/shard_map/ppermute | solution.py:21
  70.1 14.8 %collective-permute-start.21 = (bf16[160,1280]{1,0:T(8,128)(2,1)S(1)}, bf16[160,1280]{1,0:T(8,128)(2,1)S(1)}, u32[]{:S(2)}, u32[]{:S(2)}) collective-permute-start(bf16[160,1280]{1,0:T(8,128)(2,1)S(1)} %collective-permute-done.19.refs_5_), channel_id=1, source_target_pairs={{0,8},{8,0},{1,9},{9,1},{2,10},{10,2},{3,11},{11,3},{4,12},{12,4},... | collective-permute-start | bytes 1228808 | tf_op jit(solution)/shard_map/ppermute | solution.py:21
  72.8 14.8 %collective-permute-start.13 = (f32[512,640]{1,0:T(8,128)S(1)}, f32[512,640]{1,0:T(8,128)S(1)}, u32[]{:S(2)}, u32[]{:S(2)}) collective-permute-start(f32[512,640]{1,0:T(8,128)S(1)} %get-tuple-element.10), channel_id=1, source_target_pairs={{0,1},{1,0},{2,3},{3,2},{4,5},{5,4},{6,7},{7,6},{8,9},{9,8},{10,11... | collective-permute-start | bytes 3932168 | tf_op jit(solution)/shard_map/ppermute | solution.py:21
  87.6 3.1 %collective-permute-start.22 = (f32[512,640]{1,0:T(8,128)S(1)}, f32[512,640]{1,0:T(8,128)S(1)}, u32[]{:S(2)}, u32[]{:S(2)}) collective-permute-start(f32[512,640]{1,0:T(8,128)S(1)} %get-tuple-element.12), channel_id=1, source_target_pairs={{0,1},{1,0},{2,3},{3,2},{4,5},{5,4},{6,7},{7,6},{8,9},{9,8},{10,11... | collective-permute-start | bytes 3932168 | tf_op jit(solution)/shard_map/ppermute | solution.py:21
  87.8 24.1 %collective-permute-start.14 = (bf16[256,640]{1,0:T(8,128)(2,1)S(1)}, bf16[256,640]{1,0:T(8,128)(2,1)S(1)}, u32[]{:S(2)}, u32[]{:S(2)}) collective-permute-start(bf16[256,640]{1,0:T(8,128)(2,1)S(1)} %slice.31), channel_id=1, source_target_pairs={{0,16},{16,0},{1,17},{17,1},{2,18},{18,2},{3,19},{19,3},{4,20},{20... | collective-permute-start | bytes 983048 | tf_op jit(solution)/shard_map/ppermute | solution.py:21
  90.8 28.1 %collective-permute-start.23 = (bf16[256,640]{1,0:T(8,128)(2,1)S(1)}, bf16[256,640]{1,0:T(8,128)(2,1)S(1)}, u32[]{:S(2)}, u32[]{:S(2)}) collective-permute-start(bf16[256,640]{1,0:T(8,128)(2,1)S(1)} %slice.30), channel_id=1, source_target_pairs={{0,16},{16,0},{1,17},{17,1},{2,18},{18,2},{3,19},{19,3},{4,20},{20... | collective-permute-start | bytes 983048 | tf_op jit(solution)/shard_map/ppermute | solution.py:21

commit v5 on v4

--- a/solution.py
+++ b/solution.py
@@ -11,7 +11,7 @@
 HEAD_DIM = 128
 ANC = 3
 NEG_BIG = -1e30
-CHUNKS = 2
+CHUNKS = (0,5,10)
 
 NODE_AXES = ("h", "q", "l", "x")
 HEAD_AXES = ("y", "c")
@@ -83,44 +83,47 @@
         ),
         compiler_params=pltpu.CompilerParams(vmem_limit_bytes=8 * 2**20),
         cost_estimate=pl.CostEstimate(
-            flops=capacity * capacity * (ANC + 1) * width,
-            bytes_accessed=4 * capacity * width + 4 * capacity * kv_width * (ANC + 1),
-            transcendentals=capacity * capacity * (ANC + 1) * width // HEAD_DIM,
+            flops=0,
+            bytes_accessed=0,
+            transcendentals=0,
         ),
     )(jnp.stack([half, node]).astype(jnp.int32), parents, lengths, query, *kv_blocks)
 
 
 def project_kernel(where_ref, far_ref, far_y_ref, near_ref, near_y_ref, *refs):
-    pieces, (theirs_ref, mine_ref, weight_ref) = refs[:8], refs[8:]
+    pieces, (far_theirs_ref, far_mine_ref, near_theirs_ref, near_mine_ref, weight_ref) = refs[:8], refs[8:]
     rows, depth = pieces[0].shape[0], far_ref.shape[1]
-    tokens, half = far_ref.shape[0], theirs_ref.shape[1]
+    half = far_mine_ref.shape[1]
     for i, piece in enumerate(pieces):
         block = where_ref[0] ^ (i % 4)
         start = pl.multiple_of(block * rows + (i // 4) * depth, 32)
         weight_ref[pl.ds(start, rows), :] = piece[...]
-    for place, (a_ref, b_ref) in enumerate([(far_ref, far_y_ref), (near_ref, near_y_ref)]):
-        out_rows = slice(place * tokens, (place + 1) * tokens)
+    for a_ref, b_ref, theirs_ref, mine_ref in (
+        (far_ref, far_y_ref, far_theirs_ref, far_mine_ref),
+        (near_ref, near_y_ref, near_theirs_ref, near_mine_ref),
+    ):
         for out_ref, cols in ((theirs_ref, slice(0, half)), (mine_ref, slice(half, 2 * half))):
             total = jnp.dot(a_ref[...], weight_ref[:depth, cols], preferred_element_type=jnp.float32)
             total = total + jnp.dot(b_ref[...], weight_ref[depth:, cols], preferred_element_type=jnp.float32)
-            out_ref[out_rows, :] = total
+            out_ref[...] = total.astype(out_ref.dtype)
 
 
 def project(place, inputs, pieces):
     tokens, depth = inputs[0].shape
     columns = pieces[0].shape[1]
     vmem = pl.BlockSpec(memory_space=pltpu.VMEM)
-    out = jax.ShapeDtypeStruct((2 * tokens, columns // 2), jnp.float32)
+    out = jax.ShapeDtypeStruct((tokens, columns // 2), jnp.float32)
+    sent = jax.ShapeDtypeStruct((tokens, columns // 2), jnp.float32)
     return pl.pallas_call(
         project_kernel,
-        out_shape=(out, out),
+        out_shape=(sent, out, sent, out),
         in_specs=[pl.BlockSpec(memory_space=pltpu.SMEM)] + [vmem] * (len(inputs) + len(pieces)),
-        out_specs=(vmem, vmem),
+        out_specs=(vmem,) * 4,
         scratch_shapes=[pltpu.VMEM((2 * depth, columns), jnp.bfloat16)],
         compiler_params=pltpu.CompilerParams(vmem_limit_bytes=24 * 2**20),
         cost_estimate=pl.CostEstimate(
-            flops=2 * tokens * 2 * depth * columns,
-            bytes_accessed=4 * depth * columns + 8 * tokens * columns,
+            flops=0,
+            bytes_accessed=0,
             transcendentals=0,
         ),
     )(jnp.reshape(place, (1,)).astype(jnp.int32), *inputs, *pieces)
@@ -136,20 +139,26 @@
     if parts > 1:
         out_weight = lax.all_gather(out_weight, "q", axis=0, tiled=True)
     width = out_weight.shape[1] // 4
-    step = width // CHUNKS
-
-    def chunk_of(y_index, chunk):
-        starts = [(y_index * 2 + c_index) * width + chunk * step for c_index in (1 - c, c)]
-        return jnp.concatenate([lax.dynamic_slice_in_dim(out_weight, s, step, 1) for s in starts], 1)
+    bounds = [width // CHUNKS[-1] * place for place in CHUNKS]
+
+    def chunk_of(y_index, begin, end):
+        starts = [(y_index * 2 + c_index) * width + begin for c_index in (1 - c, c)]
+        return jnp.concatenate([lax.dynamic_slice_in_dim(out_weight, s, end - begin, 1) for s in starts], 1)
 
     chunks = []
-    for chunk in range(CHUNKS):
-        own_y = swapped(chunk_of(1 - y, chunk), "y")
-        own = chunk_of(y, chunk)
+    for chunk in zip(bounds[:-1], bounds[1:]):
+        own_y = swapped(chunk_of(1 - y, *chunk), "y")
+        own = chunk_of(y, *chunk)
         own_x, own_l = swapped(own, "x"), swapped(own, "l")
         y_x, y_l = swapped(own_y, "x"), swapped(own_y, "l")
         own_lx, y_lx = swapped(own_l, "x"), swapped(y_x, "l")
         chunks.append([own, own_x, own_l, own_lx, own_y, y_x, y_l, y_lx])
+
+    def after(value, pins):
+        value, picked = lax.optimization_barrier((value, [chunks[j][i] for j, i in pins]))
+        for (j, i), piece in zip(pins, picked):
+            chunks[j][i] = piece
+        return value
 
     sent = attend(1 - h, node, parents, lengths, query, kv_blocks)
     far = swapped(sent, "h")
@@ -162,14 +171,20 @@
         return jnp.swapaxes(split, 1, 2).reshape(attended.shape)
 
     near, far = ordered(near), ordered(far)
-    tokens = near.shape[0]
     inputs = [far, swapped(far, "y"), near, swapped(near, "y")]
     outputs = []
-    for pieces in chunks:
-        theirs, mine = project(l * 2 + x, inputs, pieces)
-        both = mine + swapped(theirs, "c")
-        arrived = swapped(both[:tokens].astype(jnp.bfloat16), "h")
-        outputs.append((both[tokens:] + arrived.astype(jnp.float32)).astype(jnp.bfloat16))
+    for number, pieces in enumerate(chunks):
+        far_theirs, far_mine, near_theirs, near_mine = project(l * 2 + x, inputs, pieces)
+        if number + 1 < len(chunks):
+            far_sum = far_theirs + swapped(far_mine.astype(jnp.bfloat16), "c").astype(jnp.float32)
+            arrived = swapped(far_sum.astype(jnp.bfloat16), "h")
+            total = near_mine + swapped(near_theirs + arrived.astype(jnp.float32), "c")
+        else:
+            far_sum = far_mine + swapped(far_theirs.astype(jnp.bfloat16), "c").astype(jnp.float32)
+            near_sum = near_mine + swapped(near_theirs, "c")
+            arrived = swapped(far_sum.astype(jnp.bfloat16), "h")
+            total = near_sum + arrived.astype(jnp.float32)
+        outputs.append(total.astype(jnp.bfloat16))
     return jnp.concatenate(outputs, 1)
 
 

time: 120 us -> 116 us (0.967)
  starting transfers between devices: 22.4 us -> 19.3 us
  waiting for transfers between devices: 80.8 us -> 78.6 us
    ppermute x3, waiting for transfers between devices: 15.4 us -> 9.41 us  [passed_along(): lax.ppermute(value, NODE_AXES, [(i, (i + by) % size) for i in range(size)])]
    ppermute x21 -> x23, waiting for transfers between devices: 65.3 us -> 69.2 us  [swapped(): return lax.ppermute(value, axis, [(0, 1), (1, 0)])]
    ppermute x21 -> x23, starting transfers between devices: 15.3 us -> 12.2 us  [swapped(): return lax.ppermute(value, axis, [(0, 1), (1, 0)])]
  transfers between devices with their start and end apart: 24 -> 26, of which waited for: 13 -> 14; matrix products, arithmetic and copies ran while one was open for 3% -> 3% of each run, Pallas kernels for 10% -> 11%
where the time goes in v5:
time: 116 us
  waiting for transfers between devices  78.6 us (68%)
  starting transfers between devices  19.3 us (17%)
  Pallas kernels  12.9 us (11%)
  local copies, waits for them, and re-layouts  2.35 us (2%)
  other arithmetic  2.32 us (2%)
    ppermute x23, waiting for transfers between devices, swapped(): return lax.ppermute(value, axis, [(0, 1), (1, 0)])  69.2 us
    ppermute x23, starting transfers between devices, swapped(): return lax.ppermute(value, axis, [(0, 1), (1, 0)])  12.2 us
    ppermute x3, waiting for transfers between devices, passed_along(): lax.ppermute(value, NODE_AXES, [(i, (i + by) % size) for i in range(size)])  9.41 us
    ppermute x3, starting transfers between devices, passed_along(): lax.ppermute(value, NODE_AXES, [(i, (i + by) % size) for i in range(size)])  7.08 us
    pallas_call x2, Pallas kernels, project(): pl.pallas_call(project_kernel, out_shape=(sent, out, sent, out), in_specs...  6.52 us
    pallas_call x2, Pallas kernels, attend(): pl.pallas_call(attend_kernel, out_shape=jax.ShapeDtypeStruct((capacity, w...  6.39 us
    dynamic_slice x1, local copies, waits for them, and re-layouts, chunk_of(): lax.dynamic_slice_in_dim(out_weight, s, end - begin, 1)  2.32 us
  transfers between devices with their start and end apart: 26, of which 14 were waited for; matrix products, arithmetic and copies ran while one was open for 3% of the time, Pallas kernels for 11%

profile of v5, /device:TPU:0, one launch (start us, length us, event | category | flops | bytes accessed | tf_op | source)
XLA Modules:
  0.0 115.7 jit_solution(8919337745306901520)
XLA Ops:
  0.0 2.9 %collective-permute-start = (bf16[2,256,256]{2,1,0:T(8,128)(2,1)}, bf16[2,256,256]{2,1,0:T(8,128)(2,1)S(1)}, u32[]{:S(2)}, u32[]{:S(2)}) collective-permute-start(bf16[2,256,256]{2,1,0:T(8,128)(2,1)} %refs_0_.3), channel_id=1, source_target_pairs={{0,4},{4,8},{8,12},{12,16},{16,20},{20,24},{24,28},{28,0},{1,5},{5... | collective-permute-start | bytes 786440 | tf_op jit(solution)/shard_map/ppermute | solution.py:26
  2.9 1.6 %collective-permute-start.1 = (bf16[2,256,256]{2,1,0:T(8,128)(2,1)}, bf16[2,256,256]{2,1,0:T(8,128)(2,1)S(1)}, u32[]{:S(2)}, u32[]{:S(2)}) collective-permute-start(bf16[2,256,256]{2,1,0:T(8,128)(2,1)} %refs_0_.3), channel_id=1, source_target_pairs={{0,8},{4,12},{8,16},{12,20},{16,24},{20,28},{24,0},{28,4},{1,9},{5... | collective-permute-start | bytes 786440 | tf_op jit(solution)/shard_map/ppermute | solution.py:26
  4.5 2.6 %collective-permute-start.2 = (bf16[2,256,256]{2,1,0:T(8,128)(2,1)}, bf16[2,256,256]{2,1,0:T(8,128)(2,1)S(1)}, u32[]{:S(2)}, u32[]{:S(2)}) collective-permute-start(bf16[2,256,256]{2,1,0:T(8,128)(2,1)} %refs_0_.3), channel_id=1, source_target_pairs={{0,12},{4,16},{8,20},{12,24},{16,28},{20,0},{24,4},{28,8},{1,13},{... | collective-permute-start | bytes 786440 | tf_op jit(solution)/shard_map/ppermute | solution.py:26
  7.1 2.3 %constant_dynamic-slice_fusion.5 = (bf16[160,640]{1,0:T(8,128)(2,1)S(1)}, bf16[160,640]{1,0:T(8,128)(2,1)S(1)}, bf16[160,640]{1,0:T(8,128)(2,1)}, bf16[160,640]{...) fusion(bf16[160,5120]{1,0:T(8,128)(2,1)} %param.7, ...), kind=kLoop, calls=%fused_computation.15 | loop fusion | bytes 3276832 | tf_op jit(solution)/shard_map/dynamic_slice | solution.py:146
  9.5 1.6 %collective-permute-start.9 = (bf16[160,1280]{1,0:T(8,128)(2,1)S(1)}, bf16[160,1280]{1,0:T(8,128)(2,1)S(1)}, u32[]{:S(2)}, u32[]{:S(2)}) collective-permute-start(bf16[160,1280]{1,0:T(8,128)(2,1)S(1)} %pad_maximum_fusion.2), channel_id=1, source_target_pairs={{0,2},{2,0},{1,3},{3,1},{4,6},{6,4},{5,7},{7,5},{8,10},{10,8},{9,1... | collective-permute-start | bytes 1228808 | tf_op jit(solution)/shard_map/ppermute | solution.py:21
  11.1 0.3 collective-permute-start.7
  11.4 0.8 pad_maximum_fusion.4
  12.2 1.3 %collective-permute-done.refs_1_ = bf16[2,256,256]{2,1,0:T(8,128)(2,1)S(1)} collective-permute-done((bf16[2,256,256]{2,1,0:T(8,128)(2,1)}, bf16[2,256,256]{2,1,0:T(8,128)(2,1)S(1)}, u32[]{:S(2)}, u32[]{:S(2)}) %collective-permute-start) | collective-permute-done | bytes 262176 | tf_op jit(solution)/shard_map/ppermute | solution.py:26
  13.7 0.6 collective-permute-done.1.refs_2_
  14.3 1.5 %collective-permute-start.19 = (bf16[160,1280]{1,0:T(8,128)(2,1)}, bf16[160,1280]{1,0:T(8,128)(2,1)S(1)}, u32[]{:S(2)}, u32[]{:S(2)}) collective-permute-start(bf16[160,1280]{1,0:T(8,128)(2,1)} %pad_maximum_fusion.4), channel_id=1, source_target_pairs={{0,2},{2,0},{1,3},{3,1},{4,6},{6,4},{5,7},{7,5},{8,10},{10,8},{9,1... | collective-permute-start | bytes 1228808 | tf_op jit(solution)/shard_map/ppermute | solution.py:21
  15.8 6.2 %collective-permute-done.9.refs_4_ = bf16[160,1280]{1,0:T(8,128)(2,1)S(1)} collective-permute-done((bf16[160,1280]{1,0:T(8,128)(2,1)S(1)}, bf16[160,1280]{1,0:T(8,128)(2,1)S(1)}, u32[]{:S(2)}, u32[]{:S(2)}) %collective-permute-start.9) | collective-permute-done | bytes 409632 | tf_op jit(solution)/shard_map/ppermute | solution.py:21
  22.0 7.5 %collective-permute-done.2.refs_3_ = bf16[2,256,256]{2,1,0:T(8,128)(2,1)S(1)} collective-permute-done((bf16[2,256,256]{2,1,0:T(8,128)(2,1)}, bf16[2,256,256]{2,1,0:T(8,128)(2,1)S(1)}, u32[]{:S(2)}, u32[]{:S(2)}) %collective-permute-start.2) | collective-permute-done | bytes 262176 | tf_op jit(solution)/shard_map/ppermute | solution.py:26
  29.6 3.2 %shard_map.55 = bf16[256,640]{1,0:T(8,128)(2,1)S(1)} custom-call(s32[2]{0:T(128)S(1)} %pad_add_fusion.where_ref, s32[8]{0:T(128)S(1)} %copy-done.2, s32[8]{0:T(128)S(1)} %copy-done.3, bf16[256,1280]{1,0:T(8,128)(2,1)S(1)} %copy-done, bf16[2,256,256]{2,1,0:T(8,128)(2,1)S(1)} %copy-done.1, bf16[2,256,256]{2,1,0:T(8,128)(2,1)S(1)} %collective-permute-done.refs_1_, ...), custom_call_target="tpu_custom_call" | custom-call | tf_op jit(solution)/shard_map/pallas_call | solution.py:74
  32.9 2.1 %collective-permute-start.11 = (bf16[160,1280]{1,0:T(8,128)(2,1)S(1)}, bf16[160,1280]{1,0:T(8,128)(2,1)S(1)}, u32[]{:S(2)}, u32[]{:S(2)}) collective-permute-start(bf16[160,1280]{1,0:T(8,128)(2,1)S(1)} %collective-permute-done.9.refs_4_), channel_id=1, source_target_pairs={{0,8},{8,0},{1,9},{9,1},{2,10},{10,2},{3,11},{11,3},{4,12},{12,4},... | collective-permute-start | bytes 1228808 | tf_op jit(solution)/shard_map/ppermute | solution.py:21
  35.0 3.2 %shard_map.56.near_ref = bf16[256,640]{1,0:T(8,128)(2,1)S(1)} custom-call(s32[2]{0:T(128)S(1)} %pad_add_fusion.1.where_ref, s32[8]{0:T(128)S(1)} %copy-done.2, s32[8]{0:T(128)S(1)} %copy-done.3, bf16[256,1280]{1,0:T(8,128)(2,1)S(1)} %copy-done, bf16[2,256,256]{2,1,0:T(8,128)(2,1)S(1)} %copy-done.1, bf16[2,256,256]{2,1,0:T(8,128)(2,1)S(1)} %collective-permute-done.refs_1_, ...), custom_call_target="tpu_custom_call" | custom-call | tf_op jit(solution)/shard_map/pallas_call | solution.py:74
  38.2 1.6 %collective-permute-start.5 = (bf16[256,640]{1,0:T(8,128)(2,1)S(1)}, bf16[256,640]{1,0:T(8,128)(2,1)S(1)}, u32[]{:S(2)}, u32[]{:S(2)}) collective-permute-start(bf16[256,640]{1,0:T(8,128)(2,1)S(1)} %shard_map.56.near_ref), channel_id=1, source_target_pairs={{0,2},{2,0},{1,3},{3,1},{4,6},{6,4},{5,7},{7,5},{8,10},{10,8},{9,1... | collective-permute-start | bytes 983048 | tf_op jit(solution)/shard_map/ppermute | solution.py:21
  40.0 8.3 %collective-permute-done.3.far_ref = bf16[256,640]{1,0:T(8,128)(2,1)S(1)} collective-permute-done((bf16[256,640]{1,0:T(8,128)(2,1)S(1)}, bf16[256,640]{1,0:T(8,128)(2,1)S(1)}, u32[]{:S(2)}, u32[]{:S(2)}) %collective-permute-start.3) | collective-permute-done | bytes 327712 | tf_op jit(solution)/shard_map/ppermute | solution.py:21
  48.3 1.5 %collective-permute-start.4 = (bf16[256,640]{1,0:T(8,128)(2,1)S(1)}, bf16[256,640]{1,0:T(8,128)(2,1)S(1)}, u32[]{:S(2)}, u32[]{:S(2)}) collective-permute-start(bf16[256,640]{1,0:T(8,128)(2,1)S(1)} %collective-permute-done.3.far_ref), channel_id=1, source_target_pairs={{0,2},{2,0},{1,3},{3,1},{4,6},{6,4},{5,7},{7,5},{8,10},{10,8},{9,1... | collective-permute-start | bytes 983048 | tf_op jit(solution)/shard_map/ppermute | solution.py:21
  49.9 2.4 %collective-permute-done.11.refs_6_ = bf16[160,1280]{1,0:T(8,128)(2,1)S(1)} collective-permute-done((bf16[160,1280]{1,0:T(8,128)(2,1)S(1)}, bf16[160,1280]{1,0:T(8,128)(2,1)S(1)}, u32[]{:S(2)}, u32[]{:S(2)}) %collective-permute-start.11) | collective-permute-done | bytes 409632 | tf_op jit(solution)/shard_map/ppermute | solution.py:21
  52.3 5.5 %collective-permute-done.4.far_y_ref = bf16[256,640]{1,0:T(8,128)(2,1)S(1)} collective-permute-done((bf16[256,640]{1,0:T(8,128)(2,1)S(1)}, bf16[256,640]{1,0:T(8,128)(2,1)S(1)}, u32[]{:S(2)}, u32[]{:S(2)}) %collective-permute-start.4) | collective-permute-done | bytes 327712 | tf_op jit(solution)/shard_map/ppermute | solution.py:21
  57.8 3.2 %collective-permute-done.12.refs_7_ = bf16[160,1280]{1,0:T(8,128)(2,1)S(1)} collective-permute-done((bf16[160,1280]{1,0:T(8,128)(2,1)}, bf16[160,1280]{1,0:T(8,128)(2,1)S(1)}, u32[]{:S(2)}, u32[]{:S(2)}) %collective-permute-start.12) | collective-permute-done | bytes 409632 | tf_op jit(solution)/shard_map/ppermute | solution.py:21
  61.1 3.8 %shard_map.57 = (f32[256,640]{1,0:T(8,128)S(1)}, f32[256,640]{1,0:T(8,128)S(1)}, f32[256,640]{1,0:T(8,128)S(1)}, f32[256,640]{1,0:T(8,128)S(1)}) custom-call(s32[1]{0:T(128)} %bitcast.where_ref, bf16[256,640]{1,0:T(8,128)(2,1)S(1)} %collective-permute-done.3.far_ref, bf16[256,640]{1,0:T(8,128)(2,1)S(1)} %collective-permute-done.4.far_y_ref, ...), custom_call_target="tpu_custom_call" | custom-call | tf_op jit(solution)/shard_map/pallas_call | solution.py:117
  65.2 4.2 %collective-permute-done.17.refs_2_ = bf16[160,1280]{1,0:T(8,128)(2,1)S(1)} collective-permute-done((bf16[160,1280]{1,0:T(8,128)(2,1)S(1)}, bf16[160,1280]{1,0:T(8,128)(2,1)S(1)}, u32[]{:S(2)}, u32[]{:S(2)}) %collective-permute-start.17) | collective-permute-done | bytes 409632 | tf_op jit(solution)/shard_map/ppermute | solution.py:21
  69.7 1.9 %collective-permute-start.14 = (bf16[256,640]{1,0:T(8,128)(2,1)S(1)}, bf16[256,640]{1,0:T(8,128)(2,1)S(1)}, u32[]{:S(2)}, u32[]{:S(2)}) collective-permute-start(bf16[256,640]{1,0:T(8,128)(2,1)S(1)} %add_convert_fusion.3), channel_id=1, source_target_pairs={{0,16},{16,0},{1,17},{17,1},{2,18},{18,2},{3,19},{19,3},{4,20},{20... | collective-permute-start | bytes 983048 | tf_op jit(solution)/shard_map/ppermute | solution.py:21
  71.6 5.8 %collective-permute-done.16.refs_1_ = bf16[160,1280]{1,0:T(8,128)(2,1)S(1)} collective-permute-done((bf16[160,1280]{1,0:T(8,128)(2,1)S(1)}, bf16[160,1280]{1,0:T(8,128)(2,1)S(1)}, u32[]{:S(2)}, u32[]{:S(2)}) %collective-permute-start.16) | collective-permute-done | bytes 409632 | tf_op jit(solution)/shard_map/ppermute | solution.py:21
  77.4 8.3 %collective-permute-done.18.refs_3_ = bf16[160,1280]{1,0:T(8,128)(2,1)S(1)} collective-permute-done((bf16[160,1280]{1,0:T(8,128)(2,1)S(1)}, bf16[160,1280]{1,0:T(8,128)(2,1)S(1)}, u32[]{:S(2)}, u32[]{:S(2)}) %collective-permute-start.18) | collective-permute-done | bytes 409632 | tf_op jit(solution)/shard_map/ppermute | solution.py:21
  85.7 7.7 %collective-permute-done.22.refs_7_ = bf16[160,1280]{1,0:T(8,128)(2,1)S(1)} collective-permute-done((bf16[160,1280]{1,0:T(8,128)(2,1)S(1)}, bf16[160,1280]{1,0:T(8,128)(2,1)S(1)}, u32[]{:S(2)}, u32[]{:S(2)}) %collective-permute-start.22) | collective-permute-done | bytes 409632 | tf_op jit(solution)/shard_map/ppermute | solution.py:21
  93.4 2.7 %shard_map.58 = (f32[256,640]{1,0:T(8,128)S(1)}, f32[256,640]{1,0:T(8,128)S(1)}, f32[256,640]{1,0:T(8,128)S(1)}, f32[256,640]{1,0:T(8,128)S(1)}) custom-call(s32[1]{0:T(128)} %bitcast.where_ref, bf16[256,640]{1,0:T(8,128)(2,1)S(1)} %collective-permute-done.3.far_ref, bf16[256,640]{1,0:T(8,128)(2,1)S(1)} %collective-permute-done.4.far_y_ref, ...), custom_call_target="tpu_custom_call" | custom-call | tf_op jit(solution)/shard_map/pallas_call | solution.py:117
  96.2 0.5 collective-permute-start.23
  96.9 0.9 collective-permute-done.24
  98.0 16.6 %collective-permute-done.25 = bf16[256,640]{1,0:T(8,128)(2,1)S(1)} collective-permute-done((bf16[256,640]{1,0:T(8,128)(2,1)S(1)}, bf16[256,640]{1,0:T(8,128)(2,1)S(1)}, u32[]{:S(2)}, u32[]{:S(2)}) %collective-permute-start.25) | collective-permute-done | bytes 327712 | tf_op jit(solution)/shard_map/ppermute | solution.py:21
  114.8 0.9 pad_maximum_fusion
  (49 shorter events, 1.9 us)
Async XLA Ops:
  0.0 13.4 %collective-permute-start = (bf16[2,256,256]{2,1,0:T(8,128)(2,1)}, bf16[2,256,256]{2,1,0:T(8,128)(2,1)S(1)}, u32[]{:S(2)}, u32[]{:S(2)}) collective-permute-start(bf16[2,256,256]{2,1,0:T(8,128)(2,1)} %refs_0_.3), channel_id=1, source_target_pairs={{0,4},{4,8},{8,12},{12,16},{16,20},{20,24},{24,28},{28,0},{1,5},{5... | collective-permute-start | bytes 786440 | tf_op jit(solution)/shard_map/ppermute | solution.py:26
  2.9 11.3 %collective-permute-start.1 = (bf16[2,256,256]{2,1,0:T(8,128)(2,1)}, bf16[2,256,256]{2,1,0:T(8,128)(2,1)S(1)}, u32[]{:S(2)}, u32[]{:S(2)}) collective-permute-start(bf16[2,256,256]{2,1,0:T(8,128)(2,1)} %refs_0_.3), channel_id=1, source_target_pairs={{0,8},{4,12},{8,16},{12,20},{16,24},{20,28},{24,0},{28,4},{1,9},{5... | collective-permute-start | bytes 786440 | tf_op jit(solution)/shard_map/ppermute | solution.py:26
  4.5 25.0 %collective-permute-start.2 = (bf16[2,256,256]{2,1,0:T(8,128)(2,1)}, bf16[2,256,256]{2,1,0:T(8,128)(2,1)S(1)}, u32[]{:S(2)}, u32[]{:S(2)}) collective-permute-start(bf16[2,256,256]{2,1,0:T(8,128)(2,1)} %refs_0_.3), channel_id=1, source_target_pairs={{0,12},{4,16},{8,20},{12,24},{16,28},{20,0},{24,4},{28,8},{1,13},{... | collective-permute-start | bytes 786440 | tf_op jit(solution)/shard_map/ppermute | solution.py:26
  9.4 20.1 %copy-start = (bf16[256,1280]{1,0:T(8,128)(2,1)S(1)}, bf16[256,1280]{1,0:T(8,128)(2,1)}, u32[]{:S(2)}) copy-start(bf16[256,1280]{1,0:T(8,128)(2,1)} %query_ref.3) | copy-start | bytes 1966084
  9.4 20.1 %copy-start.1 = (bf16[2,256,256]{2,1,0:T(8,128)(2,1)S(1)}, bf16[2,256,256]{2,1,0:T(8,128)(2,1)}, u32[]{:S(2)}) copy-start(bf16[2,256,256]{2,1,0:T(8,128)(2,1)} %refs_0_.3) | copy-start | bytes 786436
  9.4 20.1 %copy-start.2 = (s32[8]{0:T(128)S(1)}, s32[8]{0:T(128)}, u32[]{:S(2)}) copy-start(s32[8]{0:T(128)} %parents_ref.3) | copy-start | bytes 100
  9.4 20.1 %copy-start.3 = (s32[8]{0:T(128)S(1)}, s32[8]{0:T(128)}, u32[]{:S(2)}) copy-start(s32[8]{0:T(128)} %lengths_ref.3) | copy-start | bytes 100
  9.5 12.5 %collective-permute-start.9 = (bf16[160,1280]{1,0:T(8,128)(2,1)S(1)}, bf16[160,1280]{1,0:T(8,128)(2,1)S(1)}, u32[]{:S(2)}, u32[]{:S(2)}) collective-permute-start(bf16[160,1280]{1,0:T(8,128)(2,1)S(1)} %pad_maximum_fusion.2), channel_id=1, source_target_pairs={{0,2},{2,0},{1,3},{3,1},{4,6},{6,4},{5,7},{7,5},{8,10},{10,8},{9,1... | collective-permute-start | bytes 1228808 | tf_op jit(solution)/shard_map/ppermute | solution.py:21
  11.1 21.8 %collective-permute-start.7 = (bf16[160,1280]{1,0:T(8,128)(2,1)S(1)}, bf16[160,1280]{1,0:T(8,128)(2,1)S(1)}, u32[]{:S(2)}, u32[]{:S(2)}) collective-permute-start(bf16[160,1280]{1,0:T(8,128)(2,1)S(1)} %pad_maximum_fusion.1.refs_0_), channel_id=1, source_target_pairs={{0,8},{8,0},{1,9},{9,1},{2,10},{10,2},{3,11},{11,3},{4,12},{12,4},... | collective-permute-start | bytes 1228808 | tf_op jit(solution)/shard_map/ppermute | solution.py:21
  13.4 24.8 %collective-permute-start.6 = (bf16[160,1280]{1,0:T(8,128)(2,1)S(1)}, bf16[160,1280]{1,0:T(8,128)(2,1)}, u32[]{:S(2)}, u32[]{:S(2)}) collective-permute-start(bf16[160,1280]{1,0:T(8,128)(2,1)S(1)} %pad_maximum_fusion.1.refs_0_), channel_id=1, source_target_pairs={{0,4},{4,0},{1,5},{5,1},{2,6},{6,2},{3,7},{7,3},{8,12},{12,8},{9,1... | collective-permute-start | bytes 1228808 | tf_op jit(solution)/shard_map/ppermute | solution.py:21
  14.3 25.6 %collective-permute-start.19 = (bf16[160,1280]{1,0:T(8,128)(2,1)}, bf16[160,1280]{1,0:T(8,128)(2,1)S(1)}, u32[]{:S(2)}, u32[]{:S(2)}) collective-permute-start(bf16[160,1280]{1,0:T(8,128)(2,1)} %pad_maximum_fusion.4), channel_id=1, source_target_pairs={{0,2},{2,0},{1,3},{3,1},{4,6},{6,4},{5,7},{7,5},{8,10},{10,8},{9,1... | collective-permute-start | bytes 1228808 | tf_op jit(solution)/shard_map/ppermute | solution.py:21
  21.9 17.9 %collective-permute-start.10 = (bf16[160,1280]{1,0:T(8,128)(2,1)S(1)}, bf16[160,1280]{1,0:T(8,128)(2,1)}, u32[]{:S(2)}, u32[]{:S(2)}) collective-permute-start(bf16[160,1280]{1,0:T(8,128)(2,1)S(1)} %collective-permute-done.9.refs_4_), channel_id=1, source_target_pairs={{0,4},{4,0},{1,5},{5,1},{2,6},{6,2},{3,7},{7,3},{8,12},{12,8},{9,1... | collective-permute-start | bytes 1228808 | tf_op jit(solution)/shard_map/ppermute | solution.py:21
  32.8 17.0 %copy-start.4 = (bf16[160,640]{1,0:T(8,128)(2,1)S(1)}, bf16[160,640]{1,0:T(8,128)(2,1)}, u32[]{:S(2)}) copy-start(bf16[160,640]{1,0:T(8,128)(2,1)} %get-tuple-element.23) | copy-start | bytes 614404
  32.8 15.5 %collective-permute-start.3 = (bf16[256,640]{1,0:T(8,128)(2,1)S(1)}, bf16[256,640]{1,0:T(8,128)(2,1)S(1)}, u32[]{:S(2)}, u32[]{:S(2)}) collective-permute-start(bf16[256,640]{1,0:T(8,128)(2,1)S(1)} %shard_map.55), channel_id=1, source_target_pairs={{0,16},{16,0},{1,17},{17,1},{2,18},{18,2},{3,19},{19,3},{4,20},{20... | collective-permute-start | bytes 983048 | tf_op jit(solution)/shard_map/ppermute | solution.py:21
  32.9 19.4 %collective-permute-start.11 = (bf16[160,1280]{1,0:T(8,128)(2,1)S(1)}, bf16[160,1280]{1,0:T(8,128)(2,1)S(1)}, u32[]{:S(2)}, u32[]{:S(2)}) collective-permute-start(bf16[160,1280]{1,0:T(8,128)(2,1)S(1)} %collective-permute-done.9.refs_4_), channel_id=1, source_target_pairs={{0,8},{8,0},{1,9},{9,1},{2,10},{10,2},{3,11},{11,3},{4,12},{12,4},... | collective-permute-start | bytes 1228808 | tf_op jit(solution)/shard_map/ppermute | solution.py:21
  38.2 11.6 %collective-permute-start.5 = (bf16[256,640]{1,0:T(8,128)(2,1)S(1)}, bf16[256,640]{1,0:T(8,128)(2,1)S(1)}, u32[]{:S(2)}, u32[]{:S(2)}) collective-permute-start(bf16[256,640]{1,0:T(8,128)(2,1)S(1)} %shard_map.56.near_ref), channel_id=1, source_target_pairs={{0,2},{2,0},{1,3},{3,1},{4,6},{6,4},{5,7},{7,5},{8,10},{10,8},{9,1... | collective-permute-start | bytes 983048 | tf_op jit(solution)/shard_map/ppermute | solution.py:21
  39.9 12.4 %collective-permute-start.8 = (bf16[160,1280]{1,0:T(8,128)(2,1)S(1)}, bf16[160,1280]{1,0:T(8,128)(2,1)S(1)}, u32[]{:S(2)}, u32[]{:S(2)}) collective-permute-start(bf16[160,1280]{1,0:T(8,128)(2,1)S(1)} %collective-permute-done.7.refs_2_), channel_id=1, source_target_pairs={{0,4},{4,0},{1,5},{5,1},{2,6},{6,2},{3,7},{7,3},{8,12},{12,8},{9,1... | collective-permute-start | bytes 1228808 | tf_op jit(solution)/shard_map/ppermute | solution.py:21
  39.9 21.2 %collective-permute-start.12 = (bf16[160,1280]{1,0:T(8,128)(2,1)}, bf16[160,1280]{1,0:T(8,128)(2,1)S(1)}, u32[]{:S(2)}, u32[]{:S(2)}) collective-permute-start(bf16[160,1280]{1,0:T(8,128)(2,1)} %collective-permute-done.10.refs_5_), channel_id=1, source_target_pairs={{0,8},{8,0},{1,9},{9,1},{2,10},{10,2},{3,11},{11,3},{4,12},{12,4},... | collective-permute-start | bytes 1228808 | tf_op jit(solution)/shard_map/ppermute | solution.py:21
  48.3 9.6 %collective-permute-start.4 = (bf16[256,640]{1,0:T(8,128)(2,1)S(1)}, bf16[256,640]{1,0:T(8,128)(2,1)S(1)}, u32[]{:S(2)}, u32[]{:S(2)}) collective-permute-start(bf16[256,640]{1,0:T(8,128)(2,1)S(1)} %collective-permute-done.3.far_ref), channel_id=1, source_target_pairs={{0,2},{2,0},{1,3},{3,1},{4,6},{6,4},{5,7},{7,5},{8,10},{10,8},{9,1... | collective-permute-start | bytes 983048 | tf_op jit(solution)/shard_map/ppermute | solution.py:21
  49.8 19.6 %collective-permute-start.17 = (bf16[160,1280]{1,0:T(8,128)(2,1)S(1)}, bf16[160,1280]{1,0:T(8,128)(2,1)S(1)}, u32[]{:S(2)}, u32[]{:S(2)}) collective-permute-start(bf16[160,1280]{1,0:T(8,128)(2,1)S(1)} %pad_maximum_fusion.3.refs_0_), channel_id=1, source_target_pairs={{0,8},{8,0},{1,9},{9,1},{2,10},{10,2},{3,11},{11,3},{4,12},{12,4},... | collective-permute-start | bytes 1228808 | tf_op jit(solution)/shard_map/ppermute | solution.py:21
  52.3 17.1 %collective-permute-start.20 = (bf16[160,1280]{1,0:T(8,128)(2,1)S(1)}, bf16[160,1280]{1,0:T(8,128)(2,1)S(1)}, u32[]{:S(2)}, u32[]{:S(2)}) collective-permute-start(bf16[160,1280]{1,0:T(8,128)(2,1)S(1)} %collective-permute-done.19.refs_4_), channel_id=1, source_target_pairs={{0,4},{4,0},{1,5},{5,1},{2,6},{6,2},{3,7},{7,3},{8,12},{12,8},{9,1... | collective-permute-start | bytes 1228808 | tf_op jit(solution)/shard_map/ppermute | solution.py:21
  64.9 4.7 %collective-permute-start.13 = (bf16[256,640]{1,0:T(8,128)(2,1)S(1)}, bf16[256,640]{1,0:T(8,128)(2,1)S(1)}, u32[]{:S(2)}, u32[]{:S(2)}) collective-permute-start(bf16[256,640]{1,0:T(8,128)(2,1)S(1)} %convert_element_type.30), channel_id=1, source_target_pairs={{0,1},{1,0},{2,3},{3,2},{4,5},{5,4},{6,7},{7,6},{8,9},{9,8},{10,11... | collective-permute-start | bytes 983048 | tf_op jit(solution)/shard_map/ppermute | solution.py:21
  65.0 12.3 %collective-permute-start.16 = (bf16[160,1280]{1,0:T(8,128)(2,1)S(1)}, bf16[160,1280]{1,0:T(8,128)(2,1)S(1)}, u32[]{:S(2)}, u32[]{:S(2)}) collective-permute-start(bf16[160,1280]{1,0:T(8,128)(2,1)S(1)} %pad_maximum_fusion.3.refs_0_), channel_id=1, source_target_pairs={{0,4},{4,0},{1,5},{5,1},{2,6},{6,2},{3,7},{7,3},{8,12},{12,8},{9,1... | collective-permute-start | bytes 1228808 | tf_op jit(solution)/shard_map/ppermute | solution.py:21
  65.1 20.6 %collective-permute-start.21 = (bf16[160,1280]{1,0:T(8,128)(2,1)S(1)}, bf16[160,1280]{1,0:T(8,128)(2,1)S(1)}, u32[]{:S(2)}, u32[]{:S(2)}) collective-permute-start(bf16[160,1280]{1,0:T(8,128)(2,1)S(1)} %collective-permute-done.19.refs_4_), channel_id=1, source_target_pairs={{0,8},{8,0},{1,9},{9,1},{2,10},{10,2},{3,11},{11,3},{4,12},{12,4},... | collective-permute-start | bytes 1228808 | tf_op jit(solution)/shard_map/ppermute | solution.py:21
  69.4 16.3 %collective-permute-start.18 = (bf16[160,1280]{1,0:T(8,128)(2,1)S(1)}, bf16[160,1280]{1,0:T(8,128)(2,1)S(1)}, u32[]{:S(2)}, u32[]{:S(2)}) collective-permute-start(bf16[160,1280]{1,0:T(8,128)(2,1)S(1)} %collective-permute-done.17.refs_2_), channel_id=1, source_target_pairs={{0,4},{4,0},{1,5},{5,1},{2,6},{6,2},{3,7},{7,3},{8,12},{12,8},{9,1... | collective-permute-start | bytes 1228808 | tf_op jit(solution)/shard_map/ppermute | solution.py:21
  69.4 24.0 %collective-permute-start.22 = (bf16[160,1280]{1,0:T(8,128)(2,1)S(1)}, bf16[160,1280]{1,0:T(8,128)(2,1)S(1)}, u32[]{:S(2)}, u32[]{:S(2)}) collective-permute-start(bf16[160,1280]{1,0:T(8,128)(2,1)S(1)} %collective-permute-done.20.refs_5_), channel_id=1, source_target_pairs={{0,8},{8,0},{1,9},{9,1},{2,10},{10,2},{3,11},{11,3},{4,12},{12,4},... | collective-permute-start | bytes 1228808 | tf_op jit(solution)/shard_map/ppermute | solution.py:21
  69.7 27.0 %collective-permute-start.14 = (bf16[256,640]{1,0:T(8,128)(2,1)S(1)}, bf16[256,640]{1,0:T(8,128)(2,1)S(1)}, u32[]{:S(2)}, u32[]{:S(2)}) collective-permute-start(bf16[256,640]{1,0:T(8,128)(2,1)S(1)} %add_convert_fusion.3), channel_id=1, source_target_pairs={{0,16},{16,0},{1,17},{17,1},{2,18},{18,2},{3,19},{19,3},{4,20},{20... | collective-permute-start | bytes 983048 | tf_op jit(solution)/shard_map/ppermute | solution.py:21
  96.1 1.7 %collective-permute-start.24 = (bf16[256,640]{1,0:T(8,128)(2,1)S(1)}, bf16[256,640]{1,0:T(8,128)(2,1)S(1)}, u32[]{:S(2)}, u32[]{:S(2)}) collective-permute-start(bf16[256,640]{1,0:T(8,128)(2,1)S(1)} %convert_element_type.35), channel_id=1, source_target_pairs={{0,1},{1,0},{2,3},{3,2},{4,5},{5,4},{6,7},{7,6},{8,9},{9,8},{10,11... | collective-permute-start | bytes 983048 | tf_op jit(solution)/shard_map/ppermute | solution.py:21
  96.2 18.4 %collective-permute-start.23 = (f32[256,640]{1,0:T(8,128)S(1)}, f32[256,640]{1,0:T(8,128)S(1)}, u32[]{:S(2)}, u32[]{:S(2)}) collective-permute-start(f32[256,640]{1,0:T(8,128)S(1)} %get-tuple-element.18), channel_id=1, source_target_pairs={{0,1},{1,0},{2,3},{3,2},{4,5},{5,4},{6,7},{7,6},{8,9},{9,8},{10,11... | collective-permute-start | bytes 1966088 | tf_op jit(solution)/shard_map/ppermute | solution.py:21
  96.8 17.9 %collective-permute-start.15 = (f32[256,640]{1,0:T(8,128)S(1)}, f32[256,640]{1,0:T(8,128)S(1)}, u32[]{:S(2)}, u32[]{:S(2)}) collective-permute-start(f32[256,640]{1,0:T(8,128)S(1)} %convert_add_fusion), channel_id=1, source_target_pairs={{0,1},{1,0},{2,3},{3,2},{4,5},{5,4},{6,7},{7,6},{8,9},{9,8},{10,11... | collective-permute-start | bytes 1966088 | tf_op jit(solution)/shard_map/ppermute | solution.py:21
  97.9 16.7 %collective-permute-start.25 = (bf16[256,640]{1,0:T(8,128)(2,1)S(1)}, bf16[256,640]{1,0:T(8,128)(2,1)S(1)}, u32[]{:S(2)}, u32[]{:S(2)}) collective-permute-start(bf16[256,640]{1,0:T(8,128)(2,1)S(1)} %add_convert_fusion.1), channel_id=1, source_target_pairs={{0,16},{16,0},{1,17},{17,1},{2,18},{18,2},{3,19},{19,3},{4,20},{20... | collective-permute-start | bytes 983048 | tf_op jit(solution)/shard_map/ppermute | solution.py:21

commit v6 on v5

--- a/solution.py
+++ b/solution.py
@@ -151,7 +151,7 @@
         own = chunk_of(y, *chunk)
         own_x, own_l = swapped(own, "x"), swapped(own, "l")
         y_x, y_l = swapped(own_y, "x"), swapped(own_y, "l")
-        own_lx, y_lx = swapped(own_l, "x"), swapped(y_x, "l")
+        own_lx, y_lx = swapped(own_x, "l"), swapped(y_l, "x")
         chunks.append([own, own_x, own_l, own_lx, own_y, y_x, y_l, y_lx])
 
     def after(value, pins):

time: 116 us -> 115 us (level)
  waiting for transfers between devices: 78.6 us -> 62.7 us
  starting transfers between devices: 19.3 us -> 34 us
    ppermute x23, starting transfers between devices: 12.2 us -> 27 us  [swapped(): return lax.ppermute(value, axis, [(0, 1), (1, 0)])]
    ppermute x23, waiting for transfers between devices: 69.2 us -> 54.7 us  [swapped(): return lax.ppermute(value, axis, [(0, 1), (1, 0)])]
    ppermute x3, waiting for transfers between devices: 9.41 us -> 7.97 us  [passed_along(): lax.ppermute(value, NODE_AXES, [(i, (i + by) % size) for i in range(size)])]
  transfers between devices with their start and end apart: 26 -> 26, of which waited for: 14 -> 12; matrix products, arithmetic and copies ran while one was open for 3% -> 3% of each run, Pallas kernels for 11% -> 11%
where the time goes in v6:
time: 115 us
  waiting for transfers between devices  62.7 us (55%)
  starting transfers between devices  34 us (30%)
  Pallas kernels  12.9 us (11%)
  local copies, waits for them, and re-layouts  2.35 us (2%)
  other arithmetic  2.32 us (2%)
    ppermute x23, waiting for transfers between devices, swapped(): return lax.ppermute(value, axis, [(0, 1), (1, 0)])  54.7 us
    ppermute x23, starting transfers between devices, swapped(): return lax.ppermute(value, axis, [(0, 1), (1, 0)])  27 us
    ppermute x3, waiting for transfers between devices, passed_along(): lax.ppermute(value, NODE_AXES, [(i, (i + by) % size) for i in range(size)])  7.97 us
    ppermute x3, starting transfers between devices, passed_along(): lax.ppermute(value, NODE_AXES, [(i, (i + by) % size) for i in range(size)])  7.08 us
    pallas_call x2, Pallas kernels, project(): pl.pallas_call(project_kernel, out_shape=(sent, out, sent, out), in_specs...  6.52 us
    pallas_call x2, Pallas kernels, attend(): pl.pallas_call(attend_kernel, out_shape=jax.ShapeDtypeStruct((capacity, w...  6.4 us
    dynamic_slice x1, local copies, waits for them, and re-layouts, chunk_of(): lax.dynamic_slice_in_dim(out_weight, s, end - begin, 1)  2.32 us
  transfers between devices with their start and end apart: 26, of which 12 were waited for; matrix products, arithmetic and copies ran while one was open for 3% of the time, Pallas kernels for 11%

profile of v6, /device:TPU:0, one launch (start us, length us, event | category | flops | bytes accessed | tf_op | source)
XLA Modules:
  0.0 114.5 jit_solution(11169606147983438580)
XLA Ops:
  0.0 2.9 %collective-permute-start = (bf16[2,256,256]{2,1,0:T(8,128)(2,1)}, bf16[2,256,256]{2,1,0:T(8,128)(2,1)S(1)}, u32[]{:S(2)}, u32[]{:S(2)}) collective-permute-start(bf16[2,256,256]{2,1,0:T(8,128)(2,1)} %refs_0_.3), channel_id=1, source_target_pairs={{0,4},{4,8},{8,12},{12,16},{16,20},{20,24},{24,28},{28,0},{1,5},{5... | collective-permute-start | bytes 786440 | tf_op jit(solution)/shard_map/ppermute | solution.py:26
  2.9 1.6 %collective-permute-start.1 = (bf16[2,256,256]{2,1,0:T(8,128)(2,1)}, bf16[2,256,256]{2,1,0:T(8,128)(2,1)S(1)}, u32[]{:S(2)}, u32[]{:S(2)}) collective-permute-start(bf16[2,256,256]{2,1,0:T(8,128)(2,1)} %refs_0_.3), channel_id=1, source_target_pairs={{0,8},{4,12},{8,16},{12,20},{16,24},{20,28},{24,0},{28,4},{1,9},{5... | collective-permute-start | bytes 786440 | tf_op jit(solution)/shard_map/ppermute | solution.py:26
  4.5 2.6 %collective-permute-start.2 = (bf16[2,256,256]{2,1,0:T(8,128)(2,1)}, bf16[2,256,256]{2,1,0:T(8,128)(2,1)S(1)}, u32[]{:S(2)}, u32[]{:S(2)}) collective-permute-start(bf16[2,256,256]{2,1,0:T(8,128)(2,1)} %refs_0_.3), channel_id=1, source_target_pairs={{0,12},{4,16},{8,20},{12,24},{16,28},{20,0},{24,4},{28,8},{1,13},{... | collective-permute-start | bytes 786440 | tf_op jit(solution)/shard_map/ppermute | solution.py:26
  7.1 2.3 %constant_dynamic-slice_fusion.5 = (bf16[160,640]{1,0:T(8,128)(2,1)S(1)}, bf16[160,640]{1,0:T(8,128)(2,1)S(1)}, bf16[160,640]{1,0:T(8,128)(2,1)}, bf16[160,640]{...) fusion(bf16[160,5120]{1,0:T(8,128)(2,1)} %param.7, ...), kind=kLoop, calls=%fused_computation.15 | loop fusion | bytes 3276832 | tf_op jit(solution)/shard_map/dynamic_slice | solution.py:146
  9.5 1.6 %collective-permute-start.9 = (bf16[160,1280]{1,0:T(8,128)(2,1)S(1)}, bf16[160,1280]{1,0:T(8,128)(2,1)S(1)}, u32[]{:S(2)}, u32[]{:S(2)}) collective-permute-start(bf16[160,1280]{1,0:T(8,128)(2,1)S(1)} %pad_maximum_fusion.2), channel_id=1, source_target_pairs={{0,2},{2,0},{1,3},{3,1},{4,6},{6,4},{5,7},{7,5},{8,10},{10,8},{9,1... | collective-permute-start | bytes 1228808 | tf_op jit(solution)/shard_map/ppermute | solution.py:21
  11.1 1.6 %collective-permute-start.6 = (bf16[160,1280]{1,0:T(8,128)(2,1)S(1)}, bf16[160,1280]{1,0:T(8,128)(2,1)S(1)}, u32[]{:S(2)}, u32[]{:S(2)}) collective-permute-start(bf16[160,1280]{1,0:T(8,128)(2,1)S(1)} %pad_maximum_fusion.1.refs_0_), channel_id=1, source_target_pairs={{0,4},{4,0},{1,5},{5,1},{2,6},{6,2},{3,7},{7,3},{8,12},{12,8},{9,1... | collective-permute-start | bytes 1228808 | tf_op jit(solution)/shard_map/ppermute | solution.py:21
  12.6 0.8 pad_maximum_fusion.4
  14.2 1.5 %collective-permute-start.19 = (bf16[160,1280]{1,0:T(8,128)(2,1)}, bf16[160,1280]{1,0:T(8,128)(2,1)S(1)}, u32[]{:S(2)}, u32[]{:S(2)}) collective-permute-start(bf16[160,1280]{1,0:T(8,128)(2,1)} %pad_maximum_fusion.4), channel_id=1, source_target_pairs={{0,2},{2,0},{1,3},{3,1},{4,6},{6,4},{5,7},{7,5},{8,10},{10,8},{9,1... | collective-permute-start | bytes 1228808 | tf_op jit(solution)/shard_map/ppermute | solution.py:21
  15.7 6.2 %collective-permute-done.9.refs_4_ = bf16[160,1280]{1,0:T(8,128)(2,1)S(1)} collective-permute-done((bf16[160,1280]{1,0:T(8,128)(2,1)S(1)}, bf16[160,1280]{1,0:T(8,128)(2,1)S(1)}, u32[]{:S(2)}, u32[]{:S(2)}) %collective-permute-start.9) | collective-permute-done | bytes 409632 | tf_op jit(solution)/shard_map/ppermute | solution.py:21
  22.0 7.4 %collective-permute-done.2.refs_3_ = bf16[2,256,256]{2,1,0:T(8,128)(2,1)S(1)} collective-permute-done((bf16[2,256,256]{2,1,0:T(8,128)(2,1)}, bf16[2,256,256]{2,1,0:T(8,128)(2,1)S(1)}, u32[]{:S(2)}, u32[]{:S(2)}) %collective-permute-start.2) | collective-permute-done | bytes 262176 | tf_op jit(solution)/shard_map/ppermute | solution.py:26
  29.5 3.2 %shard_map.55 = bf16[256,640]{1,0:T(8,128)(2,1)S(1)} custom-call(s32[2]{0:T(128)S(1)} %pad_add_fusion.where_ref, s32[8]{0:T(128)S(1)} %copy-done.2, s32[8]{0:T(128)S(1)} %copy-done.3, bf16[256,1280]{1,0:T(8,128)(2,1)S(1)} %copy-done, bf16[2,256,256]{2,1,0:T(8,128)(2,1)S(1)} %copy-done.1, bf16[2,256,256]{2,1,0:T(8,128)(2,1)S(1)} %collective-permute-done.refs_1_, ...), custom_call_target="tpu_custom_call" | custom-call | tf_op jit(solution)/shard_map/pallas_call | solution.py:74
  33.0 3.2 %shard_map.56.near_ref = bf16[256,640]{1,0:T(8,128)(2,1)S(1)} custom-call(s32[2]{0:T(128)S(1)} %pad_add_fusion.1.where_ref, s32[8]{0:T(128)S(1)} %copy-done.2, s32[8]{0:T(128)S(1)} %copy-done.3, bf16[256,1280]{1,0:T(8,128)(2,1)S(1)} %copy-done, bf16[2,256,256]{2,1,0:T(8,128)(2,1)S(1)} %copy-done.1, bf16[2,256,256]{2,1,0:T(8,128)(2,1)S(1)} %collective-permute-done.refs_1_, ...), custom_call_target="tpu_custom_call" | custom-call | tf_op jit(solution)/shard_map/pallas_call | solution.py:74
  36.2 1.6 %collective-permute-start.5 = (bf16[256,640]{1,0:T(8,128)(2,1)S(1)}, bf16[256,640]{1,0:T(8,128)(2,1)S(1)}, u32[]{:S(2)}, u32[]{:S(2)}) collective-permute-start(bf16[256,640]{1,0:T(8,128)(2,1)S(1)} %shard_map.56.near_ref), channel_id=1, source_target_pairs={{0,2},{2,0},{1,3},{3,1},{4,6},{6,4},{5,7},{7,5},{8,10},{10,8},{9,1... | collective-permute-start | bytes 983048 | tf_op jit(solution)/shard_map/ppermute | solution.py:21
  37.8 2.0 %collective-permute-start.8 = (bf16[160,1280]{1,0:T(8,128)(2,1)S(1)}, bf16[160,1280]{1,0:T(8,128)(2,1)S(1)}, u32[]{:S(2)}, u32[]{:S(2)}) collective-permute-start(bf16[160,1280]{1,0:T(8,128)(2,1)S(1)} %collective-permute-done.6.refs_1_), channel_id=1, source_target_pairs={{0,8},{8,0},{1,9},{9,1},{2,10},{10,2},{3,11},{11,3},{4,12},{12,4},... | collective-permute-start | bytes 1228808 | tf_op jit(solution)/shard_map/ppermute | solution.py:21
  39.8 9.3 %collective-permute-start.12 = (bf16[160,1280]{1,0:T(8,128)(2,1)}, bf16[160,1280]{1,0:T(8,128)(2,1)S(1)}, u32[]{:S(2)}, u32[]{:S(2)}) collective-permute-start(bf16[160,1280]{1,0:T(8,128)(2,1)} %collective-permute-done.11.refs_6_), channel_id=1, source_target_pairs={{0,4},{4,0},{1,5},{5,1},{2,6},{6,2},{3,7},{7,3},{8,12},{12,8},{9,1... | collective-permute-start | bytes 1228808 | tf_op jit(solution)/shard_map/ppermute | solution.py:21
  49.6 1.5 %collective-permute-start.4 = (bf16[256,640]{1,0:T(8,128)(2,1)S(1)}, bf16[256,640]{1,0:T(8,128)(2,1)S(1)}, u32[]{:S(2)}, u32[]{:S(2)}) collective-permute-start(bf16[256,640]{1,0:T(8,128)(2,1)S(1)} %collective-permute-done.3.far_ref), channel_id=1, source_target_pairs={{0,2},{2,0},{1,3},{3,1},{4,6},{6,4},{5,7},{7,5},{8,10},{10,8},{9,1... | collective-permute-start | bytes 983048 | tf_op jit(solution)/shard_map/ppermute | solution.py:21
  51.2 1.0 collective-permute-start.21
  52.3 4.3 %collective-permute-done.8.refs_3_ = bf16[160,1280]{1,0:T(8,128)(2,1)S(1)} collective-permute-done((bf16[160,1280]{1,0:T(8,128)(2,1)S(1)}, bf16[160,1280]{1,0:T(8,128)(2,1)S(1)}, u32[]{:S(2)}, u32[]{:S(2)}) %collective-permute-start.8) | collective-permute-done | bytes 409632 | tf_op jit(solution)/shard_map/ppermute | solution.py:21
  56.6 2.2 %collective-permute-done.4.far_y_ref = bf16[256,640]{1,0:T(8,128)(2,1)S(1)} collective-permute-done((bf16[256,640]{1,0:T(8,128)(2,1)S(1)}, bf16[256,640]{1,0:T(8,128)(2,1)S(1)}, u32[]{:S(2)}, u32[]{:S(2)}) %collective-permute-start.4) | collective-permute-done | bytes 327712 | tf_op jit(solution)/shard_map/ppermute | solution.py:21
  58.7 0.8 collective-permute-done.12.refs_7_
  59.6 3.8 %shard_map.57 = (f32[256,640]{1,0:T(8,128)S(1)}, f32[256,640]{1,0:T(8,128)S(1)}, f32[256,640]{1,0:T(8,128)S(1)}, f32[256,640]{1,0:T(8,128)S(1)}) custom-call(s32[1]{0:T(128)} %bitcast.where_ref, bf16[256,640]{1,0:T(8,128)(2,1)S(1)} %collective-permute-done.3.far_ref, bf16[256,640]{1,0:T(8,128)(2,1)S(1)} %collective-permute-done.4.far_y_ref, ...), custom_call_target="tpu_custom_call" | custom-call | tf_op jit(solution)/shard_map/pallas_call | solution.py:117
  63.6 2.1 %collective-permute-start.20 = (bf16[160,1280]{1,0:T(8,128)(2,1)S(1)}, bf16[160,1280]{1,0:T(8,128)(2,1)S(1)}, u32[]{:S(2)}, u32[]{:S(2)}) collective-permute-start(bf16[160,1280]{1,0:T(8,128)(2,1)S(1)} %collective-permute-done.19.refs_4_), channel_id=1, source_target_pairs={{0,4},{4,0},{1,5},{5,1},{2,6},{6,2},{3,7},{7,3},{8,12},{12,8},{9,1... | collective-permute-start | bytes 1228808 | tf_op jit(solution)/shard_map/ppermute | solution.py:21
  65.7 2.5 %collective-permute-done.16.refs_1_ = bf16[160,1280]{1,0:T(8,128)(2,1)S(1)} collective-permute-done((bf16[160,1280]{1,0:T(8,128)(2,1)S(1)}, bf16[160,1280]{1,0:T(8,128)(2,1)S(1)}, u32[]{:S(2)}, u32[]{:S(2)}) %collective-permute-start.16) | collective-permute-done | bytes 409632 | tf_op jit(solution)/shard_map/ppermute | solution.py:21
  68.2 1.7 %collective-permute-start.22 = (bf16[160,1280]{1,0:T(8,128)(2,1)S(1)}, bf16[160,1280]{1,0:T(8,128)(2,1)S(1)}, u32[]{:S(2)}, u32[]{:S(2)}) collective-permute-start(bf16[160,1280]{1,0:T(8,128)(2,1)S(1)} %collective-permute-done.21.refs_6_), channel_id=1, source_target_pairs={{0,4},{4,0},{1,5},{5,1},{2,6},{6,2},{3,7},{7,3},{8,12},{12,8},{9,1... | collective-permute-start | bytes 1228808 | tf_op jit(solution)/shard_map/ppermute | solution.py:21
  70.0 0.7 collective-permute-start.14
  70.7 12.2 %collective-permute-done.17.refs_2_ = bf16[160,1280]{1,0:T(8,128)(2,1)S(1)} collective-permute-done((bf16[160,1280]{1,0:T(8,128)(2,1)S(1)}, bf16[160,1280]{1,0:T(8,128)(2,1)S(1)}, u32[]{:S(2)}, u32[]{:S(2)}) %collective-permute-start.17) | collective-permute-done | bytes 409632 | tf_op jit(solution)/shard_map/ppermute | solution.py:21
  82.9 8.3 %collective-permute-done.18.refs_3_ = bf16[160,1280]{1,0:T(8,128)(2,1)S(1)} collective-permute-done((bf16[160,1280]{1,0:T(8,128)(2,1)S(1)}, bf16[160,1280]{1,0:T(8,128)(2,1)S(1)}, u32[]{:S(2)}, u32[]{:S(2)}) %collective-permute-start.18) | collective-permute-done | bytes 409632 | tf_op jit(solution)/shard_map/ppermute | solution.py:21
  91.2 2.7 %shard_map.58 = (f32[256,640]{1,0:T(8,128)S(1)}, f32[256,640]{1,0:T(8,128)S(1)}, f32[256,640]{1,0:T(8,128)S(1)}, f32[256,640]{1,0:T(8,128)S(1)}) custom-call(s32[1]{0:T(128)} %bitcast.where_ref, bf16[256,640]{1,0:T(8,128)(2,1)S(1)} %collective-permute-done.3.far_ref, bf16[256,640]{1,0:T(8,128)(2,1)S(1)} %collective-permute-done.4.far_y_ref, ...), custom_call_target="tpu_custom_call" | custom-call | tf_op jit(solution)/shard_map/pallas_call | solution.py:117
  94.7 0.9 collective-permute-done.24
  95.7 1.0 collective-permute-start.25
  96.7 16.7 %collective-permute-done.25 = bf16[256,640]{1,0:T(8,128)(2,1)S(1)} collective-permute-done((bf16[256,640]{1,0:T(8,128)(2,1)S(1)}, bf16[256,640]{1,0:T(8,128)(2,1)S(1)}, u32[]{:S(2)}, u32[]{:S(2)}) %collective-permute-start.25) | collective-permute-done | bytes 327712 | tf_op jit(solution)/shard_map/ppermute | solution.py:21
  113.6 0.9 pad_maximum_fusion
  (49 shorter events, 3.1 us)
Async XLA Ops:
  0.0 13.4 %collective-permute-start = (bf16[2,256,256]{2,1,0:T(8,128)(2,1)}, bf16[2,256,256]{2,1,0:T(8,128)(2,1)S(1)}, u32[]{:S(2)}, u32[]{:S(2)}) collective-permute-start(bf16[2,256,256]{2,1,0:T(8,128)(2,1)} %refs_0_.3), channel_id=1, source_target_pairs={{0,4},{4,8},{8,12},{12,16},{16,20},{20,24},{24,28},{28,0},{1,5},{5... | collective-permute-start | bytes 786440 | tf_op jit(solution)/shard_map/ppermute | solution.py:26
  2.9 11.2 %collective-permute-start.1 = (bf16[2,256,256]{2,1,0:T(8,128)(2,1)}, bf16[2,256,256]{2,1,0:T(8,128)(2,1)S(1)}, u32[]{:S(2)}, u32[]{:S(2)}) collective-permute-start(bf16[2,256,256]{2,1,0:T(8,128)(2,1)} %refs_0_.3), channel_id=1, source_target_pairs={{0,8},{4,12},{8,16},{12,20},{16,24},{20,28},{24,0},{28,4},{1,9},{5... | collective-permute-start | bytes 786440 | tf_op jit(solution)/shard_map/ppermute | solution.py:26
  4.5 25.0 %collective-permute-start.2 = (bf16[2,256,256]{2,1,0:T(8,128)(2,1)}, bf16[2,256,256]{2,1,0:T(8,128)(2,1)S(1)}, u32[]{:S(2)}, u32[]{:S(2)}) collective-permute-start(bf16[2,256,256]{2,1,0:T(8,128)(2,1)} %refs_0_.3), channel_id=1, source_target_pairs={{0,12},{4,16},{8,20},{12,24},{16,28},{20,0},{24,4},{28,8},{1,13},{... | collective-permute-start | bytes 786440 | tf_op jit(solution)/shard_map/ppermute | solution.py:26
  9.4 20.1 %copy-start = (bf16[256,1280]{1,0:T(8,128)(2,1)S(1)}, bf16[256,1280]{1,0:T(8,128)(2,1)}, u32[]{:S(2)}) copy-start(bf16[256,1280]{1,0:T(8,128)(2,1)} %query_ref.3) | copy-start | bytes 1966084
  9.4 20.1 %copy-start.1 = (bf16[2,256,256]{2,1,0:T(8,128)(2,1)S(1)}, bf16[2,256,256]{2,1,0:T(8,128)(2,1)}, u32[]{:S(2)}) copy-start(bf16[2,256,256]{2,1,0:T(8,128)(2,1)} %refs_0_.3) | copy-start | bytes 786436
  9.4 20.1 %copy-start.2 = (s32[8]{0:T(128)S(1)}, s32[8]{0:T(128)}, u32[]{:S(2)}) copy-start(s32[8]{0:T(128)} %parents_ref.3) | copy-start | bytes 100
  9.4 20.1 %copy-start.3 = (s32[8]{0:T(128)S(1)}, s32[8]{0:T(128)}, u32[]{:S(2)}) copy-start(s32[8]{0:T(128)} %lengths_ref.3) | copy-start | bytes 100
  9.5 12.5 %collective-permute-start.9 = (bf16[160,1280]{1,0:T(8,128)(2,1)S(1)}, bf16[160,1280]{1,0:T(8,128)(2,1)S(1)}, u32[]{:S(2)}, u32[]{:S(2)}) collective-permute-start(bf16[160,1280]{1,0:T(8,128)(2,1)S(1)} %pad_maximum_fusion.2), channel_id=1, source_target_pairs={{0,2},{2,0},{1,3},{3,1},{4,6},{6,4},{5,7},{7,5},{8,10},{10,8},{9,1... | collective-permute-start | bytes 1228808 | tf_op jit(solution)/shard_map/ppermute | solution.py:21
  11.1 21.7 %collective-permute-start.6 = (bf16[160,1280]{1,0:T(8,128)(2,1)S(1)}, bf16[160,1280]{1,0:T(8,128)(2,1)S(1)}, u32[]{:S(2)}, u32[]{:S(2)}) collective-permute-start(bf16[160,1280]{1,0:T(8,128)(2,1)S(1)} %pad_maximum_fusion.1.refs_0_), channel_id=1, source_target_pairs={{0,4},{4,0},{1,5},{5,1},{2,6},{6,2},{3,7},{7,3},{8,12},{12,8},{9,1... | collective-permute-start | bytes 1228808 | tf_op jit(solution)/shard_map/ppermute | solution.py:21
  13.4 22.8 %collective-permute-start.7 = (bf16[160,1280]{1,0:T(8,128)(2,1)S(1)}, bf16[160,1280]{1,0:T(8,128)(2,1)}, u32[]{:S(2)}, u32[]{:S(2)}) collective-permute-start(bf16[160,1280]{1,0:T(8,128)(2,1)S(1)} %pad_maximum_fusion.1.refs_0_), channel_id=1, source_target_pairs={{0,8},{8,0},{1,9},{9,1},{2,10},{10,2},{3,11},{11,3},{4,12},{12,4},... | collective-permute-start | bytes 1228808 | tf_op jit(solution)/shard_map/ppermute | solution.py:21
  14.2 23.6 %collective-permute-start.19 = (bf16[160,1280]{1,0:T(8,128)(2,1)}, bf16[160,1280]{1,0:T(8,128)(2,1)S(1)}, u32[]{:S(2)}, u32[]{:S(2)}) collective-permute-start(bf16[160,1280]{1,0:T(8,128)(2,1)} %pad_maximum_fusion.4), channel_id=1, source_target_pairs={{0,2},{2,0},{1,3},{3,1},{4,6},{6,4},{5,7},{7,5},{8,10},{10,8},{9,1... | collective-permute-start | bytes 1228808 | tf_op jit(solution)/shard_map/ppermute | solution.py:21
  21.9 17.9 %collective-permute-start.11 = (bf16[160,1280]{1,0:T(8,128)(2,1)S(1)}, bf16[160,1280]{1,0:T(8,128)(2,1)}, u32[]{:S(2)}, u32[]{:S(2)}) collective-permute-start(bf16[160,1280]{1,0:T(8,128)(2,1)S(1)} %collective-permute-done.9.refs_4_), channel_id=1, source_target_pairs={{0,8},{8,0},{1,9},{9,1},{2,10},{10,2},{3,11},{11,3},{4,12},{12,4},... | collective-permute-start | bytes 1228808 | tf_op jit(solution)/shard_map/ppermute | solution.py:21
  32.7 18.4 %copy-start.4 = (bf16[160,640]{1,0:T(8,128)(2,1)S(1)}, bf16[160,640]{1,0:T(8,128)(2,1)}, u32[]{:S(2)}) copy-start(bf16[160,640]{1,0:T(8,128)(2,1)} %get-tuple-element.23) | copy-start | bytes 614404
  32.7 16.8 %collective-permute-start.3 = (bf16[256,640]{1,0:T(8,128)(2,1)S(1)}, bf16[256,640]{1,0:T(8,128)(2,1)S(1)}, u32[]{:S(2)}, u32[]{:S(2)}) collective-permute-start(bf16[256,640]{1,0:T(8,128)(2,1)S(1)} %shard_map.55), channel_id=1, source_target_pairs={{0,16},{16,0},{1,17},{17,1},{2,18},{18,2},{3,19},{19,3},{4,20},{20... | collective-permute-start | bytes 983048 | tf_op jit(solution)/shard_map/ppermute | solution.py:21
  32.8 18.4 %collective-permute-start.10 = (bf16[160,1280]{1,0:T(8,128)(2,1)S(1)}, bf16[160,1280]{1,0:T(8,128)(2,1)S(1)}, u32[]{:S(2)}, u32[]{:S(2)}) collective-permute-start(bf16[160,1280]{1,0:T(8,128)(2,1)S(1)} %collective-permute-done.9.refs_4_), channel_id=1, source_target_pairs={{0,4},{4,0},{1,5},{5,1},{2,6},{6,2},{3,7},{7,3},{8,12},{12,8},{9,1... | collective-permute-start | bytes 1228808 | tf_op jit(solution)/shard_map/ppermute | solution.py:21
  36.2 14.9 %collective-permute-start.5 = (bf16[256,640]{1,0:T(8,128)(2,1)S(1)}, bf16[256,640]{1,0:T(8,128)(2,1)S(1)}, u32[]{:S(2)}, u32[]{:S(2)}) collective-permute-start(bf16[256,640]{1,0:T(8,128)(2,1)S(1)} %shard_map.56.near_ref), channel_id=1, source_target_pairs={{0,2},{2,0},{1,3},{3,1},{4,6},{6,4},{5,7},{7,5},{8,10},{10,8},{9,1... | collective-permute-start | bytes 983048 | tf_op jit(solution)/shard_map/ppermute | solution.py:21
  37.8 18.8 %collective-permute-start.8 = (bf16[160,1280]{1,0:T(8,128)(2,1)S(1)}, bf16[160,1280]{1,0:T(8,128)(2,1)S(1)}, u32[]{:S(2)}, u32[]{:S(2)}) collective-permute-start(bf16[160,1280]{1,0:T(8,128)(2,1)S(1)} %collective-permute-done.6.refs_1_), channel_id=1, source_target_pairs={{0,8},{8,0},{1,9},{9,1},{2,10},{10,2},{3,11},{11,3},{4,12},{12,4},... | collective-permute-start | bytes 1228808 | tf_op jit(solution)/shard_map/ppermute | solution.py:21
  39.8 19.8 %collective-permute-start.12 = (bf16[160,1280]{1,0:T(8,128)(2,1)}, bf16[160,1280]{1,0:T(8,128)(2,1)S(1)}, u32[]{:S(2)}, u32[]{:S(2)}) collective-permute-start(bf16[160,1280]{1,0:T(8,128)(2,1)} %collective-permute-done.11.refs_6_), channel_id=1, source_target_pairs={{0,4},{4,0},{1,5},{5,1},{2,6},{6,2},{3,7},{7,3},{8,12},{12,8},{9,1... | collective-permute-start | bytes 1228808 | tf_op jit(solution)/shard_map/ppermute | solution.py:21
  49.6 9.2 %collective-permute-start.4 = (bf16[256,640]{1,0:T(8,128)(2,1)S(1)}, bf16[256,640]{1,0:T(8,128)(2,1)S(1)}, u32[]{:S(2)}, u32[]{:S(2)}) collective-permute-start(bf16[256,640]{1,0:T(8,128)(2,1)S(1)} %collective-permute-done.3.far_ref), channel_id=1, source_target_pairs={{0,2},{2,0},{1,3},{3,1},{4,6},{6,4},{5,7},{7,5},{8,10},{10,8},{9,1... | collective-permute-start | bytes 983048 | tf_op jit(solution)/shard_map/ppermute | solution.py:21
  51.2 17.1 %collective-permute-start.16 = (bf16[160,1280]{1,0:T(8,128)(2,1)S(1)}, bf16[160,1280]{1,0:T(8,128)(2,1)S(1)}, u32[]{:S(2)}, u32[]{:S(2)}) collective-permute-start(bf16[160,1280]{1,0:T(8,128)(2,1)S(1)} %pad_maximum_fusion.3.refs_0_), channel_id=1, source_target_pairs={{0,4},{4,0},{1,5},{5,1},{2,6},{6,2},{3,7},{7,3},{8,12},{12,8},{9,1... | collective-permute-start | bytes 1228808 | tf_op jit(solution)/shard_map/ppermute | solution.py:21
  51.2 17.0 %collective-permute-start.21 = (bf16[160,1280]{1,0:T(8,128)(2,1)S(1)}, bf16[160,1280]{1,0:T(8,128)(2,1)S(1)}, u32[]{:S(2)}, u32[]{:S(2)}) collective-permute-start(bf16[160,1280]{1,0:T(8,128)(2,1)S(1)} %collective-permute-done.19.refs_4_), channel_id=1, source_target_pairs={{0,8},{8,0},{1,9},{9,1},{2,10},{10,2},{3,11},{11,3},{4,12},{12,4},... | collective-permute-start | bytes 1228808 | tf_op jit(solution)/shard_map/ppermute | solution.py:21
  63.4 6.5 %collective-permute-start.13 = (bf16[256,640]{1,0:T(8,128)(2,1)S(1)}, bf16[256,640]{1,0:T(8,128)(2,1)S(1)}, u32[]{:S(2)}, u32[]{:S(2)}) collective-permute-start(bf16[256,640]{1,0:T(8,128)(2,1)S(1)} %convert_element_type.30), channel_id=1, source_target_pairs={{0,1},{1,0},{2,3},{3,2},{4,5},{5,4},{6,7},{7,6},{8,9},{9,8},{10,11... | collective-permute-start | bytes 983048 | tf_op jit(solution)/shard_map/ppermute | solution.py:21
  63.5 19.4 %collective-permute-start.17 = (bf16[160,1280]{1,0:T(8,128)(2,1)S(1)}, bf16[160,1280]{1,0:T(8,128)(2,1)S(1)}, u32[]{:S(2)}, u32[]{:S(2)}) collective-permute-start(bf16[160,1280]{1,0:T(8,128)(2,1)S(1)} %pad_maximum_fusion.3.refs_0_), channel_id=1, source_target_pairs={{0,8},{8,0},{1,9},{9,1},{2,10},{10,2},{3,11},{11,3},{4,12},{12,4},... | collective-permute-start | bytes 1228808 | tf_op jit(solution)/shard_map/ppermute | solution.py:21
  63.6 27.6 %collective-permute-start.20 = (bf16[160,1280]{1,0:T(8,128)(2,1)S(1)}, bf16[160,1280]{1,0:T(8,128)(2,1)S(1)}, u32[]{:S(2)}, u32[]{:S(2)}) collective-permute-start(bf16[160,1280]{1,0:T(8,128)(2,1)S(1)} %collective-permute-done.19.refs_4_), channel_id=1, source_target_pairs={{0,4},{4,0},{1,5},{5,1},{2,6},{6,2},{3,7},{7,3},{8,12},{12,8},{9,1... | collective-permute-start | bytes 1228808 | tf_op jit(solution)/shard_map/ppermute | solution.py:21
  68.2 23.0 %collective-permute-start.18 = (bf16[160,1280]{1,0:T(8,128)(2,1)S(1)}, bf16[160,1280]{1,0:T(8,128)(2,1)S(1)}, u32[]{:S(2)}, u32[]{:S(2)}) collective-permute-start(bf16[160,1280]{1,0:T(8,128)(2,1)S(1)} %collective-permute-done.16.refs_1_), channel_id=1, source_target_pairs={{0,8},{8,0},{1,9},{9,1},{2,10},{10,2},{3,11},{11,3},{4,12},{12,4},... | collective-permute-start | bytes 1228808 | tf_op jit(solution)/shard_map/ppermute | solution.py:21
  68.2 23.0 %collective-permute-start.22 = (bf16[160,1280]{1,0:T(8,128)(2,1)S(1)}, bf16[160,1280]{1,0:T(8,128)(2,1)S(1)}, u32[]{:S(2)}, u32[]{:S(2)}) collective-permute-start(bf16[160,1280]{1,0:T(8,128)(2,1)S(1)} %collective-permute-done.21.refs_6_), channel_id=1, source_target_pairs={{0,4},{4,0},{1,5},{5,1},{2,6},{6,2},{3,7},{7,3},{8,12},{12,8},{9,1... | collective-permute-start | bytes 1228808 | tf_op jit(solution)/shard_map/ppermute | solution.py:21
  70.0 24.5 %collective-permute-start.14 = (bf16[256,640]{1,0:T(8,128)(2,1)S(1)}, bf16[256,640]{1,0:T(8,128)(2,1)S(1)}, u32[]{:S(2)}, u32[]{:S(2)}) collective-permute-start(bf16[256,640]{1,0:T(8,128)(2,1)S(1)} %add_convert_fusion.3), channel_id=1, source_target_pairs={{0,16},{16,0},{1,17},{17,1},{2,18},{18,2},{3,19},{19,3},{4,20},{20... | collective-permute-start | bytes 983048 | tf_op jit(solution)/shard_map/ppermute | solution.py:21
  94.0 1.7 %collective-permute-start.24 = (bf16[256,640]{1,0:T(8,128)(2,1)S(1)}, bf16[256,640]{1,0:T(8,128)(2,1)S(1)}, u32[]{:S(2)}, u32[]{:S(2)}) collective-permute-start(bf16[256,640]{1,0:T(8,128)(2,1)S(1)} %convert_element_type.35), channel_id=1, source_target_pairs={{0,1},{1,0},{2,3},{3,2},{4,5},{5,4},{6,7},{7,6},{8,9},{9,8},{10,11... | collective-permute-start | bytes 983048 | tf_op jit(solution)/shard_map/ppermute | solution.py:21
  94.0 19.4 %collective-permute-start.23 = (f32[256,640]{1,0:T(8,128)S(1)}, f32[256,640]{1,0:T(8,128)S(1)}, u32[]{:S(2)}, u32[]{:S(2)}) collective-permute-start(f32[256,640]{1,0:T(8,128)S(1)} %get-tuple-element.18), channel_id=1, source_target_pairs={{0,1},{1,0},{2,3},{3,2},{4,5},{5,4},{6,7},{7,6},{8,9},{9,8},{10,11... | collective-permute-start | bytes 1966088 | tf_op jit(solution)/shard_map/ppermute | solution.py:21
  94.6 19.0 %collective-permute-start.15 = (f32[256,640]{1,0:T(8,128)S(1)}, f32[256,640]{1,0:T(8,128)S(1)}, u32[]{:S(2)}, u32[]{:S(2)}) collective-permute-start(f32[256,640]{1,0:T(8,128)S(1)} %convert_add_fusion), channel_id=1, source_target_pairs={{0,1},{1,0},{2,3},{3,2},{4,5},{5,4},{6,7},{7,6},{8,9},{9,8},{10,11... | collective-permute-start | bytes 1966088 | tf_op jit(solution)/shard_map/ppermute | solution.py:21
  95.7 17.7 %collective-permute-start.25 = (bf16[256,640]{1,0:T(8,128)(2,1)S(1)}, bf16[256,640]{1,0:T(8,128)(2,1)S(1)}, u32[]{:S(2)}, u32[]{:S(2)}) collective-permute-start(bf16[256,640]{1,0:T(8,128)(2,1)S(1)} %add_convert_fusion.1), channel_id=1, source_target_pairs={{0,16},{16,0},{1,17},{17,1},{2,18},{18,2},{3,19},{19,3},{4,20},{20... | collective-permute-start | bytes 983048 | tf_op jit(solution)/shard_map/ppermute | solution.py:21

commit v7 on v6

--- a/solution.py
+++ b/solution.py
@@ -10,6 +10,7 @@
 
 HEAD_DIM = 128
 ANC = 3
+LAST_FLOPS = 1_850_000_000
 NEG_BIG = -1e30
 CHUNKS = (0,5,10)
 
@@ -108,7 +109,7 @@
             out_ref[...] = total.astype(out_ref.dtype)
 
 
-def project(place, inputs, pieces):
+def project(place, inputs, pieces, flops):
     tokens, depth = inputs[0].shape
     columns = pieces[0].shape[1]
     vmem = pl.BlockSpec(memory_space=pltpu.VMEM)
@@ -122,7 +123,7 @@
         scratch_shapes=[pltpu.VMEM((2 * depth, columns), jnp.bfloat16)],
         compiler_params=pltpu.CompilerParams(vmem_limit_bytes=24 * 2**20),
         cost_estimate=pl.CostEstimate(
-            flops=0,
+            flops=flops,
             bytes_accessed=0,
             transcendentals=0,
         ),
@@ -174,7 +175,7 @@
     inputs = [far, swapped(far, "y"), near, swapped(near, "y")]
     outputs = []
     for number, pieces in enumerate(chunks):
-        far_theirs, far_mine, near_theirs, near_mine = project(l * 2 + x, inputs, pieces)
+        far_theirs, far_mine, near_theirs, near_mine = project(l * 2 + x, inputs, pieces, LAST_FLOPS if number + 1 == len(chunks) else 0)
         if number + 1 < len(chunks):
             far_sum = far_theirs + swapped(far_mine.astype(jnp.bfloat16), "c").astype(jnp.float32)
             arrived = swapped(far_sum.astype(jnp.bfloat16), "h")

time: 115 us -> 112 us (0.974)
  waiting for transfers between devices: 62.7 us -> 60.1 us
    ppermute x23, starting transfers between devices: 27 us -> 30.3 us  [swapped(): return lax.ppermute(value, axis, [(0, 1), (1, 0)])]
    ppermute x3, starting transfers between devices: 7.08 us -> 4.52 us  [passed_along(): lax.ppermute(value, NODE_AXES, [(i, (i + by) % size) for i in range(size)])]
    ppermute x23, waiting for transfers between devices: 54.7 us -> 53 us  [swapped(): return lax.ppermute(value, axis, [(0, 1), (1, 0)])]
  transfers between devices with their start and end apart: 26 -> 26, of which waited for: 12 -> 11; matrix products, arithmetic and copies ran while one was open for 3% -> 4% of each run, Pallas kernels for 11% -> 11%
where the time goes in v7:
time: 112 us
  waiting for transfers between devices  60.1 us (54%)
  starting transfers between devices  34.8 us (31%)
  Pallas kernels  11.8 us (11%)
  other arithmetic  3.06 us (3%)
  local copies, waits for them, and re-layouts  2.34 us (2%)
    ppermute x23, waiting for transfers between devices, swapped(): return lax.ppermute(value, axis, [(0, 1), (1, 0)])  53 us
    ppermute x23, starting transfers between devices, swapped(): return lax.ppermute(value, axis, [(0, 1), (1, 0)])  30.3 us
    ppermute x3, waiting for transfers between devices, passed_along(): lax.ppermute(value, NODE_AXES, [(i, (i + by) % size) for i in range(size)])  7.07 us
    pallas_call x2, Pallas kernels, attend(): pl.pallas_call(attend_kernel, out_shape=jax.ShapeDtypeStruct((capacity, w...  6.4 us
    pallas_call x2, Pallas kernels, project(): pl.pallas_call(project_kernel, out_shape=(sent, out, sent, out), in_specs...  5.39 us
    ppermute x3, starting transfers between devices, passed_along(): lax.ppermute(value, NODE_AXES, [(i, (i + by) % size) for i in range(size)])  4.52 us
    dynamic_slice x1, local copies, waits for them, and re-layouts, chunk_of(): lax.dynamic_slice_in_dim(out_weight, s, end - begin, 1)  2.31 us
  transfers between devices with their start and end apart: 26, of which 11 were waited for; matrix products, arithmetic and copies ran while one was open for 4% of the time, Pallas kernels for 11%

profile of v7, /device:TPU:0, one launch (start us, length us, event | category | flops | bytes accessed | tf_op | source)
XLA Modules:
  0.0 112.3 jit_solution(13697880881306825068)
XLA Ops:
  0.0 2.9 %collective-permute-start = (bf16[2,256,256]{2,1,0:T(8,128)(2,1)}, bf16[2,256,256]{2,1,0:T(8,128)(2,1)S(1)}, u32[]{:S(2)}, u32[]{:S(2)}) collective-permute-start(bf16[2,256,256]{2,1,0:T(8,128)(2,1)} %refs_0_.3), channel_id=1, source_target_pairs={{0,4},{4,8},{8,12},{12,16},{16,20},{20,24},{24,28},{28,0},{1,5},{5... | collective-permute-start | bytes 786440 | tf_op jit(solution)/shard_map/ppermute | solution.py:27
  2.9 1.6 %collective-permute-start.1 = (bf16[2,256,256]{2,1,0:T(8,128)(2,1)}, bf16[2,256,256]{2,1,0:T(8,128)(2,1)S(1)}, u32[]{:S(2)}, u32[]{:S(2)}) collective-permute-start(bf16[2,256,256]{2,1,0:T(8,128)(2,1)} %refs_0_.3), channel_id=1, source_target_pairs={{0,8},{4,12},{8,16},{12,20},{16,24},{20,28},{24,0},{28,4},{1,9},{5... | collective-permute-start | bytes 786440 | tf_op jit(solution)/shard_map/ppermute | solution.py:27
  4.5 2.3 %constant_dynamic-slice_fusion.5 = (bf16[160,640]{1,0:T(8,128)(2,1)S(1)}, bf16[160,640]{1,0:T(8,128)(2,1)S(1)}, bf16[160,640]{1,0:T(8,128)(2,1)}, bf16[160,640]{...) fusion(bf16[160,5120]{1,0:T(8,128)(2,1)} %param.7, ...), kind=kLoop, calls=%fused_computation.15 | loop fusion | bytes 3276832 | tf_op jit(solution)/shard_map/dynamic_slice | solution.py:147
  6.9 0.8 pad_maximum_fusion.2
  7.6 1.5 %collective-permute-start.9 = (bf16[160,1280]{1,0:T(8,128)(2,1)}, bf16[160,1280]{1,0:T(8,128)(2,1)S(1)}, u32[]{:S(2)}, u32[]{:S(2)}) collective-permute-start(bf16[160,1280]{1,0:T(8,128)(2,1)} %pad_maximum_fusion.2), channel_id=1, source_target_pairs={{0,2},{2,0},{1,3},{3,1},{4,6},{6,4},{5,7},{7,5},{8,10},{10,8},{9,1... | collective-permute-start | bytes 1228808 | tf_op jit(solution)/shard_map/ppermute | solution.py:22
  9.2 1.6 %collective-permute-start.6 = (bf16[160,1280]{1,0:T(8,128)(2,1)S(1)}, bf16[160,1280]{1,0:T(8,128)(2,1)S(1)}, u32[]{:S(2)}, u32[]{:S(2)}) collective-permute-start(bf16[160,1280]{1,0:T(8,128)(2,1)S(1)} %pad_maximum_fusion.1.refs_0_), channel_id=1, source_target_pairs={{0,4},{4,0},{1,5},{5,1},{2,6},{6,2},{3,7},{7,3},{8,12},{12,8},{9,1... | collective-permute-start | bytes 1228808 | tf_op jit(solution)/shard_map/ppermute | solution.py:22
  10.8 1.6 %collective-permute-start.7 = (bf16[160,1280]{1,0:T(8,128)(2,1)S(1)}, bf16[160,1280]{1,0:T(8,128)(2,1)S(1)}, u32[]{:S(2)}, u32[]{:S(2)}) collective-permute-start(bf16[160,1280]{1,0:T(8,128)(2,1)S(1)} %pad_maximum_fusion.1.refs_0_), channel_id=1, source_target_pairs={{0,8},{8,0},{1,9},{9,1},{2,10},{10,2},{3,11},{11,3},{4,12},{12,4},... | collective-permute-start | bytes 1228808 | tf_op jit(solution)/shard_map/ppermute | solution.py:22
  12.4 1.0 collective-permute-done.refs_1_
  13.4 0.8 pad_maximum_fusion.4
  14.2 1.7 %collective-permute-start.19 = (bf16[160,1280]{1,0:T(8,128)(2,1)}, bf16[160,1280]{1,0:T(8,128)(2,1)S(1)}, u32[]{:S(2)}, u32[]{:S(2)}) collective-permute-start(bf16[160,1280]{1,0:T(8,128)(2,1)} %pad_maximum_fusion.4), channel_id=1, source_target_pairs={{0,2},{2,0},{1,3},{3,1},{4,6},{6,4},{5,7},{7,5},{8,10},{10,8},{9,1... | collective-permute-start | bytes 1228808 | tf_op jit(solution)/shard_map/ppermute | solution.py:22
  16.0 4.3 %collective-permute-done.9.refs_4_ = bf16[160,1280]{1,0:T(8,128)(2,1)S(1)} collective-permute-done((bf16[160,1280]{1,0:T(8,128)(2,1)}, bf16[160,1280]{1,0:T(8,128)(2,1)S(1)}, u32[]{:S(2)}, u32[]{:S(2)}) %collective-permute-start.9) | collective-permute-done | bytes 409632 | tf_op jit(solution)/shard_map/ppermute | solution.py:22
  20.2 1.6 %collective-permute-start.11 = (bf16[160,1280]{1,0:T(8,128)(2,1)S(1)}, bf16[160,1280]{1,0:T(8,128)(2,1)S(1)}, u32[]{:S(2)}, u32[]{:S(2)}) collective-permute-start(bf16[160,1280]{1,0:T(8,128)(2,1)S(1)} %collective-permute-done.9.refs_4_), channel_id=1, source_target_pairs={{0,8},{8,0},{1,9},{9,1},{2,10},{10,2},{3,11},{11,3},{4,12},{12,4},... | collective-permute-start | bytes 1228808 | tf_op jit(solution)/shard_map/ppermute | solution.py:22
  21.9 6.0 %collective-permute-done.2.refs_3_ = bf16[2,256,256]{2,1,0:T(8,128)(2,1)S(1)} collective-permute-done((bf16[2,256,256]{2,1,0:T(8,128)(2,1)S(1)}, bf16[2,256,256]{2,1,0:T(8,128)(2,1)S(1)}, u32[]{:S(2)}, u32[]{:S(2)}) %collective-permute-start.2) | collective-permute-done | bytes 262176 | tf_op jit(solution)/shard_map/ppermute | solution.py:27
  27.9 3.2 %shard_map.55 = bf16[256,640]{1,0:T(8,128)(2,1)S(1)} custom-call(s32[2]{0:T(128)S(1)} %pad_add_fusion.where_ref, s32[8]{0:T(128)S(1)} %copy-done.2, s32[8]{0:T(128)S(1)} %copy-done.3, bf16[256,1280]{1,0:T(8,128)(2,1)S(1)} %copy-done, bf16[2,256,256]{2,1,0:T(8,128)(2,1)S(1)} %copy-done.1, bf16[2,256,256]{2,1,0:T(8,128)(2,1)S(1)} %collective-permute-done.refs_1_, ...), custom_call_target="tpu_custom_call" | custom-call | tf_op jit(solution)/shard_map/pallas_call | solution.py:75
  31.1 6.4 %collective-permute-start.3 = (bf16[256,640]{1,0:T(8,128)(2,1)S(1)}, bf16[256,640]{1,0:T(8,128)(2,1)S(1)}, u32[]{:S(2)}, u32[]{:S(2)}) collective-permute-start(bf16[256,640]{1,0:T(8,128)(2,1)S(1)} %shard_map.55), channel_id=1, source_target_pairs={{0,16},{16,0},{1,17},{17,1},{2,18},{18,2},{3,19},{19,3},{4,20},{20... | collective-permute-start | bytes 983048 | tf_op jit(solution)/shard_map/ppermute | solution.py:22
  37.6 3.2 %shard_map.56.near_ref = bf16[256,640]{1,0:T(8,128)(2,1)S(1)} custom-call(s32[2]{0:T(128)S(1)} %pad_add_fusion.1.where_ref, s32[8]{0:T(128)S(1)} %copy-done.2, s32[8]{0:T(128)S(1)} %copy-done.3, bf16[256,1280]{1,0:T(8,128)(2,1)S(1)} %copy-done, bf16[2,256,256]{2,1,0:T(8,128)(2,1)S(1)} %copy-done.1, bf16[2,256,256]{2,1,0:T(8,128)(2,1)S(1)} %collective-permute-done.refs_1_, ...), custom_call_target="tpu_custom_call" | custom-call | tf_op jit(solution)/shard_map/pallas_call | solution.py:75
  40.8 1.6 %collective-permute-start.5 = (bf16[256,640]{1,0:T(8,128)(2,1)S(1)}, bf16[256,640]{1,0:T(8,128)(2,1)S(1)}, u32[]{:S(2)}, u32[]{:S(2)}) collective-permute-start(bf16[256,640]{1,0:T(8,128)(2,1)S(1)} %shard_map.56.near_ref), channel_id=1, source_target_pairs={{0,2},{2,0},{1,3},{3,1},{4,6},{6,4},{5,7},{7,5},{8,10},{10,8},{9,1... | collective-permute-start | bytes 983048 | tf_op jit(solution)/shard_map/ppermute | solution.py:22
  42.4 5.4 %collective-permute-start.12 = (bf16[160,1280]{1,0:T(8,128)(2,1)S(1)}, bf16[160,1280]{1,0:T(8,128)(2,1)S(1)}, u32[]{:S(2)}, u32[]{:S(2)}) collective-permute-start(bf16[160,1280]{1,0:T(8,128)(2,1)S(1)} %collective-permute-done.11.refs_6_), channel_id=1, source_target_pairs={{0,4},{4,0},{1,5},{5,1},{2,6},{6,2},{3,7},{7,3},{8,12},{12,8},{9,1... | collective-permute-start | bytes 1228808 | tf_op jit(solution)/shard_map/ppermute | solution.py:22
  47.8 2.5 %collective-permute-done.3.far_ref = bf16[256,640]{1,0:T(8,128)(2,1)S(1)} collective-permute-done((bf16[256,640]{1,0:T(8,128)(2,1)S(1)}, bf16[256,640]{1,0:T(8,128)(2,1)S(1)}, u32[]{:S(2)}, u32[]{:S(2)}) %collective-permute-start.3) | collective-permute-done | bytes 327712 | tf_op jit(solution)/shard_map/ppermute | solution.py:22
  50.4 1.5 %collective-permute-start.4 = (bf16[256,640]{1,0:T(8,128)(2,1)S(1)}, bf16[256,640]{1,0:T(8,128)(2,1)S(1)}, u32[]{:S(2)}, u32[]{:S(2)}) collective-permute-start(bf16[256,640]{1,0:T(8,128)(2,1)S(1)} %collective-permute-done.3.far_ref), channel_id=1, source_target_pairs={{0,2},{2,0},{1,3},{3,1},{4,6},{6,4},{5,7},{7,5},{8,10},{10,8},{9,1... | collective-permute-start | bytes 983048 | tf_op jit(solution)/shard_map/ppermute | solution.py:22
  52.2 5.8 %collective-permute-done.8.refs_3_ = bf16[160,1280]{1,0:T(8,128)(2,1)S(1)} collective-permute-done((bf16[160,1280]{1,0:T(8,128)(2,1)S(1)}, bf16[160,1280]{1,0:T(8,128)(2,1)S(1)}, u32[]{:S(2)}, u32[]{:S(2)}) %collective-permute-start.8) | collective-permute-done | bytes 409632 | tf_op jit(solution)/shard_map/ppermute | solution.py:22
  58.1 2.7 %shard_map.57 = (f32[256,640]{1,0:T(8,128)S(1)}, f32[256,640]{1,0:T(8,128)S(1)}, f32[256,640]{1,0:T(8,128)S(1)}, f32[256,640]{1,0:T(8,128)S(1)}) custom-call(s32[1]{0:T(128)} %bitcast.where_ref, bf16[256,640]{1,0:T(8,128)(2,1)S(1)} %collective-permute-done.3.far_ref, bf16[256,640]{1,0:T(8,128)(2,1)S(1)} %collective-permute-done.4.far_y_ref, ...), custom_call_target="tpu_custom_call" | custom-call | tf_op jit(solution)/shard_map/pallas_call | solution.py:118
  61.7 1.4 %collective-permute-start.20 = (bf16[160,1280]{1,0:T(8,128)(2,1)S(1)}, bf16[160,1280]{1,0:T(8,128)(2,1)S(1)}, u32[]{:S(2)}, u32[]{:S(2)}) collective-permute-start(bf16[160,1280]{1,0:T(8,128)(2,1)S(1)} %collective-permute-done.19.refs_4_), channel_id=1, source_target_pairs={{0,4},{4,0},{1,5},{5,1},{2,6},{6,2},{3,7},{7,3},{8,12},{12,8},{9,1... | collective-permute-start | bytes 1228808 | tf_op jit(solution)/shard_map/ppermute | solution.py:22
  63.1 3.7 %collective-permute-done.16.refs_1_ = bf16[160,1280]{1,0:T(8,128)(2,1)S(1)} collective-permute-done((bf16[160,1280]{1,0:T(8,128)(2,1)S(1)}, bf16[160,1280]{1,0:T(8,128)(2,1)S(1)}, u32[]{:S(2)}, u32[]{:S(2)}) %collective-permute-start.16) | collective-permute-done | bytes 409632 | tf_op jit(solution)/shard_map/ppermute | solution.py:22
  66.9 2.1 %collective-permute-start.22 = (bf16[160,1280]{1,0:T(8,128)(2,1)S(1)}, bf16[160,1280]{1,0:T(8,128)(2,1)S(1)}, u32[]{:S(2)}, u32[]{:S(2)}) collective-permute-start(bf16[160,1280]{1,0:T(8,128)(2,1)S(1)} %collective-permute-done.21.refs_6_), channel_id=1, source_target_pairs={{0,4},{4,0},{1,5},{5,1},{2,6},{6,2},{3,7},{7,3},{8,12},{12,8},{9,1... | collective-permute-start | bytes 1228808 | tf_op jit(solution)/shard_map/ppermute | solution.py:22
  69.1 11.4 %collective-permute-done.17.refs_2_ = bf16[160,1280]{1,0:T(8,128)(2,1)S(1)} collective-permute-done((bf16[160,1280]{1,0:T(8,128)(2,1)S(1)}, bf16[160,1280]{1,0:T(8,128)(2,1)S(1)}, u32[]{:S(2)}, u32[]{:S(2)}) %collective-permute-start.17) | collective-permute-done | bytes 409632 | tf_op jit(solution)/shard_map/ppermute | solution.py:22
  80.5 8.5 %collective-permute-done.18.refs_3_ = bf16[160,1280]{1,0:T(8,128)(2,1)S(1)} collective-permute-done((bf16[160,1280]{1,0:T(8,128)(2,1)S(1)}, bf16[160,1280]{1,0:T(8,128)(2,1)S(1)}, u32[]{:S(2)}, u32[]{:S(2)}) %collective-permute-start.18) | collective-permute-done | bytes 409632 | tf_op jit(solution)/shard_map/ppermute | solution.py:22
  89.0 2.7 %shard_map.58 = (f32[256,640]{1,0:T(8,128)S(1)}, f32[256,640]{1,0:T(8,128)S(1)}, f32[256,640]{1,0:T(8,128)S(1)}, f32[256,640]{1,0:T(8,128)S(1)}) custom-call(s32[1]{0:T(128)} %bitcast.where_ref, bf16[256,640]{1,0:T(8,128)(2,1)S(1)} %collective-permute-done.3.far_ref, bf16[256,640]{1,0:T(8,128)(2,1)S(1)} %collective-permute-done.4.far_y_ref, ...), custom_call_target="tpu_custom_call" | custom-call | flops 1850000000 | tf_op jit(solution)/shard_map/pallas_call | solution.py:118
  92.5 0.9 collective-permute-done.24
  93.5 2.0 %collective-permute-start.25 = (bf16[256,640]{1,0:T(8,128)(2,1)S(1)}, bf16[256,640]{1,0:T(8,128)(2,1)S(1)}, u32[]{:S(2)}, u32[]{:S(2)}) collective-permute-start(bf16[256,640]{1,0:T(8,128)(2,1)S(1)} %add_convert_fusion.1), channel_id=1, source_target_pairs={{0,16},{16,0},{1,17},{17,1},{2,18},{18,2},{3,19},{19,3},{4,20},{20... | collective-permute-start | bytes 983048 | tf_op jit(solution)/shard_map/ppermute | solution.py:22
  95.5 15.7 %collective-permute-done.25 = bf16[256,640]{1,0:T(8,128)(2,1)S(1)} collective-permute-done((bf16[256,640]{1,0:T(8,128)(2,1)S(1)}, bf16[256,640]{1,0:T(8,128)(2,1)S(1)}, u32[]{:S(2)}, u32[]{:S(2)}) %collective-permute-start.25) | collective-permute-done | bytes 327712 | tf_op jit(solution)/shard_map/ppermute | solution.py:22
  111.4 0.9 pad_maximum_fusion
  (49 shorter events, 2.6 us)
Async XLA Ops:
  0.0 13.4 %collective-permute-start = (bf16[2,256,256]{2,1,0:T(8,128)(2,1)}, bf16[2,256,256]{2,1,0:T(8,128)(2,1)S(1)}, u32[]{:S(2)}, u32[]{:S(2)}) collective-permute-start(bf16[2,256,256]{2,1,0:T(8,128)(2,1)} %refs_0_.3), channel_id=1, source_target_pairs={{0,4},{4,8},{8,12},{12,16},{16,20},{20,24},{24,28},{28,0},{1,5},{5... | collective-permute-start | bytes 786440 | tf_op jit(solution)/shard_map/ppermute | solution.py:27
  2.9 11.3 %collective-permute-start.1 = (bf16[2,256,256]{2,1,0:T(8,128)(2,1)}, bf16[2,256,256]{2,1,0:T(8,128)(2,1)S(1)}, u32[]{:S(2)}, u32[]{:S(2)}) collective-permute-start(bf16[2,256,256]{2,1,0:T(8,128)(2,1)} %refs_0_.3), channel_id=1, source_target_pairs={{0,8},{4,12},{8,16},{12,20},{16,24},{20,28},{24,0},{28,4},{1,9},{5... | collective-permute-start | bytes 786440 | tf_op jit(solution)/shard_map/ppermute | solution.py:27
  6.8 6.6 %copy-start.1 = (bf16[2,256,256]{2,1,0:T(8,128)(2,1)S(1)}, bf16[2,256,256]{2,1,0:T(8,128)(2,1)}, u32[]{:S(2)}) copy-start(bf16[2,256,256]{2,1,0:T(8,128)(2,1)} %refs_0_.3) | copy-start | bytes 786436
  6.8 21.1 %copy-start = (bf16[256,1280]{1,0:T(8,128)(2,1)S(1)}, bf16[256,1280]{1,0:T(8,128)(2,1)}, u32[]{:S(2)}) copy-start(bf16[256,1280]{1,0:T(8,128)(2,1)} %query_ref.3) | copy-start | bytes 1966084
  6.8 21.1 %copy-start.2 = (s32[8]{0:T(128)S(1)}, s32[8]{0:T(128)}, u32[]{:S(2)}) copy-start(s32[8]{0:T(128)} %parents_ref.3) | copy-start | bytes 100
  6.8 21.1 %copy-start.3 = (s32[8]{0:T(128)S(1)}, s32[8]{0:T(128)}, u32[]{:S(2)}) copy-start(s32[8]{0:T(128)} %lengths_ref.3) | copy-start | bytes 100
  7.6 12.6 %collective-permute-start.9 = (bf16[160,1280]{1,0:T(8,128)(2,1)}, bf16[160,1280]{1,0:T(8,128)(2,1)S(1)}, u32[]{:S(2)}, u32[]{:S(2)}) collective-permute-start(bf16[160,1280]{1,0:T(8,128)(2,1)} %pad_maximum_fusion.2), channel_id=1, source_target_pairs={{0,2},{2,0},{1,3},{3,1},{4,6},{6,4},{5,7},{7,5},{8,10},{10,8},{9,1... | collective-permute-start | bytes 1228808 | tf_op jit(solution)/shard_map/ppermute | solution.py:22
  9.2 28.4 %collective-permute-start.6 = (bf16[160,1280]{1,0:T(8,128)(2,1)S(1)}, bf16[160,1280]{1,0:T(8,128)(2,1)S(1)}, u32[]{:S(2)}, u32[]{:S(2)}) collective-permute-start(bf16[160,1280]{1,0:T(8,128)(2,1)S(1)} %pad_maximum_fusion.1.refs_0_), channel_id=1, source_target_pairs={{0,4},{4,0},{1,5},{5,1},{2,6},{6,2},{3,7},{7,3},{8,12},{12,8},{9,1... | collective-permute-start | bytes 1228808 | tf_op jit(solution)/shard_map/ppermute | solution.py:22
  10.8 30.0 %collective-permute-start.7 = (bf16[160,1280]{1,0:T(8,128)(2,1)S(1)}, bf16[160,1280]{1,0:T(8,128)(2,1)S(1)}, u32[]{:S(2)}, u32[]{:S(2)}) collective-permute-start(bf16[160,1280]{1,0:T(8,128)(2,1)S(1)} %pad_maximum_fusion.1.refs_0_), channel_id=1, source_target_pairs={{0,8},{8,0},{1,9},{9,1},{2,10},{10,2},{3,11},{11,3},{4,12},{12,4},... | collective-permute-start | bytes 1228808 | tf_op jit(solution)/shard_map/ppermute | solution.py:22
  13.4 14.5 %collective-permute-start.2 = (bf16[2,256,256]{2,1,0:T(8,128)(2,1)S(1)}, bf16[2,256,256]{2,1,0:T(8,128)(2,1)S(1)}, u32[]{:S(2)}, u32[]{:S(2)}) collective-permute-start(bf16[2,256,256]{2,1,0:T(8,128)(2,1)S(1)} %copy-done.1), channel_id=1, source_target_pairs={{0,12},{4,16},{8,20},{12,24},{16,28},{20,0},{24,4},{28,8},{1,13},{... | collective-permute-start | bytes 786440 | tf_op jit(solution)/shard_map/ppermute | solution.py:27
  14.2 28.2 %collective-permute-start.19 = (bf16[160,1280]{1,0:T(8,128)(2,1)}, bf16[160,1280]{1,0:T(8,128)(2,1)S(1)}, u32[]{:S(2)}, u32[]{:S(2)}) collective-permute-start(bf16[160,1280]{1,0:T(8,128)(2,1)} %pad_maximum_fusion.4), channel_id=1, source_target_pairs={{0,2},{2,0},{1,3},{3,1},{4,6},{6,4},{5,7},{7,5},{8,10},{10,8},{9,1... | collective-permute-start | bytes 1228808 | tf_op jit(solution)/shard_map/ppermute | solution.py:22
  20.2 22.2 %collective-permute-start.11 = (bf16[160,1280]{1,0:T(8,128)(2,1)S(1)}, bf16[160,1280]{1,0:T(8,128)(2,1)S(1)}, u32[]{:S(2)}, u32[]{:S(2)}) collective-permute-start(bf16[160,1280]{1,0:T(8,128)(2,1)S(1)} %collective-permute-done.9.refs_4_), channel_id=1, source_target_pairs={{0,8},{8,0},{1,9},{9,1},{2,10},{10,2},{3,11},{11,3},{4,12},{12,4},... | collective-permute-start | bytes 1228808 | tf_op jit(solution)/shard_map/ppermute | solution.py:22
  31.1 20.8 %copy-start.4 = (bf16[160,640]{1,0:T(8,128)(2,1)S(1)}, bf16[160,640]{1,0:T(8,128)(2,1)}, u32[]{:S(2)}) copy-start(bf16[160,640]{1,0:T(8,128)(2,1)} %get-tuple-element.23) | copy-start | bytes 614404
  31.1 19.2 %collective-permute-start.3 = (bf16[256,640]{1,0:T(8,128)(2,1)S(1)}, bf16[256,640]{1,0:T(8,128)(2,1)S(1)}, u32[]{:S(2)}, u32[]{:S(2)}) collective-permute-start(bf16[256,640]{1,0:T(8,128)(2,1)S(1)} %shard_map.55), channel_id=1, source_target_pairs={{0,16},{16,0},{1,17},{17,1},{2,18},{18,2},{3,19},{19,3},{4,20},{20... | collective-permute-start | bytes 983048 | tf_op jit(solution)/shard_map/ppermute | solution.py:22
  37.5 14.5 %collective-permute-start.10 = (bf16[160,1280]{1,0:T(8,128)(2,1)S(1)}, bf16[160,1280]{1,0:T(8,128)(2,1)S(1)}, u32[]{:S(2)}, u32[]{:S(2)}) collective-permute-start(bf16[160,1280]{1,0:T(8,128)(2,1)S(1)} %collective-permute-done.9.refs_4_), channel_id=1, source_target_pairs={{0,4},{4,0},{1,5},{5,1},{2,6},{6,2},{3,7},{7,3},{8,12},{12,8},{9,1... | collective-permute-start | bytes 1228808 | tf_op jit(solution)/shard_map/ppermute | solution.py:22
  40.8 11.1 %collective-permute-start.5 = (bf16[256,640]{1,0:T(8,128)(2,1)S(1)}, bf16[256,640]{1,0:T(8,128)(2,1)S(1)}, u32[]{:S(2)}, u32[]{:S(2)}) collective-permute-start(bf16[256,640]{1,0:T(8,128)(2,1)S(1)} %shard_map.56.near_ref), channel_id=1, source_target_pairs={{0,2},{2,0},{1,3},{3,1},{4,6},{6,4},{5,7},{7,5},{8,10},{10,8},{9,1... | collective-permute-start | bytes 983048 | tf_op jit(solution)/shard_map/ppermute | solution.py:22
  42.4 15.6 %collective-permute-start.8 = (bf16[160,1280]{1,0:T(8,128)(2,1)S(1)}, bf16[160,1280]{1,0:T(8,128)(2,1)S(1)}, u32[]{:S(2)}, u32[]{:S(2)}) collective-permute-start(bf16[160,1280]{1,0:T(8,128)(2,1)S(1)} %collective-permute-done.6.refs_1_), channel_id=1, source_target_pairs={{0,8},{8,0},{1,9},{9,1},{2,10},{10,2},{3,11},{11,3},{4,12},{12,4},... | collective-permute-start | bytes 1228808 | tf_op jit(solution)/shard_map/ppermute | solution.py:22
  42.4 15.7 %collective-permute-start.12 = (bf16[160,1280]{1,0:T(8,128)(2,1)S(1)}, bf16[160,1280]{1,0:T(8,128)(2,1)S(1)}, u32[]{:S(2)}, u32[]{:S(2)}) collective-permute-start(bf16[160,1280]{1,0:T(8,128)(2,1)S(1)} %collective-permute-done.11.refs_6_), channel_id=1, source_target_pairs={{0,4},{4,0},{1,5},{5,1},{2,6},{6,2},{3,7},{7,3},{8,12},{12,8},{9,1... | collective-permute-start | bytes 1228808 | tf_op jit(solution)/shard_map/ppermute | solution.py:22
  50.4 7.6 %collective-permute-start.4 = (bf16[256,640]{1,0:T(8,128)(2,1)S(1)}, bf16[256,640]{1,0:T(8,128)(2,1)S(1)}, u32[]{:S(2)}, u32[]{:S(2)}) collective-permute-start(bf16[256,640]{1,0:T(8,128)(2,1)S(1)} %collective-permute-done.3.far_ref), channel_id=1, source_target_pairs={{0,2},{2,0},{1,3},{3,1},{4,6},{6,4},{5,7},{7,5},{8,10},{10,8},{9,1... | collective-permute-start | bytes 983048 | tf_op jit(solution)/shard_map/ppermute | solution.py:22
  51.9 15.0 %collective-permute-start.16 = (bf16[160,1280]{1,0:T(8,128)(2,1)S(1)}, bf16[160,1280]{1,0:T(8,128)(2,1)S(1)}, u32[]{:S(2)}, u32[]{:S(2)}) collective-permute-start(bf16[160,1280]{1,0:T(8,128)(2,1)S(1)} %pad_maximum_fusion.3.refs_0_), channel_id=1, source_target_pairs={{0,4},{4,0},{1,5},{5,1},{2,6},{6,2},{3,7},{7,3},{8,12},{12,8},{9,1... | collective-permute-start | bytes 1228808 | tf_op jit(solution)/shard_map/ppermute | solution.py:22
  52.0 14.9 %collective-permute-start.21 = (bf16[160,1280]{1,0:T(8,128)(2,1)S(1)}, bf16[160,1280]{1,0:T(8,128)(2,1)S(1)}, u32[]{:S(2)}, u32[]{:S(2)}) collective-permute-start(bf16[160,1280]{1,0:T(8,128)(2,1)S(1)} %collective-permute-done.19.refs_4_), channel_id=1, source_target_pairs={{0,8},{8,0},{1,9},{9,1},{2,10},{10,2},{3,11},{11,3},{4,12},{12,4},... | collective-permute-start | bytes 1228808 | tf_op jit(solution)/shard_map/ppermute | solution.py:22
  60.9 8.1 %collective-permute-start.13 = (bf16[256,640]{1,0:T(8,128)(2,1)S(1)}, bf16[256,640]{1,0:T(8,128)(2,1)S(1)}, u32[]{:S(2)}, u32[]{:S(2)}) collective-permute-start(bf16[256,640]{1,0:T(8,128)(2,1)S(1)} %convert_element_type.30), channel_id=1, source_target_pairs={{0,1},{1,0},{2,3},{3,2},{4,5},{5,4},{6,7},{7,6},{8,9},{9,8},{10,11... | collective-permute-start | bytes 983048 | tf_op jit(solution)/shard_map/ppermute | solution.py:22
  60.9 19.5 %collective-permute-start.17 = (bf16[160,1280]{1,0:T(8,128)(2,1)S(1)}, bf16[160,1280]{1,0:T(8,128)(2,1)S(1)}, u32[]{:S(2)}, u32[]{:S(2)}) collective-permute-start(bf16[160,1280]{1,0:T(8,128)(2,1)S(1)} %pad_maximum_fusion.3.refs_0_), channel_id=1, source_target_pairs={{0,8},{8,0},{1,9},{9,1},{2,10},{10,2},{3,11},{11,3},{4,12},{12,4},... | collective-permute-start | bytes 1228808 | tf_op jit(solution)/shard_map/ppermute | solution.py:22
  61.7 27.3 %collective-permute-start.20 = (bf16[160,1280]{1,0:T(8,128)(2,1)S(1)}, bf16[160,1280]{1,0:T(8,128)(2,1)S(1)}, u32[]{:S(2)}, u32[]{:S(2)}) collective-permute-start(bf16[160,1280]{1,0:T(8,128)(2,1)S(1)} %collective-permute-done.19.refs_4_), channel_id=1, source_target_pairs={{0,4},{4,0},{1,5},{5,1},{2,6},{6,2},{3,7},{7,3},{8,12},{12,8},{9,1... | collective-permute-start | bytes 1228808 | tf_op jit(solution)/shard_map/ppermute | solution.py:22
  66.9 22.1 %collective-permute-start.18 = (bf16[160,1280]{1,0:T(8,128)(2,1)S(1)}, bf16[160,1280]{1,0:T(8,128)(2,1)S(1)}, u32[]{:S(2)}, u32[]{:S(2)}) collective-permute-start(bf16[160,1280]{1,0:T(8,128)(2,1)S(1)} %collective-permute-done.16.refs_1_), channel_id=1, source_target_pairs={{0,8},{8,0},{1,9},{9,1},{2,10},{10,2},{3,11},{11,3},{4,12},{12,4},... | collective-permute-start | bytes 1228808 | tf_op jit(solution)/shard_map/ppermute | solution.py:22
  66.9 22.1 %collective-permute-start.22 = (bf16[160,1280]{1,0:T(8,128)(2,1)S(1)}, bf16[160,1280]{1,0:T(8,128)(2,1)S(1)}, u32[]{:S(2)}, u32[]{:S(2)}) collective-permute-start(bf16[160,1280]{1,0:T(8,128)(2,1)S(1)} %collective-permute-done.21.refs_6_), channel_id=1, source_target_pairs={{0,4},{4,0},{1,5},{5,1},{2,6},{6,2},{3,7},{7,3},{8,12},{12,8},{9,1... | collective-permute-start | bytes 1228808 | tf_op jit(solution)/shard_map/ppermute | solution.py:22
  69.0 23.3 %collective-permute-start.14 = (bf16[256,640]{1,0:T(8,128)(2,1)S(1)}, bf16[256,640]{1,0:T(8,128)(2,1)S(1)}, u32[]{:S(2)}, u32[]{:S(2)}) collective-permute-start(bf16[256,640]{1,0:T(8,128)(2,1)S(1)} %add_convert_fusion.3), channel_id=1, source_target_pairs={{0,16},{16,0},{1,17},{17,1},{2,18},{18,2},{3,19},{19,3},{4,20},{20... | collective-permute-start | bytes 983048 | tf_op jit(solution)/shard_map/ppermute | solution.py:22
  91.7 1.7 %collective-permute-start.24 = (bf16[256,640]{1,0:T(8,128)(2,1)S(1)}, bf16[256,640]{1,0:T(8,128)(2,1)S(1)}, u32[]{:S(2)}, u32[]{:S(2)}) collective-permute-start(bf16[256,640]{1,0:T(8,128)(2,1)S(1)} %convert_element_type.35), channel_id=1, source_target_pairs={{0,1},{1,0},{2,3},{3,2},{4,5},{5,4},{6,7},{7,6},{8,9},{9,8},{10,11... | collective-permute-start | bytes 983048 | tf_op jit(solution)/shard_map/ppermute | solution.py:22
  91.8 19.4 %collective-permute-start.23 = (f32[256,640]{1,0:T(8,128)S(1)}, f32[256,640]{1,0:T(8,128)S(1)}, u32[]{:S(2)}, u32[]{:S(2)}) collective-permute-start(f32[256,640]{1,0:T(8,128)S(1)} %get-tuple-element.18), channel_id=1, source_target_pairs={{0,1},{1,0},{2,3},{3,2},{4,5},{5,4},{6,7},{7,6},{8,9},{9,8},{10,11... | collective-permute-start | bytes 1966088 | tf_op jit(solution)/shard_map/ppermute | solution.py:22
  92.4 19.0 %collective-permute-start.15 = (f32[256,640]{1,0:T(8,128)S(1)}, f32[256,640]{1,0:T(8,128)S(1)}, u32[]{:S(2)}, u32[]{:S(2)}) collective-permute-start(f32[256,640]{1,0:T(8,128)S(1)} %convert_add_fusion), channel_id=1, source_target_pairs={{0,1},{1,0},{2,3},{3,2},{4,5},{5,4},{6,7},{7,6},{8,9},{9,8},{10,11... | collective-permute-start | bytes 1966088 | tf_op jit(solution)/shard_map/ppermute | solution.py:22
  93.5 17.7 %collective-permute-start.25 = (bf16[256,640]{1,0:T(8,128)(2,1)S(1)}, bf16[256,640]{1,0:T(8,128)(2,1)S(1)}, u32[]{:S(2)}, u32[]{:S(2)}) collective-permute-start(bf16[256,640]{1,0:T(8,128)(2,1)S(1)} %add_convert_fusion.1), channel_id=1, source_target_pairs={{0,16},{16,0},{1,17},{17,1},{2,18},{18,2},{3,19},{19,3},{4,20},{20... | collective-permute-start | bytes 983048 | tf_op jit(solution)/shard_map/ppermute | solution.py:22
